TPU v7x, 512 devices: a whole 4x4x16 slice. The times are simulated.
512 devices in a mesh: dp: 8 (over x, core), fsdp: 4 (over y), seq: 16 (over z).
Axes of the slice: x: 4, y: 4, z: 16, core: 2. Of those that a mesh axis runs over, the one named last changes fastest.
Arguments:
- query_states: bfloat16 [32, 16, 128, 1536], P(('dp', 'fsdp'), 'seq'), may hold values from -8 to 8
- key_states: bfloat16 [32, 16, 128, 1536], P(('dp', 'fsdp'), 'seq'), may hold values from -8 to 8
- value_states: bfloat16 [32, 16, 128, 1536], P(('dp', 'fsdp'), 'seq'), may hold values from -6 to 6
- out_weight: bfloat16 [1536, 1536], P(('fsdp', 'seq')), may hold values from -0.15625 to 0.15625
- gate_space: float32 [1536], replicated, may hold values from -4 to 4
- gate_time: float32 [1536], replicated, may hold values from -4 to 4
- upstream: bfloat16 [32, 16, 128, 1536], P(('dp', 'fsdp'), 'seq'), may hold values from -6 to 6
- frame_count: int32 [32], P(('dp', 'fsdp')), may hold values from 4 to 16, as said below
- pos_count: int32 [32], P(('dp', 'fsdp')), may hold values from 32 to 128, as said below
Outputs:
- output_states: bfloat16 [32, 16, 128, 1536], P(('dp', 'fsdp'), 'seq')
- grad_query: bfloat16 [32, 16, 128, 1536], P(('dp', 'fsdp'), 'seq')
- grad_key: bfloat16 [32, 16, 128, 1536], P(('dp', 'fsdp'), 'seq')
- grad_value: bfloat16 [32, 16, 128, 1536], P(('dp', 'fsdp'), 'seq')
- grad_gate_space: float32 [1536], replicated
- grad_gate_time: float32 [1536], replicated
Inputs may be any that keep to these rules, and one draw needn't show every extreme that they name: `frame_count`: in every draw some clip has all 16 frames valid. `pos_count`: in every draw some clip has all 128 positions valid.
All inputs are finite; a program needn't handle non-finite values.
Results may differ from a plain program's by a relative error of at most 0.012.
Values may be sent and summed in bfloat16 or wider, within the bound.
No kernel may reach another device: no remote copies, remote signals or barrier semaphores. Data moves between devices by JAX's collectives and lax.ppermute only.
A program may use at most 64 MiB of HBM per device.

v0:
```python
import math

import jax
import jax.numpy as jnp
from jax import lax
from jax.sharding import PartitionSpec as P

HEAD = 128


NEGATIVE = -1e30


def other_form(form):
    return form.replace("l", "m")


def softmax_rows(scores, keep):
    masked = jnp.where(keep, scores, NEGATIVE)
    highest = jnp.max(masked, axis=-1, keepdims=True)
    raised = jnp.exp(masked - highest)
    return raised / jnp.sum(raised, axis=-1, keepdims=True)


def attention_scores(queries, keys, form):
    scale = queries.shape[-1] ** (-0.5)
    return (
        jnp.einsum(
            form + "," + other_form(form) + "->bhlm",
            queries,
            keys,
            preferred_element_type=jnp.float32,
        )
        * scale
    )


def attend(queries, keys, values, keep, form):
    probs = softmax_rows(attention_scores(queries, keys, form), keep).astype(jnp.bfloat16)
    result = jnp.einsum(
        "bhlm," + other_form(form) + "->" + form, probs, values, preferred_element_type=jnp.float32
    )
    return result.astype(jnp.bfloat16)


def attend_grad(queries, keys, values, keep, form, incoming):
    scale = queries.shape[-1] ** (-0.5)
    other = other_form(form)
    probs = softmax_rows(attention_scores(queries, keys, form), keep)
    rounded = probs.astype(jnp.bfloat16)
    grad_values = jnp.einsum(
        "bhlm," + form + "->" + other, rounded, incoming, preferred_element_type=jnp.float32
    )
    grad_probs = jnp.einsum(
        form + "," + other + "->bhlm", incoming, values, preferred_element_type=jnp.float32
    )
    inner = jnp.sum(probs * grad_probs, axis=-1, keepdims=True)
    grad_scores = (probs * (grad_probs - inner) * scale).astype(jnp.bfloat16)
    grad_queries = jnp.einsum(
        "bhlm," + other + "->" + form, grad_scores, keys, preferred_element_type=jnp.float32
    )
    grad_keys = jnp.einsum(
        "bhlm," + form + "->" + other, grad_scores, queries, preferred_element_type=jnp.float32
    )
    return (grad_queries, grad_keys, grad_values)


def split_time(array):
    frames, items, channels = (array.shape[0], array.shape[2], array.shape[3])
    return array.reshape(frames, items, channels // HEAD, HEAD)


def time_forward(moved, keep_time):
    frames, items, channels = (moved[0].shape[0], moved[0].shape[2], moved[0].shape[3])
    result = attend(
        split_time(moved[0]), split_time(moved[1]), split_time(moved[2]), keep_time, "lbhe"
    )
    return result.reshape(frames, 1, items, channels)


def time_backward(moved, keep_time):
    frames, items, channels = (moved[0].shape[0], moved[0].shape[2], moved[0].shape[3])
    grads = attend_grad(
        split_time(moved[0]),
        split_time(moved[1]),
        split_time(moved[2]),
        keep_time,
        "lbhe",
        split_time(moved[3]),
    )
    return tuple((part.astype(jnp.bfloat16).reshape(frames, 1, items, channels) for part in grads))


def on_device(
    query_states,
    key_states,
    value_states,
    out_weight,
    gate_space,
    gate_time,
    upstream,
    frame_count,
    pos_count,
):
    frames_here, positions, channels = (
        query_states.shape[1],
        query_states.shape[2],
        query_states.shape[3],
    )
    heads = channels // HEAD
    seq_count = lax.axis_size("seq")
    whole_frames = frames_here * seq_count
    rows = frames_here * positions
    keep_space = (jnp.arange(positions) < pos_count[0])[None, None, None, :]
    keep_time = (jnp.arange(whole_frames) < frame_count[0])[None, None, None, :]

    def split(array):
        return array.reshape(frames_here, positions, heads, HEAD)

    def by_owner(array):
        return array.reshape(frames_here, seq_count, positions // seq_count, channels)

    def to_frames(array):
        return array.reshape(1, frames_here, positions, channels)

    spatial = attend(
        split(query_states), split(key_states), split(value_states), keep_space, "blhe"
    ).reshape(rows, channels)
    owned = (by_owner(query_states), by_owner(key_states), by_owner(value_states))
    temporal_pos = time_forward(
        (
            lax.all_to_all(owned[0], "seq", split_axis=1, concat_axis=0, tiled=True),
            lax.all_to_all(owned[1], "seq", split_axis=1, concat_axis=0, tiled=True),
            lax.all_to_all(owned[2], "seq", split_axis=1, concat_axis=0, tiled=True),
        ),
        keep_time=keep_time,
    )
    temporal = lax.all_to_all(temporal_pos, "seq", split_axis=0, concat_axis=1, tiled=True).reshape(
        rows, channels
    )
    mixed = (
        gate_space * spatial.astype(jnp.float32) + gate_time * temporal.astype(jnp.float32)
    ).astype(jnp.bfloat16)
    flat_up = upstream.reshape(rows, channels)
    output = jnp.dot(
        mixed,
        lax.all_gather(out_weight, ("fsdp", "seq"), axis=0, tiled=True),
        preferred_element_type=jnp.float32,
    )
    grad_mixed = jnp.einsum(
        "td,nd->tn",
        flat_up,
        lax.all_gather(out_weight, ("fsdp", "seq"), axis=0, tiled=True),
        preferred_element_type=jnp.float32,
    )
    part_space = jnp.sum(grad_mixed * spatial.astype(jnp.float32), axis=0)
    part_time = jnp.sum(grad_mixed * temporal.astype(jnp.float32), axis=0)
    gate_totals = lax.psum((part_space, part_time), ("dp", "fsdp", "seq"))
    scale_total = math.sqrt(lax.axis_size("dp") * lax.axis_size("fsdp") * whole_frames * positions)
    down_space = (gate_space * grad_mixed).astype(jnp.bfloat16)
    down_time = by_owner((gate_time * grad_mixed).astype(jnp.bfloat16))
    space_grads = attend_grad(
        split(query_states),
        split(key_states),
        split(value_states),
        keep_space,
        "blhe",
        split(down_space),
    )
    moved_grads = time_backward(
        (
            lax.all_to_all(owned[0], "seq", split_axis=1, concat_axis=0, tiled=True),
            lax.all_to_all(owned[1], "seq", split_axis=1, concat_axis=0, tiled=True),
            lax.all_to_all(owned[2], "seq", split_axis=1, concat_axis=0, tiled=True),
            lax.all_to_all(down_time, "seq", split_axis=1, concat_axis=0, tiled=True),
        ),
        keep_time=keep_time,
    )
    returned = (
        lax.all_to_all(moved_grads[0], "seq", split_axis=0, concat_axis=1, tiled=True),
        lax.all_to_all(moved_grads[1], "seq", split_axis=0, concat_axis=1, tiled=True),
        lax.all_to_all(moved_grads[2], "seq", split_axis=0, concat_axis=1, tiled=True),
    )

    def combine(local, moved):
        return (to_frames(local) + to_frames(moved).astype(jnp.float32)).astype(jnp.bfloat16)

    output_states = to_frames(output.astype(jnp.bfloat16))
    return (
        output_states,
        combine(space_grads[0], returned[0]),
        combine(space_grads[1], returned[1]),
        combine(space_grads[2], returned[2]),
        gate_totals[0] / scale_total,
        gate_totals[1] / scale_total,
    )


def solution(mesh):
    return jax.shard_map(
        on_device,
        mesh=mesh,
        in_specs=(
            P(("dp", "fsdp"), "seq", None, None),
            P(("dp", "fsdp"), "seq", None, None),
            P(("dp", "fsdp"), "seq", None, None),
            P(("fsdp", "seq"), None),
            P(),
            P(),
            P(("dp", "fsdp"), "seq", None, None),
            P(("dp", "fsdp")),
            P(("dp", "fsdp")),
        ),
        out_specs=(
            P(("dp", "fsdp"), "seq", None, None),
            P(("dp", "fsdp"), "seq", None, None),
            P(("dp", "fsdp"), "seq", None, None),
            P(("dp", "fsdp"), "seq", None, None),
            P(),
            P(),
        ),
        check_vma=False,
    )
```

profile of v0, /device:TPU:6, one launch (start us, length us, event | category | flops | bytes accessed | tf_op | source)
XLA Modules:
  0.0 408.9 jit_solution(13416741167037519550)
XLA Ops:
  7.2 0.0 copy-start
  7.2 0.0 all-gather.2.cloned.1.call-start
  7.2 0.7 all-gather.2.cloned.1.call-update
  7.9 39.9 %all_to_all.32 = bf16[1,16,8,1536]{3,2,0,1:T(8,128)(2,1)S(1)} all-to-all(bf16[1,16,8,1536]{3,2,0,1:T(8,128)(2,1)} %bitcast.111), channel_id=1, replica_groups=mesh['dp'=8,'fsdp'=4,'seq'=16] {'seq'}, dimensions={1} | all-to-all | bytes 786432 | tf_op jit(solution)/shard_map/all_to_all | solution.py:133
  47.8 31.1 %all_to_all.33 = bf16[1,16,8,1536]{3,2,0,1:T(8,128)(2,1)S(1)} all-to-all(bf16[1,16,8,1536]{3,2,0,1:T(8,128)(2,1)} %bitcast.110), channel_id=1, replica_groups=mesh['dp'=8,'fsdp'=4,'seq'=16] {'seq'}, dimensions={1} | all-to-all | bytes 786432 | tf_op jit(solution)/shard_map/all_to_all | solution.py:132
  78.9 6.5 %all-to-all-start.2 = ((bf16[1,16,8,1536]{3,2,0,1:T(8,128)(2,1)}), bf16[1,16,8,1536]{3,2,0,1:T(8,128)(2,1)S(1)}, u32[]{:S(2)}, u32[]{:S(2)}) async-start(bf16[1,16,8,1536]{3,2,0,1:T(8,128)(2,1)} %bitcast.112), calls=%async_computation.2 | async-start | bytes 786432 | tf_op jit(solution)/shard_map/all_to_all | solution.py:134
  85.4 0.0 copy-start.4
  86.1 1.3 fusion.78
  87.4 22.4 %all-to-all-done.2 = bf16[1,16,8,1536]{3,2,0,1:T(8,128)(2,1)S(1)} async-done(((bf16[1,16,8,1536]{3,2,0,1:T(8,128)(2,1)}), bf16[1,16,8,1536]{3,2,0,1:T(8,128)(2,1)S(1)}, u32[]{:S(2)}, u32[]{:S(2)}) %all-to-all-start.2) | async-done | bytes 393248 | tf_op jit(solution)/shard_map/all_to_all | solution.py:134
  109.8 1.2 fusion.20
  111.0 1.0 copy.142
  112.0 5.6 %all-to-all-start.3 = ((bf16[16,1,8,1536]{3,2,1,0:T(8,128)(2,1)}), bf16[16,1,8,1536]{3,2,1,0:T(8,128)(2,1)S(1)}, u32[]{:S(2)}, u32[]{:S(2)}) async-start(bf16[16,1,8,1536]{3,2,1,0:T(8,128)(2,1)} %bitcast.107), calls=%async_computation.3 | async-start | bytes 786432 | tf_op jit(solution)/shard_map/all_to_all | solution.py:138
  117.6 0.2 copy.65
  117.9 0.2 copy.66
  118.2 0.2 copy.69
  119.1 1.4 fusion.77
  120.5 1.6 fusion.19
  122.1 0.3 copy.71
  122.4 22.6 %all-to-all-done.3 = bf16[16,1,8,1536]{3,2,1,0:T(8,128)(2,1)S(1)} async-done(((bf16[16,1,8,1536]{3,2,1,0:T(8,128)(2,1)}), bf16[16,1,8,1536]{3,2,1,0:T(8,128)(2,1)S(1)}, u32[]{:S(2)}, u32[]{:S(2)}) %all-to-all-start.3) | async-done | bytes 393248 | tf_op jit(solution)/shard_map/all_to_all | solution.py:138
  145.0 39.6 %all-gather.2.cloned.1.call-done = bf16[1536,1536]{1,0:T(8,128)(2,1)} async-done(((bf16[24,1536]{1,0:T(8,128)(2,1)}), bf16[1536,1536]{1,0:T(8,128)(2,1)}) %all-gather.2.cloned.1.call-update) | async-done | bytes 4718608 | tf_op jit(solution)/shard_map/all_gather | solution.py:147
  184.6 4.6 %fusion.36 = (f32[1536]{0:T(1024)}, f32[1536]{0:T(1024)}, bf16[1,16,8,1536]{3,2,0,1:T(8,128)(2,1)S(1)}, bf16[128,1536]{1,0:T(8,128)(2,1)S(1)}) fusion(bf16[16,1,8,1536]{3,2,1,0:T(8,128)(2,1)S(1)} %all-to-all-done.3, f32[128,1536]{1,0:T(8,128)S(1)} %copy.71, f32[1536]{0:T(1024)S(1)} %copy-done.15, f32[1536]{0:T(1024)S(1)} %copy-done.16, ...), kind=kOutput, calls=%fused_computation.44 | convolution fusion | flops 605746176 | bytes 7102464 | tf_op jit(solution)/shard_map/td,nd->tn/dot_general | solution.py:150
  189.3 25.0 %all_to_all.34 = bf16[1,16,8,1536]{3,2,0,1:T(8,128)(2,1)S(1)} all-to-all(bf16[1,16,8,1536]{3,2,0,1:T(8,128)(2,1)S(1)} %get-tuple-element.10), channel_id=1, replica_groups=mesh['dp'=8,'fsdp'=4,'seq'=16] {'seq'}, dimensions={1} | all-to-all | bytes 786432 | tf_op jit(solution)/shard_map/all_to_all | solution.py:175
  214.2 1.4 fusion.52
  215.6 2.5 fusion.22
  218.2 1.0 copy.140
  219.2 4.4 %all-to-all-start.6 = ((bf16[16,1,8,1536]{3,2,1,0:T(8,128)(2,1)}), bf16[16,1,8,1536]{3,2,1,0:T(8,128)(2,1)S(1)}, u32[]{:S(2)}, u32[]{:S(2)}) async-start(bf16[16,1,8,1536]{3,2,1,0:T(8,128)(2,1)} %bitcast.105), calls=%async_computation.6 | async-start | bytes 786432 | tf_op jit(solution)/shard_map/all_to_all | solution.py:181
  223.5 1.5 fusion.23
  225.0 1.0 copy.139
  226.0 12.9 %all-to-all-done.6 = bf16[16,1,8,1536]{3,2,1,0:T(8,128)(2,1)S(1)} async-done(((bf16[16,1,8,1536]{3,2,1,0:T(8,128)(2,1)}), bf16[16,1,8,1536]{3,2,1,0:T(8,128)(2,1)S(1)}, u32[]{:S(2)}, u32[]{:S(2)}) %all-to-all-start.6) | async-done | bytes 393248 | tf_op jit(solution)/shard_map/all_to_all | solution.py:181
  239.0 7.3 %all-to-all-start.7 = ((bf16[16,1,8,1536]{3,2,1,0:T(8,128)(2,1)}), bf16[16,1,8,1536]{3,2,1,0:T(8,128)(2,1)S(1)}, u32[]{:S(2)}, u32[]{:S(2)}) async-start(bf16[16,1,8,1536]{3,2,1,0:T(8,128)(2,1)} %bitcast.104), calls=%async_computation.7 | async-start | bytes 786432 | tf_op jit(solution)/shard_map/all_to_all | solution.py:182
  246.3 0.2 copy.78
  246.5 105.0 %all-reduce = (f32[1536]{0:T(1024)}, f32[1536]{0:T(1024)}) all-reduce(f32[1536]{0:T(1024)} %get-tuple-element.7, f32[1536]{0:T(1024)} %get-tuple-element.6), channel_id=1, replica_groups=mesh['dp'=8,'fsdp'=4,'seq'=16] {'dp','fsdp','seq'}, use_global_device_ids=true, to_apply=%region_7.8 | all-reduce | flops 3072 | bytes 24576 | tf_op jit(solution)/shard_map/psum | solution.py:158
  351.5 1.3 fusion.85
  352.8 3.4 fusion.25
  356.2 3.4 fusion.24
  359.6 2.6 fusion.62
  362.2 3.3 fusion.21
  365.5 2.0 copy.141
  367.5 8.9 %all-to-all-start.5 = ((bf16[16,1,8,1536]{3,2,1,0:T(8,128)(2,1)}), bf16[16,1,8,1536]{3,2,1,0:T(8,128)(2,1)}, u32[]{:S(2)}, u32[]{:S(2)}) async-start(bf16[16,1,8,1536]{3,2,1,0:T(8,128)(2,1)} %bitcast.106), calls=%async_computation.5 | async-start | bytes 786432 | tf_op jit(solution)/shard_map/all_to_all | solution.py:180
  376.4 1.3 broadcast_multiply_fusion
  377.7 1.2 copy.99
  378.9 1.4 copy.94
  380.3 1.4 copy.89
  381.7 4.0 fusion.4
  385.7 0.8 fusion.37
  386.6 0.8 fusion.38
  387.4 12.9 %all-to-all-done.5 = bf16[16,1,8,1536]{3,2,1,0:T(8,128)(2,1)} async-done(((bf16[16,1,8,1536]{3,2,1,0:T(8,128)(2,1)}), bf16[16,1,8,1536]{3,2,1,0:T(8,128)(2,1)}, u32[]{:S(2)}, u32[]{:S(2)}) %all-to-all-start.5) | async-done | bytes 393248 | tf_op jit(solution)/shard_map/all_to_all | solution.py:180
  400.3 1.8 fusion.39
  (41 shorter events, 0.1 us)
Async XLA Ops:
  7.2 177.5 %copy-start = (bf16[1,1,128,1536]{3,2,1,0:T(8,128)(2,1)S(1)}, bf16[1,1,128,1536]{3,2,1,0:T(8,128)(2,1)}, u32[]{:S(2)}) copy-start(bf16[1,1,128,1536]{3,2,1,0:T(8,128)(2,1)} %param.15) | copy-start | bytes 1179652
  7.2 177.5 %all-gather.2.cloned.1.call-start = ((), (), s32[]{:S(2)}) async-start(), calls=%async_computation.8 | async-start | bytes 4792320 | tf_op jit(solution)/shard_map/all_gather | solution.py:147
  47.8 64.2 %copy-start.8 = (bf16[1,16,8,1536]{3,2,0,1:T(8,128)(2,1)}, bf16[1,16,8,1536]{3,2,0,1:T(8,128)(2,1)S(1)}, u32[]{:S(2)}) copy-start(bf16[1,16,8,1536]{3,2,0,1:T(8,128)(2,1)S(1)} %all_to_all.32) | copy-start | bytes 1179652
  47.8 69.8 %copy-start.2 = (bf16[1,1,128,1536]{3,2,1,0:T(8,128)(2,1)S(1)}, bf16[1,1,128,1536]{3,2,1,0:T(8,128)(2,1)}, u32[]{:S(2)}) copy-start(bf16[1,1,128,1536]{3,2,1,0:T(8,128)(2,1)} %param.9) | copy-start | bytes 1179652
  78.9 39.0 %copy-start.13 = (bf16[1,16,8,1536]{3,2,0,1:T(8,128)(2,1)}, bf16[1,16,8,1536]{3,2,0,1:T(8,128)(2,1)S(1)}, u32[]{:S(2)}) copy-start(bf16[1,16,8,1536]{3,2,0,1:T(8,128)(2,1)S(1)} %all_to_all.33) | copy-start | bytes 1179652
  78.9 39.0 %copy-start.3 = (bf16[1,1,128,1536]{3,2,1,0:T(8,128)(2,1)S(1)}, bf16[1,1,128,1536]{3,2,1,0:T(8,128)(2,1)}, u32[]{:S(2)}) copy-start(bf16[1,1,128,1536]{3,2,1,0:T(8,128)(2,1)} %param.10) | copy-start | bytes 1179652
  78.9 31.0 %all-to-all-start.2 = ((bf16[1,16,8,1536]{3,2,0,1:T(8,128)(2,1)}), bf16[1,16,8,1536]{3,2,0,1:T(8,128)(2,1)S(1)}, u32[]{:S(2)}, u32[]{:S(2)}) async-start(bf16[1,16,8,1536]{3,2,0,1:T(8,128)(2,1)} %bitcast.112), calls=%async_computation.2 | async-start | bytes 786432 | tf_op jit(solution)/shard_map/all_to_all | solution.py:134
  85.4 32.7 %copy-start.4 = (bf16[1,1,128,1536]{3,2,1,0:T(8,128)(2,1)S(1)}, bf16[1,1,128,1536]{3,2,1,0:T(8,128)(2,1)}, u32[]{:S(2)}) copy-start(bf16[1,1,128,1536]{3,2,1,0:T(8,128)(2,1)} %param.11) | copy-start | bytes 1179652
  87.4 24.6 %copy-start.18 = (f32[8,12,16,16]{2,3,1,0:T(8,128)}, f32[8,12,16,16]{2,3,1,0:T(8,128)S(1)}, u32[]{:S(2)}) copy-start(f32[8,12,16,16]{2,3,1,0:T(8,128)S(1)} %get-tuple-element.15) | copy-start | bytes 294916
  112.0 33.0 %all-to-all-start.3 = ((bf16[16,1,8,1536]{3,2,1,0:T(8,128)(2,1)}), bf16[16,1,8,1536]{3,2,1,0:T(8,128)(2,1)S(1)}, u32[]{:S(2)}, u32[]{:S(2)}) async-start(bf16[16,1,8,1536]{3,2,1,0:T(8,128)(2,1)} %bitcast.107), calls=%async_computation.3 | async-start | bytes 786432 | tf_op jit(solution)/shard_map/all_to_all | solution.py:138
  117.9 2.6 copy-start.10
  117.9 66.7 %copy-start.15 = (f32[1536]{0:T(1024)S(1)}, f32[1536]{0:T(1024)}, u32[]{:S(2)}) copy-start(f32[1536]{0:T(1024)} %param.14) | copy-start | bytes 18436
  117.9 66.7 %copy-start.16 = (f32[1536]{0:T(1024)S(1)}, f32[1536]{0:T(1024)}, u32[]{:S(2)}) copy-start(f32[1536]{0:T(1024)} %param.13) | copy-start | bytes 18436
  118.2 3.9 copy-start.12
  119.1 3.0 copy-start.17
  120.5 1.6 copy-start.19
  122.4 93.2 %copy-start.14 = (bf16[1,16,8,1536]{3,2,0,1:T(8,128)(2,1)S(1)}, bf16[1,16,8,1536]{3,2,0,1:T(8,128)(2,1)}, u32[]{:S(2)}) copy-start(bf16[1,16,8,1536]{3,2,0,1:T(8,128)(2,1)} %copy-done.13) | copy-start | bytes 1179652
  219.2 19.8 %all-to-all-start.6 = ((bf16[16,1,8,1536]{3,2,1,0:T(8,128)(2,1)}), bf16[16,1,8,1536]{3,2,1,0:T(8,128)(2,1)S(1)}, u32[]{:S(2)}, u32[]{:S(2)}) async-start(bf16[16,1,8,1536]{3,2,1,0:T(8,128)(2,1)} %bitcast.105), calls=%async_computation.6 | async-start | bytes 786432 | tf_op jit(solution)/shard_map/all_to_all | solution.py:181
  239.0 128.5 %all-to-all-start.7 = ((bf16[16,1,8,1536]{3,2,1,0:T(8,128)(2,1)}), bf16[16,1,8,1536]{3,2,1,0:T(8,128)(2,1)S(1)}, u32[]{:S(2)}, u32[]{:S(2)}) async-start(bf16[16,1,8,1536]{3,2,1,0:T(8,128)(2,1)} %bitcast.104), calls=%async_computation.7 | async-start | bytes 786432 | tf_op jit(solution)/shard_map/all_to_all | solution.py:182
  352.8 6.8 %copy-start.11 = (bf16[1,1,128,1536]{2,3,1,0:T(8,128)(2,1)S(1)}, bf16[1,1,128,1536]{2,3,1,0:T(8,128)(2,1)}, u32[]{:S(2)}) copy-start(bf16[1,1,128,1536]{2,3,1,0:T(8,128)(2,1)} %copy-done.10) | copy-start | bytes 1179652
  356.2 6.0 %copy-start.9 = (bf16[1,16,8,1536]{3,2,0,1:T(8,128)(2,1)S(1)}, bf16[1,16,8,1536]{3,2,0,1:T(8,128)(2,1)}, u32[]{:S(2)}) copy-start(bf16[1,16,8,1536]{3,2,0,1:T(8,128)(2,1)} %copy-done.8) | copy-start | bytes 1179652
  362.2 15.5 %copy-start.7 = (f32[12,128,128]{2,1,0:T(8,128)S(1)}, f32[12,128,128]{2,1,0:T(8,128)}, u32[]{:S(2)}) copy-start(f32[12,128,128]{2,1,0:T(8,128)} %fusion.62) | copy-start | bytes 2359300
  367.5 12.8 %copy-start.5 = (bf16[16,1,8,1536]{3,2,1,0:T(8,128)(2,1)}, bf16[16,1,8,1536]{3,2,1,0:T(8,128)(2,1)S(1)}, u32[]{:S(2)}) copy-start(bf16[16,1,8,1536]{3,2,1,0:T(8,128)(2,1)S(1)} %all-to-all-done.7) | copy-start | bytes 1179652
  367.5 32.8 %all-to-all-start.5 = ((bf16[16,1,8,1536]{3,2,1,0:T(8,128)(2,1)}), bf16[16,1,8,1536]{3,2,1,0:T(8,128)(2,1)}, u32[]{:S(2)}, u32[]{:S(2)}) async-start(bf16[16,1,8,1536]{3,2,1,0:T(8,128)(2,1)} %bitcast.106), calls=%async_computation.5 | async-start | bytes 786432 | tf_op jit(solution)/shard_map/all_to_all | solution.py:180
  381.7 4.0 copy-start.1
  381.7 4.0 copy-start.6
Sparse Core Ops, SparseCore 0:
  11.0 173.6 all-gather.1
where the time goes:
time: 412 us; the launch traced here: 409 us
  blocking collectives  201 us (49%)
  waiting for transfers between devices  111 us (27%)
  matrix products  33.5 us (8%)
  starting transfers between devices  32.7 us (8%)
  between operations  15.7 us (4%)
  local copies, waits for them, and re-layouts  10.2 us (2%)
  other arithmetic  4.77 us (1%)
    psum x1, blocking collectives, on_device(): gate_totals = lax.psum((part_space, part_time), ('dp', 'fsdp', 'seq'))  105 us
    all_to_all x1, blocking collectives, on_device(): lax.all_to_all(owned[1], 'seq', split_axis=1, concat_axis=0, tiled=True)  39.9 us
    all_gather x1, waiting for transfers between devices, on_device(): lax.all_gather(out_weight, ('fsdp', 'seq'), axis=0, tiled=True)  39.6 us
    all_to_all x1, blocking collectives, on_device(): lax.all_to_all(owned[0], 'seq', split_axis=1, concat_axis=0, tiled=True)  31.1 us
    all_to_all x1, blocking collectives, on_device(): lax.all_to_all(down_time, 'seq', split_axis=1, concat_axis=0, tiled=True)  25 us
    all_to_all x1, waiting for transfers between devices, on_device(): lax.all_to_all(temporal_pos, 'seq', split_axis=0, concat_axis=1, tiled=True)  22.6 us
    all_to_all x1, waiting for transfers between devices, on_device(): lax.all_to_all(owned[2], 'seq', split_axis=1, concat_axis=0, tiled=True)  22.4 us
    all_to_all x1, waiting for transfers between devices, on_device(): lax.all_to_all(moved_grads[1], 'seq', split_axis=0, concat_axis=1, tiled=...  12.9 us
  transfers between devices with their start and end apart: 6, of which 5 were waited for; matrix products, arithmetic and copies ran while one was open for 9% of the time, Pallas kernels for 0%

commit v1 on v0

v1 whole, which is shorter than its diff:
```python
import functools
import math

import jax
import jax.numpy as jnp
from jax import lax
from jax.experimental import pallas as pl
from jax.experimental.pallas import tpu as pltpu
from jax.sharding import Mesh, PartitionSpec as P

HEAD = 128
NEGATIVE = -1e30
VMEM_BYTES = 48 * 1024 * 1024
ROWS = 8
PIECES = 5


def contract(left, right, left_dim, right_dim):
    return lax.dot_general(
        left,
        right,
        (((left_dim,), (right_dim,)), ((), ())),
        preferred_element_type=jnp.float32,
    )


def head_gradients(query, key, value, grad_mixed, gate, keep):
    scale = HEAD ** (-0.5)
    incoming = (gate * grad_mixed).astype(jnp.bfloat16)
    scores = jnp.where(keep, contract(key, query, 1, 1) * scale, NEGATIVE)
    raised = jnp.exp(scores - jnp.max(scores, axis=0, keepdims=True))
    probs = raised / jnp.sum(raised, axis=0, keepdims=True)
    rounded = probs.astype(jnp.bfloat16)
    result = contract(rounded, value, 0, 0).astype(jnp.bfloat16)
    part = jnp.sum(grad_mixed * result.astype(jnp.float32), axis=0, keepdims=True)
    grad_value = contract(rounded, incoming, 1, 0)
    grad_probs = contract(value, incoming, 1, 1)
    inner = jnp.sum(probs * grad_probs, axis=0, keepdims=True)
    grad_scores = (probs * (grad_probs - inner) * scale).astype(jnp.bfloat16)
    grad_query = contract(grad_scores, key, 0, 0)
    grad_key = contract(grad_scores, query, 1, 0)
    return result, grad_query, grad_key, grad_value, part


def time_kernel(count_ref, moved_ref, mixed_ref, gate_ref, out_ref, part_ref):
    frames, _, near, channels = moved_ref.shape
    tokens = frames * near
    key_at = lax.broadcasted_iota(jnp.int32, (tokens, tokens), 0)
    query_at = lax.broadcasted_iota(jnp.int32, (tokens, tokens), 1)
    keep = (key_at % near == query_at % near) & (key_at < count_ref[0] * near)
    for head in range(channels // HEAD):
        lanes = slice(head * HEAD, (head + 1) * HEAD)

        def load(which):
            wide = moved_ref[:, which, :, lanes].astype(jnp.float32)
            return wide.reshape(tokens, HEAD).astype(jnp.bfloat16)

        result, grad_query, grad_key, grad_value, part = head_gradients(
            load(0), load(1), load(2), mixed_ref[:, lanes], gate_ref[:, lanes], keep
        )
        part_ref[:, lanes] = part
        for which, array in enumerate((result, grad_query, grad_key, grad_value)):
            wide = array.astype(jnp.float32).reshape(frames, near, HEAD)
            out_ref[:, which, :, lanes] = wide.astype(jnp.bfloat16)


def space_kernel(
    count_ref, query_ref, key_ref, value_ref, mixed_ref, gate_ref,
    out_ref, grad_query_ref, grad_key_ref, grad_value_ref, part_ref,
):
    tokens, channels = query_ref.shape
    keep = lax.broadcasted_iota(jnp.int32, (tokens, tokens), 0) < count_ref[0]
    for head in range(channels // HEAD):
        lanes = slice(head * HEAD, (head + 1) * HEAD)
        result, grad_query, grad_key, grad_value, part = head_gradients(
            query_ref[:, lanes], key_ref[:, lanes], value_ref[:, lanes],
            mixed_ref[:, lanes], gate_ref[:, lanes], keep,
        )
        out_ref[:, lanes] = result
        grad_query_ref[:, lanes] = grad_query
        grad_key_ref[:, lanes] = grad_key
        grad_value_ref[:, lanes] = grad_value
        part_ref[:, lanes] = part


def in_vmem(count):
    return [pl.BlockSpec(memory_space=pltpu.VMEM)] * count


def attention_cost(tokens, channels):
    return pl.CostEstimate(
        flops=12 * tokens * tokens * channels,
        bytes_accessed=16 * tokens * channels,
        transcendentals=tokens * tokens * channels // HEAD,
    )


def time_attention(count, moved, grad_mixed, gate):
    frames, _, near, channels = moved.shape
    return pl.pallas_call(
        time_kernel,
        out_shape=(
            jax.ShapeDtypeStruct((frames, 4, near, channels), jnp.bfloat16),
            jax.ShapeDtypeStruct((1, channels), jnp.float32),
        ),
        in_specs=[pl.BlockSpec(memory_space=pltpu.SMEM)] + in_vmem(3),
        out_specs=tuple(in_vmem(2)),
        cost_estimate=attention_cost(frames * near, channels),
        compiler_params=pltpu.CompilerParams(vmem_limit_bytes=VMEM_BYTES),
        name="time_attention",
    )(count, moved, grad_mixed, gate)


def space_attention(count, query, key, value, grad_mixed, gate):
    tokens, channels = query.shape
    wide = jax.ShapeDtypeStruct((tokens, channels), jnp.float32)
    return pl.pallas_call(
        space_kernel,
        out_shape=(
            jax.ShapeDtypeStruct((tokens, channels), jnp.bfloat16),
            wide, wide, wide,
            jax.ShapeDtypeStruct((1, channels), jnp.float32),
        ),
        in_specs=[pl.BlockSpec(memory_space=pltpu.SMEM)] + in_vmem(5),
        out_specs=tuple(in_vmem(5)),
        cost_estimate=attention_cost(tokens, channels),
        compiler_params=pltpu.CompilerParams(vmem_limit_bytes=VMEM_BYTES),
        name="space_attention",
    )(count, query, key, value, grad_mixed, gate)


def tail_kernel(
    time_ref, moved_query_ref, moved_key_ref, moved_value_ref, space_ref,
    grad_query_ref, grad_key_ref, grad_value_ref, gate_space_ref, gate_time_ref, weight_ref,
    out_ref, out_query_ref, out_key_ref, out_value_ref, mixed_ref,
):
    tokens, columns = grad_query_ref.shape

    @pl.when(pl.program_id(0) == 0)
    def _():
        moved = time_ref[...].astype(jnp.float32).reshape(space_ref.shape)
        space = space_ref[...].astype(jnp.float32)
        mixed_ref[...] = (gate_space_ref[...] * space + gate_time_ref[...] * moved).astype(jnp.bfloat16)

    out_ref[...] = contract(mixed_ref[...], weight_ref[...], 1, 0).astype(jnp.bfloat16)
    for target, local, moved in (
        (out_query_ref, grad_query_ref, moved_query_ref),
        (out_key_ref, grad_key_ref, moved_key_ref),
        (out_value_ref, grad_value_ref, moved_value_ref),
    ):
        wide = moved[...].astype(jnp.float32).reshape(tokens, columns)
        target[...] = (local[...] + wide).astype(jnp.bfloat16)


def tail(returned, space, space_grads, gate_space, gate_time, weight, block=256):
    owners, _, near, channels = returned.shape
    tokens = owners * near

    def moved(which):
        return pl.BlockSpec((owners, 1, near, block), lambda j: (0, which, 0, j))

    whole = pl.BlockSpec((tokens, channels), lambda j: (0, 0))
    columns = pl.BlockSpec((tokens, block), lambda j: (0, j))
    gate = pl.BlockSpec((1, channels), lambda j: (0, 0))
    return pl.pallas_call(
        tail_kernel,
        grid=(channels // block,),
        out_shape=(jax.ShapeDtypeStruct((tokens, channels), jnp.bfloat16),) * 4,
        in_specs=[
            pl.BlockSpec((owners, 1, near, channels), lambda j: (0, 0, 0, 0)),
            moved(1), moved(2), moved(3), whole, columns, columns, columns, gate, gate,
            pl.BlockSpec((channels, block), lambda j: (0, j)),
        ],
        out_specs=(columns,) * 4,
        scratch_shapes=[pltpu.VMEM((tokens, channels), jnp.bfloat16)],
        compiler_params=pltpu.CompilerParams(vmem_limit_bytes=VMEM_BYTES),
        name="tail",
    )(returned, returned, returned, returned, space, *space_grads, gate_space, gate_time, weight)


def ring_of_four(block, axis):
    def shift(array, by):
        return lax.ppermute(array, axis, [(i, (i + by) % 4) for i in range(4)])

    half = block.shape[0] // 2
    before, after = shift(block, 1), shift(block, -1)
    across = jnp.concatenate([shift(before[:half], 1), shift(after[half:], -1)], axis=0)
    ring = jnp.stack([block, after, across, before] * 2)
    start = (4 - lax.axis_index(axis)) % 4
    return lax.dynamic_slice_in_dim(ring, start, 4, axis=0)


def own_pieces(out_weight):
    rows, channels = out_weight.shape
    wide = channels // lax.axis_size("x")
    block = lax.dynamic_slice_in_dim(out_weight, lax.axis_index("x") * wide, wide, axis=1)
    side = block.reshape(rows // ROWS, ROWS, wide).transpose(1, 0, 2).reshape(ROWS, rows * wide // ROWS)
    start = lax.axis_index("core") * (PIECES - 1) * HEAD
    return lax.dynamic_slice_in_dim(side, start, PIECES * HEAD, axis=1)


def whole_weight(pieces, rows, channels):
    seq = pieces.shape[0]
    along_y = ring_of_four(pieces, "fsdp")
    along_x = ring_of_four(along_y.reshape(4 * seq, ROWS, PIECES * HEAD), "x")
    other = lax.ppermute(along_x, "core", [(0, 1), (1, 0)])
    first = lax.axis_index("core") == 0
    low, high = jnp.where(first, along_x, other), jnp.where(first, other, along_x)
    side = jnp.concatenate([low, high[..., HEAD:]], axis=-1)
    wide = channels // 4
    side = side.reshape(4, 4 * seq, ROWS, rows // ROWS, wide)
    return side.transpose(1, 3, 2, 0, 4).reshape(channels, channels)


def all_sum(array, axis):
    return jnp.sum(lax.all_gather(array, axis, axis=0, tiled=True), axis=0, keepdims=True)


def on_device(
    query_states,
    key_states,
    value_states,
    out_weight,
    gate_space,
    gate_time,
    upstream,
    frame_count,
    pos_count,
):
    _, frames_here, positions, channels = query_states.shape
    owners = lax.axis_size("seq")
    near = positions // owners
    rows = out_weight.shape[0]
    gate_space, gate_time = gate_space.reshape(1, channels), gate_time.reshape(1, channels)
    query, key, value, flat_up = (
        array.reshape(positions, channels)
        for array in (query_states, key_states, value_states, upstream)
    )

    def exchange(array):
        return lax.all_to_all(array, "seq", split_axis=0, concat_axis=0, tiled=True)

    pieces = jnp.broadcast_to(own_pieces(out_weight), (owners, ROWS, PIECES * HEAD))
    first = exchange(jnp.concatenate([flat_up.reshape(owners, near, channels), pieces], axis=-1))
    second = jnp.stack([array.reshape(owners, near, channels) for array in (query, key, value)], axis=1)
    first, second = lax.optimization_barrier((first, second))
    moved = exchange(second)

    weight = whole_weight(first[..., channels:], rows, channels)
    both = jnp.concatenate([flat_up, first[..., :channels].reshape(positions, channels)], axis=0)
    grad_mixed = jnp.einsum("td,nd->tn", both, weight, preferred_element_type=jnp.float32)
    here, there = grad_mixed[:positions], grad_mixed[positions:]

    back, part_time = time_attention(frame_count, moved, there, gate_time)
    returned = exchange(back)

    space, *space_grads, part_space = space_attention(pos_count, query, key, value, here, gate_space)
    parts = jnp.concatenate([part_space, part_time], axis=1)
    for axis in (("x", "core"), "fsdp", "seq"):
        parts = all_sum(parts, axis)
    tokens = lax.axis_size("x") * lax.axis_size("core") * lax.axis_size("fsdp") * owners * frames_here * positions
    totals = parts[0] / math.sqrt(tokens)

    results = tail(returned, space, space_grads, gate_space, gate_time, weight)
    shaped = tuple(array.reshape(query_states.shape) for array in results)
    return shaped + (totals[:channels], totals[channels:])


def solution(mesh):
    chips = mesh.shape["dp"] // 2
    split = Mesh(
        mesh.devices.reshape(chips, 2, mesh.shape["fsdp"], mesh.shape["seq"]),
        ("x", "core", "fsdp", "seq"),
    )
    clips = ("x", "core", "fsdp")
    states = P(clips, "seq", None, None)
    return jax.shard_map(
        on_device,
        mesh=split,
        in_specs=(states, states, states, P(("fsdp", "seq"), None), P(), P(), states, P(clips), P(clips)),
        out_specs=(states, states, states, states, P(), P()),
        check_vma=False,
    )
```

time: 412 us -> 288 us (0.70)
  blocking collectives: 201 us -> 88.4 us
  matrix products: 33.5 us -> 1.41 us
  starting transfers between devices: 32.7 us -> 59 us
  waiting for transfers between devices: 111 us -> 84.9 us
  local copies, waits for them, and re-layouts: 10.2 us -> 31.8 us
  between operations: 15.7 us -> 2.49 us
  Pallas kernels: 0 us -> 8.64 us
  other arithmetic: 4.77 us -> 9.52 us
    psum x1 -> x0, blocking collectives: 105 us -> none  [on_device(): gate_totals = lax.psum((part_space, part_time), ('dp', 'fsdp', 'seq'))]
    all_to_all x3 -> x0, blocking collectives: 95.9 us -> none  [the longest x1 39.9 us: on_device(): lax.all_to_all(owned[1], 'seq', split_axis=1, concat_axis=0, tiled=True)]
    all_gather x0 -> x3, blocking collectives: none -> 88.4 us  [all_sum(): lax.all_gather(array, axis, axis=0, tiled=True)]
    all_gather x1 -> x0, waiting for transfers between devices: 39.6 us -> none  [on_device(): lax.all_gather(out_weight, ('fsdp', 'seq'), axis=0, tiled=True)]
    dot_general x12 -> x1, matrix products: 30.8 us -> 1.41 us  [on_device(): jnp.einsum('td,nd->tn', both, weight, preferred_element_type=jnp.float32)]
    ppermute x0 -> x9, starting transfers between devices: none -> 28.1 us  [the longest x8 26.1 us: shift(): return lax.ppermute(array, axis, [(i, (i + by) % 4) for i in range(4)])]
    ppermute x0 -> x9, waiting for transfers between devices: none -> 25 us  [the longest x8 25 us: shift(): return lax.ppermute(array, axis, [(i, (i + by) % 4) for i in range(4)])]
    unnamed x43 -> x54, local copies, waits for them, and re-layouts: 0.75 us -> 14.2 us
  transfers between devices with their start and end apart: 6 -> 12, of which waited for: 5 -> 8; matrix products, arithmetic and copies ran while one was open for 9% -> 9% of each run, Pallas kernels for 0% -> 0%
where the time goes in v1:
time: 288 us; the launch traced here: 286 us
  blocking collectives  88.4 us (31%)
  waiting for transfers between devices  84.9 us (29%)
  starting transfers between devices  59 us (20%)
  local copies, waits for them, and re-layouts  31.8 us (11%)
  other arithmetic  9.52 us (3%)
  Pallas kernels  8.64 us (3%)
    all_gather x3, blocking collectives, all_sum(): lax.all_gather(array, axis, axis=0, tiled=True)  88.4 us
    all_to_all x3, waiting for transfers between devices, exchange(): return lax.all_to_all(array, 'seq', split_axis=0, concat_axis=0, tiled=True)  59.9 us
    all_to_all x3, starting transfers between devices, exchange(): return lax.all_to_all(array, 'seq', split_axis=0, concat_axis=0, tiled=True)  30.9 us
    ppermute x8, starting transfers between devices, shift(): return lax.ppermute(array, axis, [(i, (i + by) % 4) for i in range(4)])  26.1 us
    ppermute x8, waiting for transfers between devices, shift(): return lax.ppermute(array, axis, [(i, (i + by) % 4) for i in range(4)])  25 us
    unnamed x54, local copies, waits for them, and re-layouts  14.2 us
    reshape x1, local copies, waits for them, and re-layouts, whole_weight(): side = side.reshape(4, 4 * seq, ROWS, rows // ROWS, wide)  11 us
    pallas_call x1, Pallas kernels, tail(): pl.pallas_call(tail_kernel, grid=(channels // block,), out_shape=(jax.Sha...  6.06 us
  transfers between devices with their start and end apart: 12, of which 8 were waited for; matrix products, arithmetic and copies ran while one was open for 9% of the time, Pallas kernels for 0%

profile of v1, /device:TPU:6, one launch (start us, length us, event | category | flops | bytes accessed | tf_op | source)
XLA Modules:
  0.0 286.2 jit_solution(10760078477546282675)
XLA Ops:
  0.7 0.8 copy-done
  1.6 1.8 pad_maximum_fusion.2
  3.4 15.2 %all-to-all-start = ((bf16[16,8,2176]{2,1,0:T(8,128)(2,1)}), bf16[16,8,2176]{2,1,0:T(8,128)(2,1)S(1)}, u32[]{:S(2)}, u32[]{:S(2)}) async-start(bf16[16,8,2176]{2,1,0:T(8,128)(2,1)} %pad_maximum_fusion.2), calls=%async_computation | async-start | bytes 1114112 | tf_op jit(solution)/shard_map/all_to_all | solution.py:241
  18.6 1.2 pad_maximum_fusion.1
  19.8 28.7 %all-to-all-done = bf16[16,8,2176]{2,1,0:T(8,128)(2,1)S(1)} async-done(((bf16[16,8,2176]{2,1,0:T(8,128)(2,1)}), bf16[16,8,2176]{2,1,0:T(8,128)(2,1)S(1)}, u32[]{:S(2)}, u32[]{:S(2)}) %all-to-all-start) | async-done | bytes 557088 | tf_op jit(solution)/shard_map/all_to_all | solution.py:241
  48.6 4.9 %collective-permute-start = (bf16[16,8,640]{2,1,0:T(8,128)(2,1)S(1)}, bf16[16,8,640]{2,1,0:T(8,128)(2,1)S(1)}, u32[]{:S(2)}, u32[]{:S(2)}) collective-permute-start(bf16[16,8,640]{2,1,0:T(8,128)(2,1)S(1)} %slice.34), channel_id=1, source_target_pairs={{0,48},{16,0},{32,16},{48,32},{1,49},{17,1},{33,17},{49,33},{2,50}... | collective-permute-start | bytes 491528 | tf_op jit(solution)/shard_map/ppermute | solution.py:183
  53.5 1.9 collective-permute-start.1
  55.4 1.6 collective-permute-done
  57.0 5.6 %collective-permute-start.3 = (bf16[8,8,640]{2,1,0:T(8,128)(2,1)S(1)}, bf16[8,8,640]{2,1,0:T(8,128)(2,1)S(1)}, u32[]{:S(2)}, u32[]{:S(2)}) collective-permute-start(bf16[8,8,640]{2,1,0:T(8,128)(2,1)S(1)} %slice.45), channel_id=1, source_target_pairs={{0,48},{16,0},{32,16},{48,32},{1,49},{17,1},{33,17},{49,33},{2,50}... | collective-permute-start | bytes 245768 | tf_op jit(solution)/shard_map/ppermute | solution.py:183
  62.7 1.9 collective-permute-start.2
  64.7 5.5 %collective-permute-done.2 = bf16[8,8,640]{2,1,0:T(8,128)(2,1)S(1)} collective-permute-done((bf16[8,8,640]{2,1,0:T(8,128)(2,1)S(1)}, bf16[8,8,640]{2,1,0:T(8,128)(2,1)S(1)}, u32[]{:S(2)}, u32[]{:S(2)}) %collective-permute-start.2) | collective-permute-done | bytes 81952 | tf_op jit(solution)/shard_map/ppermute | solution.py:183
  70.5 2.4 collective-permute-start.5
  72.9 3.5 %collective-permute-start.4 = (bf16[64,8,640]{2,1,0:T(8,128)(2,1)S(1)}, bf16[64,8,640]{2,1,0:T(8,128)(2,1)S(1)}, u32[]{:S(2)}, u32[]{:S(2)}) collective-permute-start(bf16[64,8,640]{2,1,0:T(8,128)(2,1)S(1)} %bitcast.69), channel_id=1, source_target_pairs={{0,384},{128,0},{256,128},{384,256},{1,385},{129,1},{257,129},{385... | collective-permute-start | bytes 1966088 | tf_op jit(solution)/shard_map/ppermute | solution.py:183
  76.3 10.1 %collective-permute-done.5 = bf16[64,8,640]{2,1,0:T(8,128)(2,1)S(1)} collective-permute-done((bf16[64,8,640]{2,1,0:T(8,128)(2,1)S(1)}, bf16[64,8,640]{2,1,0:T(8,128)(2,1)S(1)}, u32[]{:S(2)}, u32[]{:S(2)}) %collective-permute-start.5) | collective-permute-done | bytes 655392 | tf_op jit(solution)/shard_map/ppermute | solution.py:183
  86.5 3.6 %collective-permute-start.6 = (bf16[32,8,640]{2,1,0:T(8,128)(2,1)S(1)}, bf16[32,8,640]{2,1,0:T(8,128)(2,1)S(1)}, u32[]{:S(2)}, u32[]{:S(2)}) collective-permute-start(bf16[32,8,640]{2,1,0:T(8,128)(2,1)S(1)} %slice.46), channel_id=1, source_target_pairs={{0,128},{128,256},{256,384},{384,0},{1,129},{129,257},{257,385},{3... | collective-permute-start | bytes 983048 | tf_op jit(solution)/shard_map/ppermute | solution.py:183
  90.1 2.2 collective-permute-start.7
  92.6 2.9 %collective-permute-done.6 = bf16[32,8,640]{2,1,0:T(8,128)(2,1)S(1)} collective-permute-done((bf16[32,8,640]{2,1,0:T(8,128)(2,1)S(1)}, bf16[32,8,640]{2,1,0:T(8,128)(2,1)S(1)}, u32[]{:S(2)}, u32[]{:S(2)}) %collective-permute-start.6) | collective-permute-done | bytes 327712 | tf_op jit(solution)/shard_map/ppermute | solution.py:183
  95.5 4.9 %collective-permute-done.7 = bf16[32,8,640]{2,1,0:T(8,128)(2,1)S(1)} collective-permute-done((bf16[32,8,640]{2,1,0:T(8,128)(2,1)S(1)}, bf16[32,8,640]{2,1,0:T(8,128)(2,1)S(1)}, u32[]{:S(2)}, u32[]{:S(2)}) %collective-permute-start.7) | collective-permute-done | bytes 327712 | tf_op jit(solution)/shard_map/ppermute | solution.py:183
  101.0 1.9 constant_dynamic-slice_fusion
  102.9 1.3 copy-done.17
  104.2 2.0 collective-permute-start.8
  106.2 7.0 %all-to-all-start.1 = ((bf16[16,3,8,1536]{3,2,1,0:T(8,128)(2,1)}), bf16[16,3,8,1536]{3,2,1,0:T(8,128)(2,1)S(1)}, u32[]{:S(2)}, u32[]{:S(2)}) async-start(bf16[16,3,8,1536]{3,2,1,0:T(8,128)(2,1)} %pad_maximum_fusion.1), calls=%async_computation.1 | async-start | bytes 2359296 | tf_op jit(solution)/shard_map/all_to_all | solution.py:241
  114.0 3.0 %dynamic-slice_select_fusion = bf16[4,64,8,512]{3,2,1,0:T(8,128)(2,1)S(1)} fusion(bf16[8,64,8,640]{3,2,1,0:T(8,128)(2,1)} %copy-done.17, s32[]{:T(128)S(6)} %select_n.41, s32[]{:T(128)S(6)} %add.25, bf16[4,64,8,640]{3,2,1,0:T(8,128)(2,1)} %collective-permute-done.8, pred[]{:T(512)S(6)} %eq.6), kind=kLoop, calls=%fused_computation.2 | loop fusion | flops 1048576 | bytes 6291465 | tf_op jit(solution)/shard_map/jit(_where)/select_n | solution.py:208
  117.0 0.7 copy-done.18
  118.1 2.7 pad_maximum_fusion
  120.8 11.0 %reshape.65 = bf16[4,64,8,3,384]{4,3,2,1,0:T(4,128)(2,1)} reshape(bf16[4,64,8,1152]{3,2,1,0:T(8,128)(2,1)} %pad_maximum_fusion) | data formatting | bytes 9437184 | tf_op jit(solution)/shard_map/reshape | solution.py:211
  131.8 3.6 %copy.17 = bf16[64,3,8,4,384]{4,2,3,1,0:T(8,128)(2,1)S(1)} copy(bf16[64,3,8,4,384]{4,1,2,0,3:T(4,128)(2,1)} %bitcast.65) | data formatting | bytes 9437184 | tf_op jit(solution)/shard_map/transpose | solution.py:212
  135.4 1.4 fusion
  136.8 0.7 copy-done.16
  137.6 31.2 %all-to-all-done.1.moved_ref = bf16[16,3,8,1536]{3,2,1,0:T(8,128)(2,1)S(1)} async-done(((bf16[16,3,8,1536]{3,2,1,0:T(8,128)(2,1)}), bf16[16,3,8,1536]{3,2,1,0:T(8,128)(2,1)S(1)}, u32[]{:S(2)}, u32[]{:S(2)}) %all-to-all-start.1) | async-done | bytes 1179680 | tf_op jit(solution)/shard_map/all_to_all | solution.py:241
  168.8 1.3 time_attention.1
  170.1 1.2 copy-done.7
  171.3 8.7 %all-to-all-start.2 = ((bf16[16,4,8,1536]{3,2,1,0:T(8,128)(2,1)}), bf16[16,4,8,1536]{3,2,1,0:T(8,128)(2,1)S(1)}, u32[]{:S(2)}, u32[]{:S(2)}) async-start(bf16[16,4,8,1536]{3,2,1,0:T(8,128)(2,1)} %copy-done.7), calls=%async_computation.2 | async-start | bytes 3145728 | tf_op jit(solution)/shard_map/all_to_all | solution.py:241
  180.8 1.0 copy-done.6
  181.7 1.3 space_attention.1
  183.0 0.9 copy-done.8
  183.9 0.9 copy-done.10
  184.8 0.9 copy-done.12
  185.8 0.7 copy-done.14
  186.5 12.7 %all-gather.2 = f32[8,1,3072]{2,1,0:T(1,128)S(1)} all-gather(f32[1,1,3072]{2,1,0:T(1,128)S(1)} %maximum_bitcast_fusion.2), channel_id=1, replica_groups=mesh['x'=4,'core'=2,'fsdp'=4,'seq'=16] {'x','core'}, dimensions={0}, use_global_device_ids=true | all-gather | bytes 110592 | tf_op jit(solution)/shard_map/all_gather | solution.py:216
  199.3 11.9 %all-gather = f32[12288]{0:T(1024)S(1)} all-gather(f32[3072]{0:T(1024)S(1)} %reduce_sum.27), channel_id=2, replica_groups=mesh['x'=4,'core'=2,'fsdp'=4,'seq'=16] {'fsdp'}, dimensions={0}, use_global_device_ids=true | all-gather | bytes 61440 | tf_op jit(solution)/shard_map/all_gather | solution.py:216
  211.3 63.8 %all-gather.1 = f32[49152]{0:T(1024)S(1)} all-gather(f32[3072]{0:T(1024)S(1)} %reduce_sum.28), channel_id=3, replica_groups=mesh['x'=4,'core'=2,'fsdp'=4,'seq'=16] {'seq'}, dimensions={0}, use_global_device_ids=true | all-gather | bytes 208896 | tf_op jit(solution)/shard_map/all_gather | solution.py:216
  275.1 0.6 fusion.10
  275.7 1.1 copy-done.9
  276.9 1.1 copy-done.11
  278.0 1.1 copy-done.13
  279.1 1.0 copy-done.15
  280.1 6.1 %tail.1 = (bf16[128,1536]{1,0:T(8,128)(2,1)}, bf16[128,1536]{1,0:T(8,128)(2,1)}, bf16[128,1536]{1,0:T(8,128)(2,1)}, bf16[128,1536]{1,0:T(8,128)(2,1)}) custom-call(bf16[16,4,8,1536]{3,2,1,0:T(8,128)(2,1)S(1)} %all-to-all-done.2.time_ref.moved_query_ref.moved_key_ref.moved_value_ref, ...), custom_call_target="tpu_custom_call" | custom-call | tf_op jit(solution)/shard_map/tail/pallas_call | solution.py:165
  (72 shorter events, 2.0 us)
Async XLA Ops:
  0.6 0.9 copy-start
  0.6 18.0 %copy-start.5 = (bf16[1,1,128,1536]{3,2,1,0:T(8,128)(2,1)S(1)}, bf16[1,1,128,1536]{3,2,1,0:T(8,128)(2,1)}, u32[]{:S(2)}) copy-start(bf16[1,1,128,1536]{3,2,1,0:T(8,128)(2,1)} %param.9) | copy-start | bytes 1179652
  0.7 18.0 %copy-start.3 = (bf16[1,1,128,1536]{3,2,1,0:T(8,128)(2,1)S(1)}, bf16[1,1,128,1536]{3,2,1,0:T(8,128)(2,1)}, u32[]{:S(2)}) copy-start(bf16[1,1,128,1536]{3,2,1,0:T(8,128)(2,1)} %param.10) | copy-start | bytes 1179652
  0.7 18.0 %copy-start.1 = (bf16[1,1,128,1536]{3,2,1,0:T(8,128)(2,1)S(1)}, bf16[1,1,128,1536]{3,2,1,0:T(8,128)(2,1)}, u32[]{:S(2)}) copy-start(bf16[1,1,128,1536]{3,2,1,0:T(8,128)(2,1)} %param.11) | copy-start | bytes 1179652
  3.4 45.2 %all-to-all-start = ((bf16[16,8,2176]{2,1,0:T(8,128)(2,1)}), bf16[16,8,2176]{2,1,0:T(8,128)(2,1)S(1)}, u32[]{:S(2)}, u32[]{:S(2)}) async-start(bf16[16,8,2176]{2,1,0:T(8,128)(2,1)} %pad_maximum_fusion.2), calls=%async_computation | async-start | bytes 1114112 | tf_op jit(solution)/shard_map/all_to_all | solution.py:241
  48.6 8.5 %collective-permute-start = (bf16[16,8,640]{2,1,0:T(8,128)(2,1)S(1)}, bf16[16,8,640]{2,1,0:T(8,128)(2,1)S(1)}, u32[]{:S(2)}, u32[]{:S(2)}) collective-permute-start(bf16[16,8,640]{2,1,0:T(8,128)(2,1)S(1)} %slice.34), channel_id=1, source_target_pairs={{0,48},{16,0},{32,16},{48,32},{1,49},{17,1},{33,17},{49,33},{2,50}... | collective-permute-start | bytes 491528 | tf_op jit(solution)/shard_map/ppermute | solution.py:183
  53.5 9.2 %collective-permute-start.1 = (bf16[16,8,640]{2,1,0:T(8,128)(2,1)S(1)}, bf16[16,8,640]{2,1,0:T(8,128)(2,1)S(1)}, u32[]{:S(2)}, u32[]{:S(2)}) collective-permute-start(bf16[16,8,640]{2,1,0:T(8,128)(2,1)S(1)} %slice.34), channel_id=1, source_target_pairs={{0,16},{16,32},{32,48},{48,0},{1,17},{17,33},{33,49},{49,1},{2,18}... | collective-permute-start | bytes 491528 | tf_op jit(solution)/shard_map/ppermute | solution.py:183
  57.0 7.6 %collective-permute-start.3 = (bf16[8,8,640]{2,1,0:T(8,128)(2,1)S(1)}, bf16[8,8,640]{2,1,0:T(8,128)(2,1)S(1)}, u32[]{:S(2)}, u32[]{:S(2)}) collective-permute-start(bf16[8,8,640]{2,1,0:T(8,128)(2,1)S(1)} %slice.45), channel_id=1, source_target_pairs={{0,48},{16,0},{32,16},{48,32},{1,49},{17,1},{33,17},{49,33},{2,50}... | collective-permute-start | bytes 245768 | tf_op jit(solution)/shard_map/ppermute | solution.py:183
  62.7 7.5 %collective-permute-start.2 = (bf16[8,8,640]{2,1,0:T(8,128)(2,1)S(1)}, bf16[8,8,640]{2,1,0:T(8,128)(2,1)S(1)}, u32[]{:S(2)}, u32[]{:S(2)}) collective-permute-start(bf16[8,8,640]{2,1,0:T(8,128)(2,1)S(1)} %slice.44), channel_id=1, source_target_pairs={{0,16},{16,32},{32,48},{48,0},{1,17},{17,33},{33,49},{49,1},{2,18}... | collective-permute-start | bytes 245768 | tf_op jit(solution)/shard_map/ppermute | solution.py:183
  70.5 16.0 %collective-permute-start.5 = (bf16[64,8,640]{2,1,0:T(8,128)(2,1)S(1)}, bf16[64,8,640]{2,1,0:T(8,128)(2,1)S(1)}, u32[]{:S(2)}, u32[]{:S(2)}) collective-permute-start(bf16[64,8,640]{2,1,0:T(8,128)(2,1)S(1)} %bitcast.68), channel_id=1, source_target_pairs={{0,128},{128,256},{256,384},{384,0},{1,129},{129,257},{257,385},{3... | collective-permute-start | bytes 1966088 | tf_op jit(solution)/shard_map/ppermute | solution.py:183
  72.9 17.2 %collective-permute-start.4 = (bf16[64,8,640]{2,1,0:T(8,128)(2,1)S(1)}, bf16[64,8,640]{2,1,0:T(8,128)(2,1)S(1)}, u32[]{:S(2)}, u32[]{:S(2)}) collective-permute-start(bf16[64,8,640]{2,1,0:T(8,128)(2,1)S(1)} %bitcast.69), channel_id=1, source_target_pairs={{0,384},{128,0},{256,128},{384,256},{1,385},{129,1},{257,129},{385... | collective-permute-start | bytes 1966088 | tf_op jit(solution)/shard_map/ppermute | solution.py:183
  86.5 9.0 %collective-permute-start.6 = (bf16[32,8,640]{2,1,0:T(8,128)(2,1)S(1)}, bf16[32,8,640]{2,1,0:T(8,128)(2,1)S(1)}, u32[]{:S(2)}, u32[]{:S(2)}) collective-permute-start(bf16[32,8,640]{2,1,0:T(8,128)(2,1)S(1)} %slice.46), channel_id=1, source_target_pairs={{0,128},{128,256},{256,384},{384,0},{1,129},{129,257},{257,385},{3... | collective-permute-start | bytes 983048 | tf_op jit(solution)/shard_map/ppermute | solution.py:183
  90.1 10.2 %collective-permute-start.7 = (bf16[32,8,640]{2,1,0:T(8,128)(2,1)S(1)}, bf16[32,8,640]{2,1,0:T(8,128)(2,1)S(1)}, u32[]{:S(2)}, u32[]{:S(2)}) collective-permute-start(bf16[32,8,640]{2,1,0:T(8,128)(2,1)S(1)} %slice.47), channel_id=1, source_target_pairs={{0,384},{128,0},{256,128},{384,256},{1,385},{129,1},{257,129},{385... | collective-permute-start | bytes 983048 | tf_op jit(solution)/shard_map/ppermute | solution.py:183
  101.0 3.2 %copy-start.17 = (bf16[8,64,8,640]{3,2,1,0:T(8,128)(2,1)}, bf16[8,64,8,640]{3,2,1,0:T(8,128)(2,1)S(1)}, u32[]{:S(2)}) copy-start(bf16[8,64,8,640]{3,2,1,0:T(8,128)(2,1)S(1)} %bitcast_dynamic-update-slice_fusion.1) | copy-start | bytes 15728644
  104.2 9.7 %copy-start.20 = (f32[1536]{0:T(1024)S(1)}, f32[1536]{0:T(1024)}, u32[]{:S(2)}) copy-start(f32[1536]{0:T(1024)} %param.14) | copy-start | bytes 18436
  104.2 9.7 %collective-permute-start.8 = (bf16[4,64,8,640]{3,2,1,0:T(8,128)(2,1)}, bf16[4,64,8,640]{3,2,1,0:T(8,128)(2,1)}, u32[]{:S(2)}, u32[]{:S(2)}) collective-permute-start(bf16[4,64,8,640]{3,2,1,0:T(8,128)(2,1)} %constant_dynamic-slice_fusion), channel_id=1, source_target_pairs={{0,64},{64,0},{1,65},{65,1},{2,66},{66,2},{3,67},{67,3},{4,68},{68... | collective-permute-start | bytes 7864328 | tf_op jit(solution)/shard_map/ppermute | solution.py:206
  106.2 62.5 %all-to-all-start.1 = ((bf16[16,3,8,1536]{3,2,1,0:T(8,128)(2,1)}), bf16[16,3,8,1536]{3,2,1,0:T(8,128)(2,1)S(1)}, u32[]{:S(2)}, u32[]{:S(2)}) async-start(bf16[16,3,8,1536]{3,2,1,0:T(8,128)(2,1)} %pad_maximum_fusion.1), calls=%async_computation.1 | async-start | bytes 2359296 | tf_op jit(solution)/shard_map/all_to_all | solution.py:241
  113.9 3.7 %copy-start.18 = (bf16[8,64,8,640]{3,2,1,0:T(8,128)(2,1)S(1)}, bf16[8,64,8,640]{3,2,1,0:T(8,128)(2,1)}, u32[]{:S(2)}) copy-start(bf16[8,64,8,640]{3,2,1,0:T(8,128)(2,1)} %copy-done.17) | copy-start | bytes 15728644
  131.7 3.6 %copy-start.19 = (bf16[1,1,128,1536]{3,2,1,0:T(8,128)(2,1)S(1)}, bf16[1,1,128,1536]{3,2,1,0:T(8,128)(2,1)}, u32[]{:S(2)}) copy-start(bf16[1,1,128,1536]{3,2,1,0:T(8,128)(2,1)} %param.15) | copy-start | bytes 1179652
  135.4 2.1 copy-start.16
  168.8 11.9 %copy-start.21 = (f32[1536]{0:T(1024)S(1)}, f32[1536]{0:T(1024)}, u32[]{:S(2)}) copy-start(f32[1536]{0:T(1024)} %param.13) | copy-start | bytes 18436
  170.1 1.2 copy-start.7
  171.3 9.4 %copy-start.2 = (bf16[1,1,128,1536]{3,2,1,0:T(8,128)(2,1)S(1)}, bf16[1,1,128,1536]{3,2,1,0:T(8,128)(2,1)}, u32[]{:S(2)}) copy-start(bf16[1,1,128,1536]{3,2,1,0:T(8,128)(2,1)} %param.11) | copy-start | bytes 1179652
  171.3 9.4 %copy-start.4 = (bf16[1,1,128,1536]{3,2,1,0:T(8,128)(2,1)S(1)}, bf16[1,1,128,1536]{3,2,1,0:T(8,128)(2,1)}, u32[]{:S(2)}) copy-start(bf16[1,1,128,1536]{3,2,1,0:T(8,128)(2,1)} %param.10) | copy-start | bytes 1179652
  171.3 104.4 %all-to-all-start.2 = ((bf16[16,4,8,1536]{3,2,1,0:T(8,128)(2,1)}), bf16[16,4,8,1536]{3,2,1,0:T(8,128)(2,1)S(1)}, u32[]{:S(2)}, u32[]{:S(2)}) async-start(bf16[16,4,8,1536]{3,2,1,0:T(8,128)(2,1)} %copy-done.7), calls=%async_computation.2 | async-start | bytes 3145728 | tf_op jit(solution)/shard_map/all_to_all | solution.py:241
  180.7 1.0 copy-start.6
  183.0 0.9 copy-start.8
  183.9 0.9 copy-start.10
  184.8 0.9 copy-start.12
  185.8 0.7 copy-start.14
  275.7 1.1 copy-start.9
  276.9 1.1 copy-start.11
  278.0 1.1 copy-start.13
  279.1 1.0 copy-start.15

commit v2 on v1

v2 whole, which is shorter than its diff:
```python
import functools
import math

import jax
import jax.numpy as jnp
from jax import lax
from jax.experimental import pallas as pl
from jax.experimental.pallas import tpu as pltpu
from jax.sharding import Mesh, PartitionSpec as P

HEAD = 128
NEGATIVE = -1e30
VMEM_BYTES = 20 * 1024 * 1024
DISTANCES = (((0, 8), (4, -4)), ((1, -1), (7, -7)), ((2, -2), (6, -6)), ((3, -3), (5, -5)))


def contract(left, right, left_dim, right_dim):
    return lax.dot_general(
        left,
        right,
        (((left_dim,), (right_dim,)), ((), ())),
        preferred_element_type=jnp.float32,
    )


def head_gradients(query, key, value, grad_mixed, gate, keep):
    scale = HEAD ** (-0.5)
    incoming = (gate * grad_mixed).astype(jnp.bfloat16)
    scores = jnp.where(keep, contract(key, query, 1, 1) * scale, NEGATIVE)
    raised = jnp.exp(scores - jnp.max(scores, axis=0, keepdims=True))
    probs = raised / jnp.sum(raised, axis=0, keepdims=True)
    rounded = probs.astype(jnp.bfloat16)
    result = contract(rounded, value, 0, 0).astype(jnp.bfloat16)
    part = jnp.sum(grad_mixed * result.astype(jnp.float32), axis=0, keepdims=True)
    grad_value = contract(rounded, incoming, 1, 0)
    grad_probs = contract(value, incoming, 1, 1)
    inner = jnp.sum(probs * grad_probs, axis=0, keepdims=True)
    grad_scores = (probs * (grad_probs - inner) * scale).astype(jnp.bfloat16)
    grad_query = contract(grad_scores, key, 0, 0)
    grad_key = contract(grad_scores, query, 1, 0)
    return result, grad_query, grad_key, grad_value, part


def time_kernel(count_ref, moved_ref, mixed_ref, gate_ref, out_ref, grad_ref, part_ref):
    frames, _, near, channels = moved_ref.shape
    tokens = frames * near
    key_at = lax.broadcasted_iota(jnp.int32, (tokens, tokens), 0)
    query_at = lax.broadcasted_iota(jnp.int32, (tokens, tokens), 1)
    keep = (key_at % near == query_at % near) & (key_at < count_ref[0] * near)
    for head in range(channels // HEAD):
        lanes = slice(head * HEAD, (head + 1) * HEAD)

        def load(which):
            wide = moved_ref[:, which, :, lanes].astype(jnp.float32)
            return wide.reshape(tokens, HEAD).astype(jnp.bfloat16)

        result, grad_query, grad_key, grad_value, part = head_gradients(
            load(0), load(1), load(2), mixed_ref[:, lanes], gate_ref[:, lanes], keep
        )
        part_ref[:, lanes] = part
        for target, which, array in (
            (out_ref, 0, result), (out_ref, 1, grad_query), (grad_ref, 0, grad_key), (grad_ref, 1, grad_value),
        ):
            wide = array.astype(jnp.float32).reshape(frames, near, HEAD)
            target[:, which, :, lanes] = wide.astype(jnp.bfloat16)


def space_kernel(
    count_ref, query_ref, key_ref, value_ref, mixed_ref, gate_ref,
    out_ref, grad_query_ref, grad_key_ref, grad_value_ref, part_ref,
):
    tokens, channels = query_ref.shape
    keep = lax.broadcasted_iota(jnp.int32, (tokens, tokens), 0) < count_ref[0]
    for head in range(channels // HEAD):
        lanes = slice(head * HEAD, (head + 1) * HEAD)
        result, grad_query, grad_key, grad_value, part = head_gradients(
            query_ref[:, lanes], key_ref[:, lanes], value_ref[:, lanes],
            mixed_ref[:, lanes], gate_ref[:, lanes], keep,
        )
        out_ref[:, lanes] = result
        grad_query_ref[:, lanes] = grad_query
        grad_key_ref[:, lanes] = grad_key
        grad_value_ref[:, lanes] = grad_value
        part_ref[:, lanes] = part


def in_vmem(count):
    return [pl.BlockSpec(memory_space=pltpu.VMEM)] * count


def attention_cost(tokens, channels):
    return pl.CostEstimate(
        flops=12 * tokens * tokens * channels,
        bytes_accessed=16 * tokens * channels,
        transcendentals=tokens * tokens * channels // HEAD,
    )


def time_attention(count, moved, grad_mixed, gate):
    frames, _, near, channels = moved.shape
    pair = jax.ShapeDtypeStruct((frames, 2, near, channels), jnp.bfloat16)
    return pl.pallas_call(
        time_kernel,
        out_shape=(pair, pair, jax.ShapeDtypeStruct((1, channels), jnp.float32)),
        in_specs=[pl.BlockSpec(memory_space=pltpu.SMEM)] + in_vmem(3),
        out_specs=tuple(in_vmem(3)),
        cost_estimate=attention_cost(frames * near, channels),
        compiler_params=pltpu.CompilerParams(vmem_limit_bytes=VMEM_BYTES),
        name="time_attention",
    )(count, moved, grad_mixed, gate)


def space_attention(count, query, key, value, grad_mixed, gate):
    tokens, channels = query.shape
    wide = jax.ShapeDtypeStruct((tokens, channels), jnp.float32)
    return pl.pallas_call(
        space_kernel,
        out_shape=(
            jax.ShapeDtypeStruct((tokens, channels), jnp.bfloat16),
            wide, wide, wide,
            jax.ShapeDtypeStruct((1, channels), jnp.float32),
        ),
        in_specs=[pl.BlockSpec(memory_space=pltpu.SMEM)] + in_vmem(5),
        out_specs=tuple(in_vmem(5)),
        cost_estimate=attention_cost(tokens, channels),
        compiler_params=pltpu.CompilerParams(vmem_limit_bytes=VMEM_BYTES),
        name="space_attention",
    )(count, query, key, value, grad_mixed, gate)


def combine(local, moved):
    wide = moved.astype(jnp.float32).reshape(local.shape)
    return (local + wide).astype(jnp.bfloat16)


def output_kernel(
    time_ref, moved_ref, space_ref, grad_ref, gate_space_ref, gate_time_ref, weight_ref,
    out_ref, out_grad_ref, mixed_ref,
):
    @pl.when(pl.program_id(0) == 0)
    def _():
        moved = time_ref[...].astype(jnp.float32).reshape(space_ref.shape)
        space = space_ref[...].astype(jnp.float32)
        mixed_ref[...] = (gate_space_ref[...] * space + gate_time_ref[...] * moved).astype(jnp.bfloat16)

    out_ref[...] = contract(mixed_ref[...], weight_ref[...], 1, 0).astype(jnp.bfloat16)
    out_grad_ref[...] = combine(grad_ref[...], moved_ref[...])


def output(returned, space, grad, gate_space, gate_time, weight, block=256):
    owners, _, near, channels = returned.shape
    tokens = owners * near
    whole = pl.BlockSpec((tokens, channels), lambda j: (0, 0))
    columns = pl.BlockSpec((tokens, block), lambda j: (0, j))
    gate = pl.BlockSpec((1, channels), lambda j: (0, 0))
    return pl.pallas_call(
        output_kernel,
        grid=(channels // block,),
        out_shape=(jax.ShapeDtypeStruct((tokens, channels), jnp.bfloat16),) * 2,
        in_specs=[
            pl.BlockSpec((owners, 1, near, channels), lambda j: (0, 0, 0, 0)),
            pl.BlockSpec((owners, 1, near, block), lambda j: (0, 1, 0, j)),
            whole, columns, gate, gate,
            pl.BlockSpec((channels, block), lambda j: (0, j)),
        ],
        out_specs=(columns,) * 2,
        scratch_shapes=[pltpu.VMEM((tokens, channels), jnp.bfloat16)],
        compiler_params=pltpu.CompilerParams(vmem_limit_bytes=VMEM_BYTES),
        name="output",
    )(returned, returned, space, grad, gate_space, gate_time, weight)


def add_kernel(moved_ref, key_ref, value_ref, out_key_ref, out_value_ref):
    out_key_ref[...] = combine(key_ref[...], moved_ref[:, 0])
    out_value_ref[...] = combine(value_ref[...], moved_ref[:, 1])


def add_returned(returned, grad_key, grad_value, block=512):
    owners, _, near, channels = returned.shape
    tokens = owners * near
    columns = pl.BlockSpec((tokens, block), lambda j: (0, j))
    return pl.pallas_call(
        add_kernel,
        grid=(channels // block,),
        out_shape=(jax.ShapeDtypeStruct((tokens, channels), jnp.bfloat16),) * 2,
        in_specs=[pl.BlockSpec((owners, 2, near, block), lambda j: (0, 0, 0, j)), columns, columns],
        out_specs=(columns,) * 2,
        compiler_params=pltpu.CompilerParams(vmem_limit_bytes=VMEM_BYTES),
        name="add_returned",
    )(returned, grad_key, grad_value)


def shift(array, axis, by):
    size = lax.axis_size(axis)
    return lax.ppermute(array, axis, [(i, (i + by) % size) for i in range(size)])


def ring_of_four(block, axis):
    half = block.shape[0] // 2
    before, after = shift(block, axis, 1), shift(block, axis, -1)
    across = (shift(before[:half], axis, 1), shift(after[half:], axis, -1))
    return after, across, before


def fetch_rows(out_weight):
    size = lax.axis_size("seq")
    fetched = []
    for slot in range(2):
        pairs = []
        for x, by_core in enumerate(DISTANCES):
            for core, distances in enumerate(by_core):
                first = (2 * x + core) * size
                if distances[slot]:
                    pairs += [(first + (i + distances[slot]) % size, first + i) for i in range(size)]
        fetched.append(lax.ppermute(out_weight, ("x", "core", "seq"), pairs))
    keeps_own = (lax.axis_index("x") == 0) & (lax.axis_index("core") == 0)
    return jnp.stack([jnp.where(keeps_own, out_weight, fetched[0]), fetched[1]])


def weight_kernel(place_ref, *refs):
    *block_refs, out_ref = refs
    number = 0
    for block_ref in block_refs:
        for row in range(block_ref.shape[0]):
            for slot in range(2):
                out_ref[place_ref[number]] = block_ref[row, slot]
                number += 1


def whole_weight(fetched):
    rows, channels = fetched.shape[1:]
    seq = lax.axis_size("seq")
    along_y = jnp.stack([fetched] + [shift(fetched, "fsdp", -by) for by in range(1, 4)])
    after, across, before = ring_of_four(along_y, "x")
    arrays, places = [], []
    distances = jnp.array(DISTANCES, jnp.int32)
    at_x, at_core, at_y, at_seq = (lax.axis_index(axis) for axis in ("x", "core", "fsdp", "seq"))
    for array, by_x, first in (
        (along_y, 0, 0), (after, 1, 0), (across[0], 2, 0), (across[1], 2, 2), (before, 3, 0),
    ):
        for other in range(2):
            arrays.append(shift(array, "core", 1) if other else array)
            core = (at_core + other) % 2
            from_seq = (at_seq + distances[(at_x + by_x) % 4, core]) % seq
            from_y = (at_y + first + jnp.arange(array.shape[0])) % 4
            places.append((from_y[:, None] * seq + from_seq[None, :]).reshape(-1))
    size = 2 * channels * channels
    whole = pl.pallas_call(
        weight_kernel,
        out_shape=jax.ShapeDtypeStruct((4 * seq, rows, channels), jnp.bfloat16),
        in_specs=[pl.BlockSpec(memory_space=pltpu.SMEM)] + in_vmem(len(arrays)),
        out_specs=in_vmem(1)[0],
        cost_estimate=pl.CostEstimate(flops=0, bytes_accessed=size, transcendentals=0),
        compiler_params=pltpu.CompilerParams(vmem_limit_bytes=VMEM_BYTES),
        name="weight_in_place",
    )(jnp.concatenate(places).astype(jnp.int32), *arrays)
    return whole.reshape(channels, channels)


def all_sum(array, axis):
    return jnp.sum(lax.all_gather(array, axis, axis=0, tiled=True), axis=0, keepdims=True)


def frame_pair(array):
    size, chips = lax.axis_size("seq"), lax.axis_size("x")
    fetched = []
    for step in range(2):
        pairs = []
        for group in range(2 * chips):
            by = 2 * group + step
            if by:
                pairs += [(group * size + i, group * size + (i ^ by)) for i in range(size)]
        fetched.append(lax.ppermute(array, ("x", "core", "seq"), pairs))
    own = jnp.where((lax.axis_index("x") == 0) & (lax.axis_index("core") == 0), array, 0.0)
    return (fetched[0] + own) + fetched[1]


def group_sum(total):
    total = total + shift(total, "core", 1)
    for by in (1, 2):
        total = total + lax.ppermute(total, "x", [(i, i ^ by) for i in range(lax.axis_size("x"))])
    return total


def on_device(
    query_states,
    key_states,
    value_states,
    out_weight,
    gate_space,
    gate_time,
    upstream,
    frame_count,
    pos_count,
):
    _, frames_here, positions, channels = query_states.shape
    owners = lax.axis_size("seq")
    near = positions // owners
    gate_space, gate_time = gate_space.reshape(1, channels), gate_time.reshape(1, channels)
    query, key, value, flat_up = (
        array.reshape(positions, channels)
        for array in (query_states, key_states, value_states, upstream)
    )

    def exchange(array):
        return lax.all_to_all(array, "seq", split_axis=0, concat_axis=0, tiled=True)

    fetched = fetch_rows(out_weight)
    sent = jnp.stack(
        [array.reshape(owners, near, channels) for array in (query, key, value, flat_up)], axis=1
    )
    fetched, sent = lax.optimization_barrier((fetched, sent))
    moved = exchange(sent)

    weight = whole_weight(fetched)

    def project(array):
        return jnp.einsum("td,nd->tn", array, weight, preferred_element_type=jnp.float32)

    space, grad_query, grad_key, grad_value, part_space = space_attention(
        pos_count, query, key, value, project(flat_up), gate_space
    )
    moved, part_space = lax.optimization_barrier((moved, part_space))
    there = project(moved[:, 3].reshape(positions, channels))
    early, late, part_time = time_attention(frame_count, moved, there, gate_time)
    early = exchange(early)

    parts = jnp.concatenate([part_space, part_time], axis=1)
    parts = frame_pair(all_sum(all_sum(parts, ("x", "core")), "fsdp"))
    early, late, parts = lax.optimization_barrier((early, late, parts))
    late = exchange(late)
    tokens = lax.axis_size("x") * lax.axis_size("core") * lax.axis_size("fsdp") * owners * frames_here * positions
    totals = group_sum(parts)[0] / math.sqrt(tokens)

    results = output(early, space, grad_query, gate_space, gate_time, weight)
    results += add_returned(late, grad_key, grad_value)
    shaped = tuple(array.reshape(query_states.shape) for array in results)
    return shaped + (totals[:channels], totals[channels:])


def solution(mesh):
    chips = mesh.shape["dp"] // 2
    split = Mesh(
        mesh.devices.reshape(chips, 2, mesh.shape["fsdp"], mesh.shape["seq"]),
        ("x", "core", "fsdp", "seq"),
    )
    clips = ("x", "core", "fsdp")
    states = P(clips, "seq", None, None)
    return jax.shard_map(
        on_device,
        mesh=split,
        in_specs=(states, states, states, P(("fsdp", "seq"), None), P(), P(), states, P(clips), P(clips)),
        out_specs=(states, states, states, states, P(), P()),
        check_vma=False,
    )
```

time: 288 us -> 212 us (0.74)
  blocking collectives: 88.4 us -> 25.2 us
  starting transfers between devices: 59 us -> 94.3 us
  waiting for transfers between devices: 84.9 us -> 57.8 us
  local copies, waits for them, and re-layouts: 31.8 us -> 9.08 us
  other arithmetic: 9.52 us -> 4.6 us
  matrix products: 1.41 us -> 5.58 us
    all_gather x3 -> x2, blocking collectives: 88.4 us -> 25.2 us  [all_sum(): lax.all_gather(array, axis, axis=0, tiled=True)]
    ppermute x9 -> x19, starting transfers between devices: 28.1 us -> 68.1 us  [the longest x13 34.9 us: shift(): lax.ppermute(array, axis, [(i, (i + by) % size) for i in range(size)])]
    all_to_all x3, waiting for transfers between devices: 59.9 us -> 27.3 us  [exchange(): return lax.all_to_all(array, 'seq', split_axis=0, concat_axis=0, tiled=True)]
    reshape x2 -> x0, local copies, waits for them, and re-layouts: 11 us -> none  [the longest x1 11 us: whole_weight(): side = side.reshape(4, 4 * seq, ROWS, rows // ROWS, wide)]
    unnamed x54 -> x32, local copies, waits for them, and re-layouts: 14.2 us -> 6.05 us
    ppermute x9 -> x19, waiting for transfers between devices: 25 us -> 30.6 us  [the longest x13 16.9 us: shift(): lax.ppermute(array, axis, [(i, (i + by) % size) for i in range(size)])]
    all_to_all x3, starting transfers between devices: 30.9 us -> 26.2 us  [exchange(): return lax.all_to_all(array, 'seq', split_axis=0, concat_axis=0, tiled=True)]
    concatenate x2 -> x0, other arithmetic: 4.53 us -> none  [the longest x1 2.7 us: whole_weight(): side = jnp.concatenate([low, high[..., HEAD:]], axis=-1)]
  transfers between devices with their start and end apart: 12 -> 22, of which waited for: 8 -> 14; matrix products, arithmetic and copies ran while one was open for 9% -> 4% of each run, Pallas kernels for 0% -> 3%
where the time goes in v2:
time: 212 us; the launch traced here: 210 us
  starting transfers between devices  94.3 us (44%)
  waiting for transfers between devices  57.8 us (27%)
  blocking collectives  25.2 us (12%)
  Pallas kernels  11 us (5%)
  local copies, waits for them, and re-layouts  9.08 us (4%)
  matrix products  5.58 us (3%)
  other arithmetic  4.6 us (2%)
  between operations  2.47 us (1%)
    ppermute x13, starting transfers between devices, shift(): lax.ppermute(array, axis, [(i, (i + by) % size) for i in range(size)])  34.9 us
    all_to_all x3, waiting for transfers between devices, exchange(): return lax.all_to_all(array, 'seq', split_axis=0, concat_axis=0, tiled=True)  27.3 us
    all_to_all x3, starting transfers between devices, exchange(): return lax.all_to_all(array, 'seq', split_axis=0, concat_axis=0, tiled=True)  26.2 us
    all_gather x2, blocking collectives, all_sum(): lax.all_gather(array, axis, axis=0, tiled=True)  25.2 us
    ppermute x13, waiting for transfers between devices, shift(): lax.ppermute(array, axis, [(i, (i + by) % size) for i in range(size)])  16.9 us
    ppermute x2, starting transfers between devices, fetch_rows(): fetched.append(lax.ppermute(out_weight, ('x', 'core', 'seq'), pairs))  14.2 us
    ppermute x2, starting transfers between devices, frame_pair(): fetched.append(lax.ppermute(array, ('x', 'core', 'seq'), pairs))  11.1 us
    ppermute x2, starting transfers between devices, group_sum(): lax.ppermute(total, 'x', [(i, i ^ by) for i in range(lax.axis_size('x'))])  7.85 us
  transfers between devices with their start and end apart: 22, of which 14 were waited for; matrix products, arithmetic and copies ran while one was open for 4% of the time, Pallas kernels for 3%

profile of v2, /device:TPU:6, one launch (start us, length us, event | category | flops | bytes accessed | tf_op | source)
XLA Modules:
  0.0 210.0 jit_solution(1621308379851805296)
XLA Ops:
  0.6 12.3 %collective-permute-start = (bf16[24,1536]{1,0:T(8,128)(2,1)}, bf16[24,1536]{1,0:T(8,128)(2,1)S(1)}, u32[]{:S(2)}, u32[]{:S(2)}) collective-permute-start(bf16[24,1536]{1,0:T(8,128)(2,1)} %param.13), channel_id=1, source_target_pairs={{68,64},{69,65},{70,66},{71,67},{72,68},{73,69},{74,70},{75,71},{7... | collective-permute-start | bytes 221192 | tf_op jit(solution)/shard_map/ppermute | solution.py:215
  12.9 1.9 collective-permute-start.1
  14.9 2.8 %pad_maximum_fusion = bf16[16,4,8,1536]{3,2,1,0:T(8,128)(2,1)} fusion(bf16[16,1,8,1536]{3,2,1,0:T(8,128)(2,1)} %bitcast.89, bf16[16,1,8,1536]{3,2,1,0:T(8,128)(2,1)} %bitcast.83, bf16[16,1,8,1536]{3,2,1,0:T(8,128)(2,1)} %bitcast.85, bf16[16,1,8,1536]{3,2,1,0:T(8,128)(2,1)} %bitcast.87), kind=kLoop, calls=%fused_computation.1 | loop fusion | flops 2359296 | bytes 3145728 | tf_op jit(solution)/shard_map/stack | solution.py:309
  17.7 2.5 %collective-permute-done = bf16[24,1536]{1,0:T(8,128)(2,1)S(1)} collective-permute-done((bf16[24,1536]{1,0:T(8,128)(2,1)}, bf16[24,1536]{1,0:T(8,128)(2,1)S(1)}, u32[]{:S(2)}, u32[]{:S(2)}) %collective-permute-start) | collective-permute-done | bytes 73760 | tf_op jit(solution)/shard_map/ppermute | solution.py:215
  20.2 4.3 %collective-permute-done.1 = bf16[24,1536]{1,0:T(8,128)(2,1)S(1)} collective-permute-done((bf16[24,1536]{1,0:T(8,128)(2,1)}, bf16[24,1536]{1,0:T(8,128)(2,1)S(1)}, u32[]{:S(2)}, u32[]{:S(2)}) %collective-permute-start.1) | collective-permute-done | bytes 73760 | tf_op jit(solution)/shard_map/ppermute | solution.py:215
  24.5 7.5 %all-to-all-start = ((bf16[16,4,8,1536]{3,2,1,0:T(8,128)(2,1)}), bf16[16,4,8,1536]{3,2,1,0:T(8,128)(2,1)S(1)}, u32[]{:S(2)}, u32[]{:S(2)}) async-start(bf16[16,4,8,1536]{3,2,1,0:T(8,128)(2,1)} %pad_maximum_fusion), calls=%async_computation | async-start | bytes 3145728 | tf_op jit(solution)/shard_map/all_to_all | solution.py:306
  32.0 3.5 %collective-permute-start.4 = (bf16[2,24,1536]{2,1,0:T(8,128)(2,1)S(1)}, bf16[2,24,1536]{2,1,0:T(8,128)(2,1)S(1)}, u32[]{:S(2)}, u32[]{:S(2)}) collective-permute-start(bf16[2,24,1536]{2,1,0:T(8,128)(2,1)S(1)} %pad_maximum_fusion.2), channel_id=1, source_target_pairs={{0,16},{16,32},{32,48},{48,0},{1,17},{17,33},{33,49},{49,1},{2,18}... | collective-permute-start | bytes 442376 | tf_op jit(solution)/shard_map/ppermute | solution.py:195
  35.5 4.8 %collective-permute-start.3 = (bf16[2,24,1536]{2,1,0:T(8,128)(2,1)S(1)}, bf16[2,24,1536]{2,1,0:T(8,128)(2,1)S(1)}, u32[]{:S(2)}, u32[]{:S(2)}) collective-permute-start(bf16[2,24,1536]{2,1,0:T(8,128)(2,1)S(1)} %pad_maximum_fusion.2), channel_id=1, source_target_pairs={{0,32},{16,48},{32,0},{48,16},{1,33},{17,49},{33,1},{49,17},{2,34}... | collective-permute-start | bytes 442376 | tf_op jit(solution)/shard_map/ppermute | solution.py:195
  40.3 3.3 %collective-permute-start.2 = (bf16[2,24,1536]{2,1,0:T(8,128)(2,1)S(1)}, bf16[2,24,1536]{2,1,0:T(8,128)(2,1)S(1)}, u32[]{:S(2)}, u32[]{:S(2)}) collective-permute-start(bf16[2,24,1536]{2,1,0:T(8,128)(2,1)S(1)} %pad_maximum_fusion.2), channel_id=1, source_target_pairs={{0,48},{16,0},{32,16},{48,32},{1,49},{17,1},{33,17},{49,33},{2,50}... | collective-permute-start | bytes 442376 | tf_op jit(solution)/shard_map/ppermute | solution.py:195
  43.6 2.4 %collective-permute-done.3 = bf16[2,24,1536]{2,1,0:T(8,128)(2,1)S(1)} collective-permute-done((bf16[2,24,1536]{2,1,0:T(8,128)(2,1)S(1)}, bf16[2,24,1536]{2,1,0:T(8,128)(2,1)S(1)}, u32[]{:S(2)}, u32[]{:S(2)}) %collective-permute-start.3) | collective-permute-done | bytes 147488 | tf_op jit(solution)/shard_map/ppermute | solution.py:195
  46.0 2.1 %collective-permute-done.2 = bf16[2,24,1536]{2,1,0:T(8,128)(2,1)S(1)} collective-permute-done((bf16[2,24,1536]{2,1,0:T(8,128)(2,1)S(1)}, bf16[2,24,1536]{2,1,0:T(8,128)(2,1)S(1)}, u32[]{:S(2)}, u32[]{:S(2)}) %collective-permute-start.2) | collective-permute-done | bytes 147488 | tf_op jit(solution)/shard_map/ppermute | solution.py:195
  48.3 3.5 %collective-permute-start.8 = (bf16[4,2,24,1536]{3,2,1,0:T(8,128)(2,1)S(1)}, bf16[4,2,24,1536]{3,2,1,0:T(8,128)(2,1)S(1)}, u32[]{:S(2)}, u32[]{:S(2)}) collective-permute-start(bf16[4,2,24,1536]{3,2,1,0:T(8,128)(2,1)S(1)} %pad_maximum_fusion.1.refs_0_), channel_id=1, source_target_pairs={{0,128},{128,256},{256,384},{384,0},{1,129},{129,257},{257,385},{3... | collective-permute-start | bytes 1769480 | tf_op jit(solution)/shard_map/ppermute | solution.py:195
  51.7 2.4 %collective-permute-start.6 = (bf16[4,2,24,1536]{3,2,1,0:T(8,128)(2,1)S(1)}, bf16[4,2,24,1536]{3,2,1,0:T(8,128)(2,1)S(1)}, u32[]{:S(2)}, u32[]{:S(2)}) collective-permute-start(bf16[4,2,24,1536]{3,2,1,0:T(8,128)(2,1)S(1)} %pad_maximum_fusion.1.refs_0_), channel_id=1, source_target_pairs={{0,384},{128,0},{256,128},{384,256},{1,385},{129,1},{257,129},{385... | collective-permute-start | bytes 1769480 | tf_op jit(solution)/shard_map/ppermute | solution.py:195
  54.3 1.9 collective-permute-start.5
  56.2 8.6 %collective-permute-done.8.refs_8_ = bf16[4,2,24,1536]{3,2,1,0:T(8,128)(2,1)S(1)} collective-permute-done((bf16[4,2,24,1536]{3,2,1,0:T(8,128)(2,1)S(1)}, bf16[4,2,24,1536]{3,2,1,0:T(8,128)(2,1)S(1)}, u32[]{:S(2)}, u32[]{:S(2)}) %collective-permute-start.8) | collective-permute-done | bytes 589856 | tf_op jit(solution)/shard_map/ppermute | solution.py:195
  64.7 0.7 slice.28
  65.5 3.4 %collective-permute-start.9 = (bf16[2,2,24,1536]{3,2,1,0:T(8,128)(2,1)}, bf16[2,2,24,1536]{3,2,1,0:T(8,128)(2,1)}, u32[]{:S(2)}, u32[]{:S(2)}) collective-permute-start(bf16[2,2,24,1536]{3,2,1,0:T(8,128)(2,1)} %slice.28), channel_id=1, source_target_pairs={{0,128},{128,256},{256,384},{384,0},{1,129},{129,257},{257,385},{3... | collective-permute-start | bytes 884744 | tf_op jit(solution)/shard_map/ppermute | solution.py:195
  69.9 2.1 %collective-permute-start.11 = (bf16[2,2,24,1536]{3,2,1,0:T(8,128)(2,1)}, bf16[2,2,24,1536]{3,2,1,0:T(8,128)(2,1)}, u32[]{:S(2)}, u32[]{:S(2)}) collective-permute-start(bf16[2,2,24,1536]{3,2,1,0:T(8,128)(2,1)} %slice.29), channel_id=1, source_target_pairs={{0,384},{128,0},{256,128},{384,256},{1,385},{129,1},{257,129},{385... | collective-permute-start | bytes 884744 | tf_op jit(solution)/shard_map/ppermute | solution.py:195
  72.1 1.9 collective-permute-start.13
  74.0 2.4 %collective-permute-start.7 = (bf16[4,2,24,1536]{3,2,1,0:T(8,128)(2,1)S(1)}, bf16[4,2,24,1536]{3,2,1,0:T(8,128)(2,1)}, u32[]{:S(2)}, u32[]{:S(2)}) collective-permute-start(bf16[4,2,24,1536]{3,2,1,0:T(8,128)(2,1)S(1)} %collective-permute-done.6.refs_2_), channel_id=1, source_target_pairs={{0,64},{64,0},{1,65},{65,1},{2,66},{66,2},{3,67},{67,3},{4,68},{68... | collective-permute-start | bytes 1769480 | tf_op jit(solution)/shard_map/ppermute | solution.py:195
  78.2 1.9 collective-permute-start.10
  80.1 0.9 collective-permute-done.11.refs_6_
  81.0 1.9 collective-permute-start.12
  83.6 1.2 collective-permute-done.12.refs_7_
  84.8 2.1 weight_in_place.1
  87.0 1.6 convolution_bitcast_fusion.mixed_ref
  89.1 1.3 space_attention.1
  90.4 0.9 copy-done.5
  91.8 11.3 %all-to-all-done.moved_ref = bf16[16,4,8,1536]{3,2,1,0:T(8,128)(2,1)S(1)} async-done(((bf16[16,4,8,1536]{3,2,1,0:T(8,128)(2,1)}), bf16[16,4,8,1536]{3,2,1,0:T(8,128)(2,1)S(1)}, u32[]{:S(2)}, u32[]{:S(2)}) %all-to-all-start) | async-done | bytes 1572896 | tf_op jit(solution)/shard_map/all_to_all | solution.py:306
  103.1 4.0 %fusion.mixed_ref = f32[128,1536]{1,0:T(8,128)S(1)} fusion(bf16[1536,1536]{1,0:T(8,128)(2,1)} %bitcast.81, bf16[16,4,8,1536]{3,2,1,0:T(8,128)(2,1)S(1)} %all-to-all-done.moved_ref), kind=kOutput, calls=%fused_computation.3 | convolution fusion | flops 603979776 | bytes 5898240 | tf_op jit(solution)/shard_map/td,nd->tn/dot_general | solution.py:318
  107.1 2.5 %time_attention.1 = (bf16[16,2,8,1536]{3,2,1,0:T(8,128)(2,1)}, bf16[16,2,8,1536]{3,2,1,0:T(8,128)(2,1)}, f32[1,1536]{1,0:T(1,128)S(1)}) custom-call(s32[1]{0:T(128)S(6)} %copy.21.count_ref, bf16[16,4,8,1536]{3,2,1,0:T(8,128)(2,1)S(1)} %all-to-all-done.moved_ref, f32[128,1536]{1,0:T(8,128)S(1)} %fusion.mixed_ref, f32[1,1536]{1,0:T(1,128)S(1)} %reshape.298.gate_ref.gate_time_ref), custom_call_target="tpu_custom_call" | custom-call | flops 301989888 | bytes 3145728 | tf_op jit(solution)/shard_map/time_attention/pallas_call | solution.py:102
  110.2 10.6 %all-to-all-start.1 = ((bf16[16,2,8,1536]{3,2,1,0:T(8,128)(2,1)}), bf16[16,2,8,1536]{3,2,1,0:T(8,128)(2,1)S(1)}, u32[]{:S(2)}, u32[]{:S(2)}) async-start(bf16[16,2,8,1536]{3,2,1,0:T(8,128)(2,1)} %get-tuple-element.29), calls=%async_computation.1 | async-start | bytes 1572864 | tf_op jit(solution)/shard_map/all_to_all | solution.py:306
  120.9 12.7 %all-gather.1 = f32[8,1,3072]{2,1,0:T(1,128)S(1)} all-gather(f32[1,1,3072]{2,1,0:T(1,128)S(1)} %maximum_bitcast_fusion), channel_id=1, replica_groups=mesh['x'=4,'core'=2,'fsdp'=4,'seq'=16] {'x','core'}, dimensions={0}, use_global_device_ids=true | all-gather | bytes 110592 | tf_op jit(solution)/shard_map/all_gather | solution.py:261
  133.7 12.4 %all-gather = f32[12288]{0:T(1024)S(1)} all-gather(f32[3072]{0:T(1024)S(1)} %reduce_sum.18), channel_id=2, replica_groups=mesh['x'=4,'core'=2,'fsdp'=4,'seq'=16] {'fsdp'}, dimensions={0}, use_global_device_ids=true | all-gather | bytes 61440 | tf_op jit(solution)/shard_map/all_gather | solution.py:261
  146.2 6.8 %collective-permute-start.15 = (f32[1,3072]{1,0:T(1,128)S(1)}, f32[1,3072]{1,0:T(1,128)S(1)}, u32[]{:S(2)}, u32[]{:S(2)}) collective-permute-start(f32[1,3072]{1,0:T(1,128)S(1)} %bitcast.95), channel_id=1, source_target_pairs={{0,1},{1,0},{2,3},{3,2},{4,5},{5,4},{6,7},{7,6},{8,9},{9,8},{10,11... | collective-permute-start | bytes 36872 | tf_op jit(solution)/shard_map/ppermute | solution.py:273
  153.0 4.3 %collective-permute-start.14 = (f32[1,3072]{1,0:T(1,128)S(1)}, f32[1,3072]{1,0:T(1,128)S(1)}, u32[]{:S(2)}, u32[]{:S(2)}) collective-permute-start(f32[1,3072]{1,0:T(1,128)S(1)} %bitcast.96), channel_id=1, source_target_pairs={{64,66},{65,67},{66,64},{67,65},{68,70},{69,71},{70,68},{71,69},{7... | collective-permute-start | bytes 36872 | tf_op jit(solution)/shard_map/ppermute | solution.py:273
  158.0 4.6 %collective-permute-done.14 = f32[1,3072]{1,0:T(1,128)S(1)} collective-permute-done((f32[1,3072]{1,0:T(1,128)S(1)}, f32[1,3072]{1,0:T(1,128)S(1)}, u32[]{:S(2)}, u32[]{:S(2)}) %collective-permute-start.14) | collective-permute-done | bytes 12320 | tf_op jit(solution)/shard_map/ppermute | solution.py:273
  163.2 8.0 %all-to-all-start.2 = ((bf16[16,2,8,1536]{3,2,1,0:T(8,128)(2,1)}), bf16[16,2,8,1536]{3,2,1,0:T(8,128)(2,1)S(1)}, u32[]{:S(2)}, u32[]{:S(2)}) async-start(bf16[16,2,8,1536]{3,2,1,0:T(8,128)(2,1)} %get-tuple-element.38), calls=%async_computation.2 | async-start | bytes 1572864 | tf_op jit(solution)/shard_map/all_to_all | solution.py:306
  171.2 1.9 collective-permute-start.16
  173.1 1.4 collective-permute-done.16
  175.2 5.9 %collective-permute-start.17 = (f32[1,3072]{1,0:T(1,128)S(1)}, f32[1,3072]{1,0:T(1,128)S(1)}, u32[]{:S(2)}, u32[]{:S(2)}) collective-permute-start(f32[1,3072]{1,0:T(1,128)S(1)} %add.589), channel_id=1, source_target_pairs={{0,128},{128,0},{256,384},{384,256},{1,129},{129,1},{257,385},{385... | collective-permute-start | bytes 36872 | tf_op jit(solution)/shard_map/ppermute | solution.py:281
  181.2 1.7 collective-permute-done.17
  182.8 1.9 collective-permute-start.18
  184.8 2.3 %copy-done.1 = bf16[64,24,1536]{2,1,0:T(8,128)(2,1)S(1)} copy-done((bf16[64,24,1536]{2,1,0:T(8,128)(2,1)S(1)}, bf16[64,24,1536]{2,1,0:T(8,128)(2,1)}, u32[]{:S(2)}) %copy-start.1) | copy-done | bytes 4718616
  187.1 1.1 copy-done.6
  188.2 3.5 %output.1 = (bf16[128,1536]{1,0:T(8,128)(2,1)}, bf16[128,1536]{1,0:T(8,128)(2,1)}) custom-call(bf16[16,2,8,1536]{3,2,1,0:T(8,128)(2,1)S(1)} %all-to-all-done.1.time_ref.moved_ref, bf16[16,2,8,1536]{3,2,1,0:T(8,128)(2,1)S(1)} %all-to-all-done.1.time_ref.moved_ref, bf16[128,1536]{1,0:T(8,128)(2,1)S(1)} %get-tuple-element.34.space_ref, ...), custom_call_target="tpu_custom_call" | custom-call | tf_op jit(solution)/shard_map/output/pallas_call | solution.py:156
  192.4 16.0 %all-to-all-done.2.moved_ref = bf16[16,2,8,1536]{3,2,1,0:T(8,128)(2,1)S(1)} async-done(((bf16[16,2,8,1536]{3,2,1,0:T(8,128)(2,1)}), bf16[16,2,8,1536]{3,2,1,0:T(8,128)(2,1)S(1)}, u32[]{:S(2)}, u32[]{:S(2)}) %all-to-all-start.2) | async-done | bytes 786464 | tf_op jit(solution)/shard_map/all_to_all | solution.py:306
  208.4 1.6 add_returned.1
  (70 shorter events, 6.8 us)
Async XLA Ops:
  0.6 19.5 %collective-permute-start = (bf16[24,1536]{1,0:T(8,128)(2,1)}, bf16[24,1536]{1,0:T(8,128)(2,1)S(1)}, u32[]{:S(2)}, u32[]{:S(2)}) collective-permute-start(bf16[24,1536]{1,0:T(8,128)(2,1)} %param.13), channel_id=1, source_target_pairs={{68,64},{69,65},{70,66},{71,67},{72,68},{73,69},{74,70},{75,71},{7... | collective-permute-start | bytes 221192 | tf_op jit(solution)/shard_map/ppermute | solution.py:215
  12.9 11.5 %collective-permute-start.1 = (bf16[24,1536]{1,0:T(8,128)(2,1)}, bf16[24,1536]{1,0:T(8,128)(2,1)S(1)}, u32[]{:S(2)}, u32[]{:S(2)}) collective-permute-start(bf16[24,1536]{1,0:T(8,128)(2,1)} %param.13), channel_id=1, source_target_pairs={{8,0},{9,1},{10,2},{11,3},{12,4},{13,5},{14,6},{15,7},{0,8},{1,9},... | collective-permute-start | bytes 221192 | tf_op jit(solution)/shard_map/ppermute | solution.py:215
  14.9 5.3 %copy-start.12 = (bf16[24,1536]{1,0:T(8,128)(2,1)S(1)}, bf16[24,1536]{1,0:T(8,128)(2,1)}, u32[]{:S(2)}) copy-start(bf16[24,1536]{1,0:T(8,128)(2,1)} %param.13) | copy-start | bytes 221188
  24.5 29.7 %copy-start.15 = (s32[4,2,2]{2,1,0:T(2,128)S(1)}, s32[4,2,2]{2,1,0:T(2,128)}, u32[]{:S(2)}) copy-start(s32[4,2,2]{2,1,0:T(2,128)} %constant.192.clone) | copy-start | bytes 196
  24.5 78.6 %all-to-all-start = ((bf16[16,4,8,1536]{3,2,1,0:T(8,128)(2,1)}), bf16[16,4,8,1536]{3,2,1,0:T(8,128)(2,1)S(1)}, u32[]{:S(2)}, u32[]{:S(2)}) async-start(bf16[16,4,8,1536]{3,2,1,0:T(8,128)(2,1)} %pad_maximum_fusion), calls=%async_computation | async-start | bytes 3145728 | tf_op jit(solution)/shard_map/all_to_all | solution.py:306
  32.0 46.1 %copy-start.13 = (f32[1536]{0:T(1024)S(1)}, f32[1536]{0:T(1024)}, u32[]{:S(2)}) copy-start(f32[1536]{0:T(1024)} %param.14) | copy-start | bytes 18436
  32.0 46.1 %copy-start.14 = (f32[1536]{0:T(1024)S(1)}, f32[1536]{0:T(1024)}, u32[]{:S(2)}) copy-start(f32[1536]{0:T(1024)} %param.15) | copy-start | bytes 18436
  32.0 11.6 %collective-permute-start.4 = (bf16[2,24,1536]{2,1,0:T(8,128)(2,1)S(1)}, bf16[2,24,1536]{2,1,0:T(8,128)(2,1)S(1)}, u32[]{:S(2)}, u32[]{:S(2)}) collective-permute-start(bf16[2,24,1536]{2,1,0:T(8,128)(2,1)S(1)} %pad_maximum_fusion.2), channel_id=1, source_target_pairs={{0,16},{16,32},{32,48},{48,0},{1,17},{17,33},{33,49},{49,1},{2,18}... | collective-permute-start | bytes 442376 | tf_op jit(solution)/shard_map/ppermute | solution.py:195
  35.5 10.5 %collective-permute-start.3 = (bf16[2,24,1536]{2,1,0:T(8,128)(2,1)S(1)}, bf16[2,24,1536]{2,1,0:T(8,128)(2,1)S(1)}, u32[]{:S(2)}, u32[]{:S(2)}) collective-permute-start(bf16[2,24,1536]{2,1,0:T(8,128)(2,1)S(1)} %pad_maximum_fusion.2), channel_id=1, source_target_pairs={{0,32},{16,48},{32,0},{48,16},{1,33},{17,49},{33,1},{49,17},{2,34}... | collective-permute-start | bytes 442376 | tf_op jit(solution)/shard_map/ppermute | solution.py:195
  40.3 7.8 %collective-permute-start.2 = (bf16[2,24,1536]{2,1,0:T(8,128)(2,1)S(1)}, bf16[2,24,1536]{2,1,0:T(8,128)(2,1)S(1)}, u32[]{:S(2)}, u32[]{:S(2)}) collective-permute-start(bf16[2,24,1536]{2,1,0:T(8,128)(2,1)S(1)} %pad_maximum_fusion.2), channel_id=1, source_target_pairs={{0,48},{16,0},{32,16},{48,32},{1,49},{17,1},{33,17},{49,33},{2,50}... | collective-permute-start | bytes 442376 | tf_op jit(solution)/shard_map/ppermute | solution.py:195
  48.3 16.5 %collective-permute-start.8 = (bf16[4,2,24,1536]{3,2,1,0:T(8,128)(2,1)S(1)}, bf16[4,2,24,1536]{3,2,1,0:T(8,128)(2,1)S(1)}, u32[]{:S(2)}, u32[]{:S(2)}) collective-permute-start(bf16[4,2,24,1536]{3,2,1,0:T(8,128)(2,1)S(1)} %pad_maximum_fusion.1.refs_0_), channel_id=1, source_target_pairs={{0,128},{128,256},{256,384},{384,0},{1,129},{129,257},{257,385},{3... | collective-permute-start | bytes 1769480 | tf_op jit(solution)/shard_map/ppermute | solution.py:195
  51.7 17.5 %collective-permute-start.6 = (bf16[4,2,24,1536]{3,2,1,0:T(8,128)(2,1)S(1)}, bf16[4,2,24,1536]{3,2,1,0:T(8,128)(2,1)S(1)}, u32[]{:S(2)}, u32[]{:S(2)}) collective-permute-start(bf16[4,2,24,1536]{3,2,1,0:T(8,128)(2,1)S(1)} %pad_maximum_fusion.1.refs_0_), channel_id=1, source_target_pairs={{0,384},{128,0},{256,128},{384,256},{1,385},{129,1},{257,129},{385... | collective-permute-start | bytes 1769480 | tf_op jit(solution)/shard_map/ppermute | solution.py:195
  54.3 29.4 %collective-permute-start.5 = (bf16[4,2,24,1536]{3,2,1,0:T(8,128)(2,1)S(1)}, bf16[4,2,24,1536]{3,2,1,0:T(8,128)(2,1)}, u32[]{:S(2)}, u32[]{:S(2)}) collective-permute-start(bf16[4,2,24,1536]{3,2,1,0:T(8,128)(2,1)S(1)} %pad_maximum_fusion.1.refs_0_), channel_id=1, source_target_pairs={{0,64},{64,0},{1,65},{65,1},{2,66},{66,2},{3,67},{67,3},{4,68},{68... | collective-permute-start | bytes 1769480 | tf_op jit(solution)/shard_map/ppermute | solution.py:195
  65.5 12.7 %collective-permute-start.9 = (bf16[2,2,24,1536]{3,2,1,0:T(8,128)(2,1)}, bf16[2,2,24,1536]{3,2,1,0:T(8,128)(2,1)}, u32[]{:S(2)}, u32[]{:S(2)}) collective-permute-start(bf16[2,2,24,1536]{3,2,1,0:T(8,128)(2,1)} %slice.28), channel_id=1, source_target_pairs={{0,128},{128,256},{256,384},{384,0},{1,129},{129,257},{257,385},{3... | collective-permute-start | bytes 884744 | tf_op jit(solution)/shard_map/ppermute | solution.py:195
  69.9 11.1 %collective-permute-start.11 = (bf16[2,2,24,1536]{3,2,1,0:T(8,128)(2,1)}, bf16[2,2,24,1536]{3,2,1,0:T(8,128)(2,1)}, u32[]{:S(2)}, u32[]{:S(2)}) collective-permute-start(bf16[2,2,24,1536]{3,2,1,0:T(8,128)(2,1)} %slice.29), channel_id=1, source_target_pairs={{0,384},{128,0},{256,128},{384,256},{1,385},{129,1},{257,129},{385... | collective-permute-start | bytes 884744 | tf_op jit(solution)/shard_map/ppermute | solution.py:195
  72.1 11.6 %collective-permute-start.13 = (bf16[4,2,24,1536]{3,2,1,0:T(8,128)(2,1)S(1)}, bf16[4,2,24,1536]{3,2,1,0:T(8,128)(2,1)}, u32[]{:S(2)}, u32[]{:S(2)}) collective-permute-start(bf16[4,2,24,1536]{3,2,1,0:T(8,128)(2,1)S(1)} %collective-permute-done.8.refs_8_), channel_id=1, source_target_pairs={{0,64},{64,0},{1,65},{65,1},{2,66},{66,2},{3,67},{67,3},{4,68},{68... | collective-permute-start | bytes 1769480 | tf_op jit(solution)/shard_map/ppermute | solution.py:195
  74.0 10.8 %collective-permute-start.7 = (bf16[4,2,24,1536]{3,2,1,0:T(8,128)(2,1)S(1)}, bf16[4,2,24,1536]{3,2,1,0:T(8,128)(2,1)}, u32[]{:S(2)}, u32[]{:S(2)}) collective-permute-start(bf16[4,2,24,1536]{3,2,1,0:T(8,128)(2,1)S(1)} %collective-permute-done.6.refs_2_), channel_id=1, source_target_pairs={{0,64},{64,0},{1,65},{65,1},{2,66},{66,2},{3,67},{67,3},{4,68},{68... | collective-permute-start | bytes 1769480 | tf_op jit(solution)/shard_map/ppermute | solution.py:195
  78.2 5.4 %collective-permute-start.10 = (bf16[2,2,24,1536]{3,2,1,0:T(8,128)(2,1)}, bf16[2,2,24,1536]{3,2,1,0:T(8,128)(2,1)}, u32[]{:S(2)}, u32[]{:S(2)}) collective-permute-start(bf16[2,2,24,1536]{3,2,1,0:T(8,128)(2,1)} %collective-permute-done.9.refs_4_), channel_id=1, source_target_pairs={{0,64},{64,0},{1,65},{65,1},{2,66},{66,2},{3,67},{67,3},{4,68},{68... | collective-permute-start | bytes 884744 | tf_op jit(solution)/shard_map/ppermute | solution.py:195
  81.0 3.8 %collective-permute-start.12 = (bf16[2,2,24,1536]{3,2,1,0:T(8,128)(2,1)}, bf16[2,2,24,1536]{3,2,1,0:T(8,128)(2,1)}, u32[]{:S(2)}, u32[]{:S(2)}) collective-permute-start(bf16[2,2,24,1536]{3,2,1,0:T(8,128)(2,1)} %collective-permute-done.11.refs_6_), channel_id=1, source_target_pairs={{0,64},{64,0},{1,65},{65,1},{2,66},{66,2},{3,67},{67,3},{4,68},{68... | collective-permute-start | bytes 884744 | tf_op jit(solution)/shard_map/ppermute | solution.py:195
  83.6 3.3 %copy-start.11 = (bf16[1,1,128,1536]{3,2,1,0:T(8,128)(2,1)S(1)}, bf16[1,1,128,1536]{3,2,1,0:T(8,128)(2,1)}, u32[]{:S(2)}) copy-start(bf16[1,1,128,1536]{3,2,1,0:T(8,128)(2,1)} %param.16) | copy-start | bytes 1179652
  86.9 2.1 %copy-start = (bf16[64,24,1536]{2,1,0:T(8,128)(2,1)}, bf16[64,24,1536]{2,1,0:T(8,128)(2,1)S(1)}, u32[]{:S(2)}) copy-start(bf16[64,24,1536]{2,1,0:T(8,128)(2,1)S(1)} %weight_in_place.1) | copy-start | bytes 14155780
  86.9 2.1 %copy-start.2 = (bf16[1,1,128,1536]{3,2,1,0:T(8,128)(2,1)S(1)}, bf16[1,1,128,1536]{3,2,1,0:T(8,128)(2,1)}, u32[]{:S(2)}) copy-start(bf16[1,1,128,1536]{3,2,1,0:T(8,128)(2,1)} %param.12) | copy-start | bytes 1179652
  86.9 2.1 %copy-start.3 = (bf16[1,1,128,1536]{3,2,1,0:T(8,128)(2,1)S(1)}, bf16[1,1,128,1536]{3,2,1,0:T(8,128)(2,1)}, u32[]{:S(2)}) copy-start(bf16[1,1,128,1536]{3,2,1,0:T(8,128)(2,1)} %param.11) | copy-start | bytes 1179652
  87.0 2.1 %copy-start.4 = (bf16[1,1,128,1536]{3,2,1,0:T(8,128)(2,1)S(1)}, bf16[1,1,128,1536]{3,2,1,0:T(8,128)(2,1)}, u32[]{:S(2)}) copy-start(bf16[1,1,128,1536]{3,2,1,0:T(8,128)(2,1)} %param.10) | copy-start | bytes 1179652
  90.3 0.9 copy-start.5
  91.2 0.6 copy-start.7
  109.6 0.6 copy-start.9
  110.2 10.7 %copy-start.8 = (f32[1,1536]{1,0:T(1,128)S(1)}, f32[1,1536]{1,0:T(1,128)}, u32[]{:S(2)}) copy-start(f32[1,1536]{1,0:T(1,128)} %copy-done.7) | copy-start | bytes 18436
  110.2 10.7 %copy-start.10 = (f32[1,1536]{1,0:T(1,128)S(1)}, f32[1,1536]{1,0:T(1,128)}, u32[]{:S(2)}) copy-start(f32[1,1536]{1,0:T(1,128)} %copy-done.9) | copy-start | bytes 18436
  110.2 53.0 %all-to-all-start.1 = ((bf16[16,2,8,1536]{3,2,1,0:T(8,128)(2,1)}), bf16[16,2,8,1536]{3,2,1,0:T(8,128)(2,1)S(1)}, u32[]{:S(2)}, u32[]{:S(2)}) async-start(bf16[16,2,8,1536]{3,2,1,0:T(8,128)(2,1)} %get-tuple-element.29), calls=%async_computation.1 | async-start | bytes 1572864 | tf_op jit(solution)/shard_map/all_to_all | solution.py:306
  146.2 11.8 %collective-permute-start.15 = (f32[1,3072]{1,0:T(1,128)S(1)}, f32[1,3072]{1,0:T(1,128)S(1)}, u32[]{:S(2)}, u32[]{:S(2)}) collective-permute-start(f32[1,3072]{1,0:T(1,128)S(1)} %bitcast.95), channel_id=1, source_target_pairs={{0,1},{1,0},{2,3},{3,2},{4,5},{5,4},{6,7},{7,6},{8,9},{9,8},{10,11... | collective-permute-start | bytes 36872 | tf_op jit(solution)/shard_map/ppermute | solution.py:273
  153.0 9.5 %collective-permute-start.14 = (f32[1,3072]{1,0:T(1,128)S(1)}, f32[1,3072]{1,0:T(1,128)S(1)}, u32[]{:S(2)}, u32[]{:S(2)}) collective-permute-start(f32[1,3072]{1,0:T(1,128)S(1)} %bitcast.96), channel_id=1, source_target_pairs={{64,66},{65,67},{66,64},{67,65},{68,70},{69,71},{70,68},{71,69},{7... | collective-permute-start | bytes 36872 | tf_op jit(solution)/shard_map/ppermute | solution.py:273
  163.2 45.2 %all-to-all-start.2 = ((bf16[16,2,8,1536]{3,2,1,0:T(8,128)(2,1)}), bf16[16,2,8,1536]{3,2,1,0:T(8,128)(2,1)S(1)}, u32[]{:S(2)}, u32[]{:S(2)}) async-start(bf16[16,2,8,1536]{3,2,1,0:T(8,128)(2,1)} %get-tuple-element.38), calls=%async_computation.2 | async-start | bytes 1572864 | tf_op jit(solution)/shard_map/all_to_all | solution.py:306
  171.2 3.3 %collective-permute-start.16 = (f32[1,3072]{1,0:T(1,128)}, f32[1,3072]{1,0:T(1,128)S(1)}, u32[]{:S(2)}, u32[]{:S(2)}) collective-permute-start(f32[1,3072]{1,0:T(1,128)} %fusion.5), channel_id=1, source_target_pairs={{0,64},{64,0},{1,65},{65,1},{2,66},{66,2},{3,67},{67,3},{4,68},{68... | collective-permute-start | bytes 36872 | tf_op jit(solution)/shard_map/ppermute | solution.py:195
  175.2 7.6 %collective-permute-start.17 = (f32[1,3072]{1,0:T(1,128)S(1)}, f32[1,3072]{1,0:T(1,128)S(1)}, u32[]{:S(2)}, u32[]{:S(2)}) collective-permute-start(f32[1,3072]{1,0:T(1,128)S(1)} %add.589), channel_id=1, source_target_pairs={{0,128},{128,0},{256,384},{384,256},{1,129},{129,1},{257,385},{385... | collective-permute-start | bytes 36872 | tf_op jit(solution)/shard_map/ppermute | solution.py:281
  182.8 8.9 %collective-permute-start.18 = (f32[1,3072]{1,0:T(1,128)S(1)}, f32[1,3072]{1,0:T(1,128)S(1)}, u32[]{:S(2)}, u32[]{:S(2)}) collective-permute-start(f32[1,3072]{1,0:T(1,128)S(1)} %add.590), channel_id=1, source_target_pairs={{0,256},{128,384},{256,0},{384,128},{1,257},{129,385},{257,1},{385... | collective-permute-start | bytes 36872 | tf_op jit(solution)/shard_map/ppermute | solution.py:281
  184.8 2.3 %copy-start.1 = (bf16[64,24,1536]{2,1,0:T(8,128)(2,1)S(1)}, bf16[64,24,1536]{2,1,0:T(8,128)(2,1)}, u32[]{:S(2)}) copy-start(bf16[64,24,1536]{2,1,0:T(8,128)(2,1)} %copy-done) | copy-start | bytes 14155780
  187.1 1.1 copy-start.6

commit v3 on v2

--- a/solution.py
+++ b/solution.py
@@ -11,6 +11,7 @@
 HEAD = 128
 NEGATIVE = -1e30
 VMEM_BYTES = 20 * 1024 * 1024
+WEIGHT_FLOPS = 36_800_000_000
 DISTANCES = (((0, 8), (4, -4)), ((1, -1), (7, -7)), ((2, -2), (6, -6)), ((3, -3), (5, -5)))
 
 
@@ -250,7 +251,7 @@
         out_shape=jax.ShapeDtypeStruct((4 * seq, rows, channels), jnp.bfloat16),
         in_specs=[pl.BlockSpec(memory_space=pltpu.SMEM)] + in_vmem(len(arrays)),
         out_specs=in_vmem(1)[0],
-        cost_estimate=pl.CostEstimate(flops=0, bytes_accessed=size, transcendentals=0),
+        cost_estimate=pl.CostEstimate(flops=WEIGHT_FLOPS, bytes_accessed=size, transcendentals=0),
         compiler_params=pltpu.CompilerParams(vmem_limit_bytes=VMEM_BYTES),
         name="weight_in_place",
     )(jnp.concatenate(places).astype(jnp.int32), *arrays)
@@ -276,10 +277,10 @@
 
 
 def group_sum(total):
-    total = total + shift(total, "core", 1)
-    for by in (1, 2):
-        total = total + lax.ppermute(total, "x", [(i, i ^ by) for i in range(lax.axis_size("x"))])
-    return total
+    terms = list(lax.all_gather(total, ("x", "core"), axis=0, tiled=True))
+    while len(terms) > 1:
+        terms = [left + right for left, right in zip(terms[::2], terms[1::2])]
+    return terms[0]
 
 
 def on_device(
@@ -309,7 +310,6 @@
     sent = jnp.stack(
         [array.reshape(owners, near, channels) for array in (query, key, value, flat_up)], axis=1
     )
-    fetched, sent = lax.optimization_barrier((fetched, sent))
     moved = exchange(sent)
 
     weight = whole_weight(fetched)
@@ -330,7 +330,7 @@
     early, late, parts = lax.optimization_barrier((early, late, parts))
     late = exchange(late)
     tokens = lax.axis_size("x") * lax.axis_size("core") * lax.axis_size("fsdp") * owners * frames_here * positions
-    totals = group_sum(parts)[0] / math.sqrt(tokens)
+    totals = group_sum(parts) / math.sqrt(tokens)
 
     results = output(early, space, grad_query, gate_space, gate_time, weight)
     results += add_returned(late, grad_key, grad_value)

time: 212 us -> 208 us (0.981)
  blocking collectives: 25.2 us -> 38.7 us
  waiting for transfers between devices: 57.8 us -> 48.3 us
  starting transfers between devices: 94.3 us -> 86.5 us
    all_gather x0 -> x1, blocking collectives: none -> 13.6 us  [group_sum(): terms = list(lax.all_gather(total, ('x', 'core'), axis=0, tiled=True))]
    ppermute x2 -> x0, starting transfers between devices: 7.85 us -> none  [group_sum(): lax.ppermute(total, 'x', [(i, i ^ by) for i in range(lax.axis_size('x'))])]
    ppermute x2, waiting for transfers between devices: 6.79 us -> 0.01 us  [fetch_rows(): fetched.append(lax.ppermute(out_weight, ('x', 'core', 'seq'), pairs))]
    all_to_all x3, waiting for transfers between devices: 27.3 us -> 24.2 us  [exchange(): return lax.all_to_all(array, 'seq', split_axis=0, concat_axis=0, tiled=True)]
    all_to_all x3, starting transfers between devices: 26.2 us -> 28.4 us  [exchange(): return lax.all_to_all(array, 'seq', split_axis=0, concat_axis=0, tiled=True)]
    ppermute x13 -> x12, starting transfers between devices: 34.9 us -> 32.7 us  [shift(): lax.ppermute(array, axis, [(i, (i + by) % size) for i in range(size)])]
    ppermute x13 -> x12, waiting for transfers between devices: 16.9 us -> 18.8 us  [shift(): lax.ppermute(array, axis, [(i, (i + by) % size) for i in range(size)])]
    unnamed x32 -> x34, local copies, waits for them, and re-layouts: 6.05 us -> 6.05 us
  transfers between devices with their start and end apart: 22 -> 19, of which waited for: 14 -> 9; matrix products, arithmetic and copies ran while one was open for 4% -> 4% of each run, Pallas kernels for 3% -> 3%
where the time goes in v3:
time: 208 us; the launch traced here: 205 us
  starting transfers between devices  86.5 us (42%)
  waiting for transfers between devices  48.3 us (23%)
  blocking collectives  38.7 us (19%)
  Pallas kernels  11 us (5%)
  local copies, waits for them, and re-layouts  9.08 us (4%)
  matrix products  5.58 us (3%)
  other arithmetic  3.87 us (2%)
  between operations  2.48 us (1%)
    ppermute x12, starting transfers between devices, shift(): lax.ppermute(array, axis, [(i, (i + by) % size) for i in range(size)])  32.7 us
    all_to_all x3, starting transfers between devices, exchange(): return lax.all_to_all(array, 'seq', split_axis=0, concat_axis=0, tiled=True)  28.4 us
    all_gather x2, blocking collectives, all_sum(): lax.all_gather(array, axis, axis=0, tiled=True)  25.2 us
    all_to_all x3, waiting for transfers between devices, exchange(): return lax.all_to_all(array, 'seq', split_axis=0, concat_axis=0, tiled=True)  24.2 us
    ppermute x12, waiting for transfers between devices, shift(): lax.ppermute(array, axis, [(i, (i + by) % size) for i in range(size)])  18.8 us
    ppermute x2, starting transfers between devices, fetch_rows(): fetched.append(lax.ppermute(out_weight, ('x', 'core', 'seq'), pairs))  14.2 us
    all_gather x1, blocking collectives, group_sum(): terms = list(lax.all_gather(total, ('x', 'core'), axis=0, tiled=True))  13.6 us
    ppermute x2, starting transfers between devices, frame_pair(): fetched.append(lax.ppermute(array, ('x', 'core', 'seq'), pairs))  11.1 us
  transfers between devices with their start and end apart: 19, of which 9 were waited for; matrix products, arithmetic and copies ran while one was open for 4% of the time, Pallas kernels for 3%

profile of v3, /device:TPU:6, one launch (start us, length us, event | category | flops | bytes accessed | tf_op | source)
XLA Modules:
  0.0 205.5 jit_solution(7406438930115595138)
XLA Ops:
  0.6 12.3 %collective-permute-start = (bf16[24,1536]{1,0:T(8,128)(2,1)}, bf16[24,1536]{1,0:T(8,128)(2,1)S(1)}, u32[]{:S(2)}, u32[]{:S(2)}) collective-permute-start(bf16[24,1536]{1,0:T(8,128)(2,1)} %param.13), channel_id=1, source_target_pairs={{68,64},{69,65},{70,66},{71,67},{72,68},{73,69},{74,70},{75,71},{7... | collective-permute-start | bytes 221192 | tf_op jit(solution)/shard_map/ppermute | solution.py:216
  12.9 1.9 collective-permute-start.1
  14.9 2.8 %pad_maximum_fusion = bf16[16,4,8,1536]{3,2,1,0:T(8,128)(2,1)} fusion(bf16[16,1,8,1536]{3,2,1,0:T(8,128)(2,1)} %bitcast.93, bf16[16,1,8,1536]{3,2,1,0:T(8,128)(2,1)} %bitcast.87, bf16[16,1,8,1536]{3,2,1,0:T(8,128)(2,1)} %bitcast.89, bf16[16,1,8,1536]{3,2,1,0:T(8,128)(2,1)} %bitcast.91), kind=kLoop, calls=%fused_computation.1 | loop fusion | flops 2359296 | bytes 3145728 | tf_op jit(solution)/shard_map/stack | solution.py:310
  17.6 9.5 %all-to-all-start = ((bf16[16,4,8,1536]{3,2,1,0:T(8,128)(2,1)}), bf16[16,4,8,1536]{3,2,1,0:T(8,128)(2,1)S(1)}, u32[]{:S(2)}, u32[]{:S(2)}) async-start(bf16[16,4,8,1536]{3,2,1,0:T(8,128)(2,1)} %pad_maximum_fusion), calls=%async_computation | async-start | bytes 3145728 | tf_op jit(solution)/shard_map/all_to_all | solution.py:307
  27.3 5.1 %collective-permute-start.3 = (bf16[2,24,1536]{2,1,0:T(8,128)(2,1)S(1)}, bf16[2,24,1536]{2,1,0:T(8,128)(2,1)S(1)}, u32[]{:S(2)}, u32[]{:S(2)}) collective-permute-start(bf16[2,24,1536]{2,1,0:T(8,128)(2,1)S(1)} %get-tuple-element.43), channel_id=1, source_target_pairs={{0,32},{16,48},{32,0},{48,16},{1,33},{17,49},{33,1},{49,17},{2,34}... | collective-permute-start | bytes 442376 | tf_op jit(solution)/shard_map/ppermute | solution.py:196
  32.4 3.0 %collective-permute-start.2 = (bf16[2,24,1536]{2,1,0:T(8,128)(2,1)S(1)}, bf16[2,24,1536]{2,1,0:T(8,128)(2,1)S(1)}, u32[]{:S(2)}, u32[]{:S(2)}) collective-permute-start(bf16[2,24,1536]{2,1,0:T(8,128)(2,1)S(1)} %get-tuple-element.43), channel_id=1, source_target_pairs={{0,48},{16,0},{32,16},{48,32},{1,49},{17,1},{33,17},{49,33},{2,50}... | collective-permute-start | bytes 442376 | tf_op jit(solution)/shard_map/ppermute | solution.py:196
  35.4 2.9 %collective-permute-start.4 = (bf16[2,24,1536]{2,1,0:T(8,128)(2,1)S(1)}, bf16[2,24,1536]{2,1,0:T(8,128)(2,1)S(1)}, u32[]{:S(2)}, u32[]{:S(2)}) collective-permute-start(bf16[2,24,1536]{2,1,0:T(8,128)(2,1)S(1)} %get-tuple-element.43), channel_id=1, source_target_pairs={{0,16},{16,32},{32,48},{48,0},{1,17},{17,33},{33,49},{49,1},{2,18}... | collective-permute-start | bytes 442376 | tf_op jit(solution)/shard_map/ppermute | solution.py:196
  38.3 2.4 %collective-permute-done.2 = bf16[2,24,1536]{2,1,0:T(8,128)(2,1)S(1)} collective-permute-done((bf16[2,24,1536]{2,1,0:T(8,128)(2,1)S(1)}, bf16[2,24,1536]{2,1,0:T(8,128)(2,1)S(1)}, u32[]{:S(2)}, u32[]{:S(2)}) %collective-permute-start.2) | collective-permute-done | bytes 147488 | tf_op jit(solution)/shard_map/ppermute | solution.py:196
  40.7 4.4 %collective-permute-done.4 = bf16[2,24,1536]{2,1,0:T(8,128)(2,1)S(1)} collective-permute-done((bf16[2,24,1536]{2,1,0:T(8,128)(2,1)S(1)}, bf16[2,24,1536]{2,1,0:T(8,128)(2,1)S(1)}, u32[]{:S(2)}, u32[]{:S(2)}) %collective-permute-start.4) | collective-permute-done | bytes 147488 | tf_op jit(solution)/shard_map/ppermute | solution.py:196
  45.1 1.9 collective-permute-start.8
  47.0 3.9 %collective-permute-start.6 = (bf16[4,2,24,1536]{3,2,1,0:T(8,128)(2,1)S(1)}, bf16[4,2,24,1536]{3,2,1,0:T(8,128)(2,1)S(1)}, u32[]{:S(2)}, u32[]{:S(2)}) collective-permute-start(bf16[4,2,24,1536]{3,2,1,0:T(8,128)(2,1)S(1)} %pad_maximum_fusion.1.refs_0_), channel_id=1, source_target_pairs={{0,384},{128,0},{256,128},{384,256},{1,385},{129,1},{257,129},{385... | collective-permute-start | bytes 1769480 | tf_op jit(solution)/shard_map/ppermute | solution.py:196
  51.1 1.9 collective-permute-start.5
  53.0 9.5 %collective-permute-done.8.refs_8_ = bf16[4,2,24,1536]{3,2,1,0:T(8,128)(2,1)S(1)} collective-permute-done((bf16[4,2,24,1536]{3,2,1,0:T(8,128)(2,1)S(1)}, bf16[4,2,24,1536]{3,2,1,0:T(8,128)(2,1)S(1)}, u32[]{:S(2)}, u32[]{:S(2)}) %collective-permute-start.8) | collective-permute-done | bytes 589856 | tf_op jit(solution)/shard_map/ppermute | solution.py:196
  62.5 0.7 slice.36
  63.3 3.4 %collective-permute-start.9 = (bf16[2,2,24,1536]{3,2,1,0:T(8,128)(2,1)}, bf16[2,2,24,1536]{3,2,1,0:T(8,128)(2,1)}, u32[]{:S(2)}, u32[]{:S(2)}) collective-permute-start(bf16[2,2,24,1536]{3,2,1,0:T(8,128)(2,1)} %slice.36), channel_id=1, source_target_pairs={{0,128},{128,256},{256,384},{384,0},{1,129},{129,257},{257,385},{3... | collective-permute-start | bytes 884744 | tf_op jit(solution)/shard_map/ppermute | solution.py:196
  66.7 0.7 slice.37
  67.4 2.4 %collective-permute-start.11 = (bf16[2,2,24,1536]{3,2,1,0:T(8,128)(2,1)}, bf16[2,2,24,1536]{3,2,1,0:T(8,128)(2,1)}, u32[]{:S(2)}, u32[]{:S(2)}) collective-permute-start(bf16[2,2,24,1536]{3,2,1,0:T(8,128)(2,1)} %slice.37), channel_id=1, source_target_pairs={{0,384},{128,0},{256,128},{384,256},{1,385},{129,1},{257,129},{385... | collective-permute-start | bytes 884744 | tf_op jit(solution)/shard_map/ppermute | solution.py:196
  69.8 1.9 collective-permute-start.13
  71.8 2.4 %collective-permute-start.7 = (bf16[4,2,24,1536]{3,2,1,0:T(8,128)(2,1)S(1)}, bf16[4,2,24,1536]{3,2,1,0:T(8,128)(2,1)}, u32[]{:S(2)}, u32[]{:S(2)}) collective-permute-start(bf16[4,2,24,1536]{3,2,1,0:T(8,128)(2,1)S(1)} %collective-permute-done.6.refs_2_), channel_id=1, source_target_pairs={{0,64},{64,0},{1,65},{65,1},{2,66},{66,2},{3,67},{67,3},{4,68},{68... | collective-permute-start | bytes 1769480 | tf_op jit(solution)/shard_map/ppermute | solution.py:196
  75.9 1.9 collective-permute-start.10
  77.9 1.4 collective-permute-done.11.refs_6_
  79.2 1.9 collective-permute-start.12
  81.9 1.2 collective-permute-done.12.refs_7_
  83.0 2.1 %weight_in_place.1 = bf16[64,24,1536]{2,1,0:T(8,128)(2,1)S(1)} custom-call(s32[64]{0:T(128)S(1)} %concatenate.6.place_ref, bf16[4,2,24,1536]{3,2,1,0:T(8,128)(2,1)S(1)} %pad_maximum_fusion.1.refs_0_, bf16[4,2,24,1536]{3,2,1,0:T(8,128)(2,1)} %collective-permute-done.5.refs_1_, bf16[4,2,24,1536]{3,2,1,0:T(8,128)(2,1)S(1)} %collective-permute-done.6.refs_2_, ...), custom_call_target="tpu_custom_call" | custom-call | flops 36800000000 | bytes 4718592 | tf_op jit(solution)/shard_map/weight_in_place/pallas_call | solution.py:249
  85.2 1.6 convolution_bitcast_fusion.mixed_ref
  87.3 1.3 space_attention.1
  88.6 0.9 copy-done.5
  89.5 0.6 copy-done.7
  90.1 8.1 %all-to-all-done.moved_ref = bf16[16,4,8,1536]{3,2,1,0:T(8,128)(2,1)S(1)} async-done(((bf16[16,4,8,1536]{3,2,1,0:T(8,128)(2,1)}), bf16[16,4,8,1536]{3,2,1,0:T(8,128)(2,1)S(1)}, u32[]{:S(2)}, u32[]{:S(2)}) %all-to-all-start) | async-done | bytes 1572896 | tf_op jit(solution)/shard_map/all_to_all | solution.py:307
  98.2 4.0 %fusion.mixed_ref = f32[128,1536]{1,0:T(8,128)S(1)} fusion(bf16[1536,1536]{1,0:T(8,128)(2,1)} %bitcast.85, bf16[16,4,8,1536]{3,2,1,0:T(8,128)(2,1)S(1)} %all-to-all-done.moved_ref), kind=kOutput, calls=%fused_computation.3 | convolution fusion | flops 603979776 | bytes 5898240 | tf_op jit(solution)/shard_map/td,nd->tn/dot_general | solution.py:318
  102.2 2.5 %time_attention.1 = (bf16[16,2,8,1536]{3,2,1,0:T(8,128)(2,1)}, bf16[16,2,8,1536]{3,2,1,0:T(8,128)(2,1)}, f32[1,1536]{1,0:T(1,128)S(1)}) custom-call(s32[1]{0:T(128)S(6)} %copy.21.count_ref, bf16[16,4,8,1536]{3,2,1,0:T(8,128)(2,1)S(1)} %all-to-all-done.moved_ref, f32[128,1536]{1,0:T(8,128)S(1)} %fusion.mixed_ref, f32[1,1536]{1,0:T(1,128)S(1)} %reshape.305.gate_ref.gate_time_ref), custom_call_target="tpu_custom_call" | custom-call | flops 301989888 | bytes 3145728 | tf_op jit(solution)/shard_map/time_attention/pallas_call | solution.py:103
  104.7 0.6 copy-done.9
  105.3 10.9 %all-to-all-start.1 = ((bf16[16,2,8,1536]{3,2,1,0:T(8,128)(2,1)}), bf16[16,2,8,1536]{3,2,1,0:T(8,128)(2,1)S(1)}, u32[]{:S(2)}, u32[]{:S(2)}) async-start(bf16[16,2,8,1536]{3,2,1,0:T(8,128)(2,1)} %get-tuple-element.25), calls=%async_computation.1 | async-start | bytes 1572864 | tf_op jit(solution)/shard_map/all_to_all | solution.py:307
  116.2 12.7 %all-gather.1 = f32[8,1,3072]{2,1,0:T(1,128)S(1)} all-gather(f32[1,1,3072]{2,1,0:T(1,128)S(1)} %maximum_bitcast_fusion), channel_id=1, replica_groups=mesh['x'=4,'core'=2,'fsdp'=4,'seq'=16] {'x','core'}, dimensions={0}, use_global_device_ids=true | all-gather | bytes 110592 | tf_op jit(solution)/shard_map/all_gather | solution.py:262
  129.1 12.4 %all-gather = f32[12288]{0:T(1024)S(1)} all-gather(f32[3072]{0:T(1024)S(1)} %reduce_sum.18), channel_id=2, replica_groups=mesh['x'=4,'core'=2,'fsdp'=4,'seq'=16] {'fsdp'}, dimensions={0}, use_global_device_ids=true | all-gather | bytes 61440 | tf_op jit(solution)/shard_map/all_gather | solution.py:262
  141.5 6.8 %collective-permute-start.15 = (f32[1,3072]{1,0:T(1,128)S(1)}, f32[1,3072]{1,0:T(1,128)S(1)}, u32[]{:S(2)}, u32[]{:S(2)}) collective-permute-start(f32[1,3072]{1,0:T(1,128)S(1)} %bitcast.99), channel_id=1, source_target_pairs={{0,1},{1,0},{2,3},{3,2},{4,5},{5,4},{6,7},{7,6},{8,9},{9,8},{10,11... | collective-permute-start | bytes 36872 | tf_op jit(solution)/shard_map/ppermute | solution.py:274
  148.4 4.3 %collective-permute-start.14 = (f32[1,3072]{1,0:T(1,128)S(1)}, f32[1,3072]{1,0:T(1,128)S(1)}, u32[]{:S(2)}, u32[]{:S(2)}) collective-permute-start(f32[1,3072]{1,0:T(1,128)S(1)} %bitcast.100), channel_id=1, source_target_pairs={{64,66},{65,67},{66,64},{67,65},{68,70},{69,71},{70,68},{71,69},{7... | collective-permute-start | bytes 36872 | tf_op jit(solution)/shard_map/ppermute | solution.py:274
  152.7 0.6 collective-permute-done.15
  153.3 4.6 %collective-permute-done.14 = f32[1,3072]{1,0:T(1,128)S(1)} collective-permute-done((f32[1,3072]{1,0:T(1,128)S(1)}, f32[1,3072]{1,0:T(1,128)S(1)}, u32[]{:S(2)}, u32[]{:S(2)}) %collective-permute-start.14) | collective-permute-done | bytes 12320 | tf_op jit(solution)/shard_map/ppermute | solution.py:274
  157.9 0.6 fusion.5
  158.6 8.0 %all-to-all-start.2 = ((bf16[16,2,8,1536]{3,2,1,0:T(8,128)(2,1)}), bf16[16,2,8,1536]{3,2,1,0:T(8,128)(2,1)S(1)}, u32[]{:S(2)}, u32[]{:S(2)}) async-start(bf16[16,2,8,1536]{3,2,1,0:T(8,128)(2,1)} %get-tuple-element.34), calls=%async_computation.2 | async-start | bytes 1572864 | tf_op jit(solution)/shard_map/all_to_all | solution.py:307
  166.6 2.3 %copy-done.1 = bf16[64,24,1536]{2,1,0:T(8,128)(2,1)S(1)} copy-done((bf16[64,24,1536]{2,1,0:T(8,128)(2,1)S(1)}, bf16[64,24,1536]{2,1,0:T(8,128)(2,1)}, u32[]{:S(2)}) %copy-start.1) | copy-done | bytes 4718616
  168.9 1.1 copy-done.6
  170.0 3.5 %output.1 = (bf16[128,1536]{1,0:T(8,128)(2,1)}, bf16[128,1536]{1,0:T(8,128)(2,1)}) custom-call(bf16[16,2,8,1536]{3,2,1,0:T(8,128)(2,1)S(1)} %all-to-all-done.1.time_ref.moved_ref, bf16[16,2,8,1536]{3,2,1,0:T(8,128)(2,1)S(1)} %all-to-all-done.1.time_ref.moved_ref, bf16[128,1536]{1,0:T(8,128)(2,1)S(1)} %get-tuple-element.30.space_ref, ...), custom_call_target="tpu_custom_call" | custom-call | tf_op jit(solution)/shard_map/output/pallas_call | solution.py:157
  173.6 13.6 %all-gather.2 = f32[8,1,3072]{2,1,0:T(1,128)S(1)} all-gather(f32[1,1,3072]{2,1,0:T(1,128)S(1)} %bitcast.98), channel_id=1, replica_groups=mesh['x'=4,'core'=2,'fsdp'=4,'seq'=16] {'x','core'}, dimensions={0}, use_global_device_ids=true | all-gather | bytes 110592 | tf_op jit(solution)/shard_map/all_gather | solution.py:280
  187.2 0.6 slice_reduce_fusion
  187.8 16.1 %all-to-all-done.2.moved_ref = bf16[16,2,8,1536]{3,2,1,0:T(8,128)(2,1)S(1)} async-done(((bf16[16,2,8,1536]{3,2,1,0:T(8,128)(2,1)}), bf16[16,2,8,1536]{3,2,1,0:T(8,128)(2,1)S(1)}, u32[]{:S(2)}, u32[]{:S(2)}) %all-to-all-start.2) | async-done | bytes 786464 | tf_op jit(solution)/shard_map/all_to_all | solution.py:307
  203.9 1.6 add_returned.1
  (65 shorter events, 2.0 us)
Async XLA Ops:
  0.6 26.6 %collective-permute-start = (bf16[24,1536]{1,0:T(8,128)(2,1)}, bf16[24,1536]{1,0:T(8,128)(2,1)S(1)}, u32[]{:S(2)}, u32[]{:S(2)}) collective-permute-start(bf16[24,1536]{1,0:T(8,128)(2,1)} %param.13), channel_id=1, source_target_pairs={{68,64},{69,65},{70,66},{71,67},{72,68},{73,69},{74,70},{75,71},{7... | collective-permute-start | bytes 221192 | tf_op jit(solution)/shard_map/ppermute | solution.py:216
  12.9 14.3 %collective-permute-start.1 = (bf16[24,1536]{1,0:T(8,128)(2,1)}, bf16[24,1536]{1,0:T(8,128)(2,1)S(1)}, u32[]{:S(2)}, u32[]{:S(2)}) collective-permute-start(bf16[24,1536]{1,0:T(8,128)(2,1)} %param.13), channel_id=1, source_target_pairs={{8,0},{9,1},{10,2},{11,3},{12,4},{13,5},{14,6},{15,7},{0,8},{1,9},... | collective-permute-start | bytes 221192 | tf_op jit(solution)/shard_map/ppermute | solution.py:216
  17.6 9.6 %copy-start.12 = (bf16[24,1536]{1,0:T(8,128)(2,1)S(1)}, bf16[24,1536]{1,0:T(8,128)(2,1)}, u32[]{:S(2)}) copy-start(bf16[24,1536]{1,0:T(8,128)(2,1)} %param.13) | copy-start | bytes 221188
  17.6 80.6 %all-to-all-start = ((bf16[16,4,8,1536]{3,2,1,0:T(8,128)(2,1)}), bf16[16,4,8,1536]{3,2,1,0:T(8,128)(2,1)S(1)}, u32[]{:S(2)}, u32[]{:S(2)}) async-start(bf16[16,4,8,1536]{3,2,1,0:T(8,128)(2,1)} %pad_maximum_fusion), calls=%async_computation | async-start | bytes 3145728 | tf_op jit(solution)/shard_map/all_to_all | solution.py:307
  27.2 23.9 %copy-start.16 = (s32[4,2,2]{2,1,0:T(2,128)S(1)}, s32[4,2,2]{2,1,0:T(2,128)}, u32[]{:S(2)}) copy-start(s32[4,2,2]{2,1,0:T(2,128)} %constant.192.clone) | copy-start | bytes 196
  27.2 48.7 %copy-start.14 = (f32[1536]{0:T(1024)S(1)}, f32[1536]{0:T(1024)}, u32[]{:S(2)}) copy-start(f32[1536]{0:T(1024)} %param.14) | copy-start | bytes 18436
  27.2 48.7 %copy-start.15 = (f32[1536]{0:T(1024)S(1)}, f32[1536]{0:T(1024)}, u32[]{:S(2)}) copy-start(f32[1536]{0:T(1024)} %param.15) | copy-start | bytes 18436
  27.3 11.0 %collective-permute-start.3 = (bf16[2,24,1536]{2,1,0:T(8,128)(2,1)S(1)}, bf16[2,24,1536]{2,1,0:T(8,128)(2,1)S(1)}, u32[]{:S(2)}, u32[]{:S(2)}) collective-permute-start(bf16[2,24,1536]{2,1,0:T(8,128)(2,1)S(1)} %get-tuple-element.43), channel_id=1, source_target_pairs={{0,32},{16,48},{32,0},{48,16},{1,33},{17,49},{33,1},{49,17},{2,34}... | collective-permute-start | bytes 442376 | tf_op jit(solution)/shard_map/ppermute | solution.py:196
  32.4 8.3 %collective-permute-start.2 = (bf16[2,24,1536]{2,1,0:T(8,128)(2,1)S(1)}, bf16[2,24,1536]{2,1,0:T(8,128)(2,1)S(1)}, u32[]{:S(2)}, u32[]{:S(2)}) collective-permute-start(bf16[2,24,1536]{2,1,0:T(8,128)(2,1)S(1)} %get-tuple-element.43), channel_id=1, source_target_pairs={{0,48},{16,0},{32,16},{48,32},{1,49},{17,1},{33,17},{49,33},{2,50}... | collective-permute-start | bytes 442376 | tf_op jit(solution)/shard_map/ppermute | solution.py:196
  35.4 9.7 %collective-permute-start.4 = (bf16[2,24,1536]{2,1,0:T(8,128)(2,1)S(1)}, bf16[2,24,1536]{2,1,0:T(8,128)(2,1)S(1)}, u32[]{:S(2)}, u32[]{:S(2)}) collective-permute-start(bf16[2,24,1536]{2,1,0:T(8,128)(2,1)S(1)} %get-tuple-element.43), channel_id=1, source_target_pairs={{0,16},{16,32},{32,48},{48,0},{1,17},{17,33},{33,49},{49,1},{2,18}... | collective-permute-start | bytes 442376 | tf_op jit(solution)/shard_map/ppermute | solution.py:196
  45.1 17.4 %collective-permute-start.8 = (bf16[4,2,24,1536]{3,2,1,0:T(8,128)(2,1)S(1)}, bf16[4,2,24,1536]{3,2,1,0:T(8,128)(2,1)S(1)}, u32[]{:S(2)}, u32[]{:S(2)}) collective-permute-start(bf16[4,2,24,1536]{3,2,1,0:T(8,128)(2,1)S(1)} %pad_maximum_fusion.1.refs_0_), channel_id=1, source_target_pairs={{0,128},{128,256},{256,384},{384,0},{1,129},{129,257},{257,385},{3... | collective-permute-start | bytes 1769480 | tf_op jit(solution)/shard_map/ppermute | solution.py:196
  47.0 19.6 %collective-permute-start.6 = (bf16[4,2,24,1536]{3,2,1,0:T(8,128)(2,1)S(1)}, bf16[4,2,24,1536]{3,2,1,0:T(8,128)(2,1)S(1)}, u32[]{:S(2)}, u32[]{:S(2)}) collective-permute-start(bf16[4,2,24,1536]{3,2,1,0:T(8,128)(2,1)S(1)} %pad_maximum_fusion.1.refs_0_), channel_id=1, source_target_pairs={{0,384},{128,0},{256,128},{384,256},{1,385},{129,1},{257,129},{385... | collective-permute-start | bytes 1769480 | tf_op jit(solution)/shard_map/ppermute | solution.py:196
  51.1 30.7 %collective-permute-start.5 = (bf16[4,2,24,1536]{3,2,1,0:T(8,128)(2,1)S(1)}, bf16[4,2,24,1536]{3,2,1,0:T(8,128)(2,1)}, u32[]{:S(2)}, u32[]{:S(2)}) collective-permute-start(bf16[4,2,24,1536]{3,2,1,0:T(8,128)(2,1)S(1)} %pad_maximum_fusion.1.refs_0_), channel_id=1, source_target_pairs={{0,64},{64,0},{1,65},{65,1},{2,66},{66,2},{3,67},{67,3},{4,68},{68... | collective-permute-start | bytes 1769480 | tf_op jit(solution)/shard_map/ppermute | solution.py:196
  63.3 12.7 %collective-permute-start.9 = (bf16[2,2,24,1536]{3,2,1,0:T(8,128)(2,1)}, bf16[2,2,24,1536]{3,2,1,0:T(8,128)(2,1)}, u32[]{:S(2)}, u32[]{:S(2)}) collective-permute-start(bf16[2,2,24,1536]{3,2,1,0:T(8,128)(2,1)} %slice.36), channel_id=1, source_target_pairs={{0,128},{128,256},{256,384},{384,0},{1,129},{129,257},{257,385},{3... | collective-permute-start | bytes 884744 | tf_op jit(solution)/shard_map/ppermute | solution.py:196
  67.4 11.8 %collective-permute-start.11 = (bf16[2,2,24,1536]{3,2,1,0:T(8,128)(2,1)}, bf16[2,2,24,1536]{3,2,1,0:T(8,128)(2,1)}, u32[]{:S(2)}, u32[]{:S(2)}) collective-permute-start(bf16[2,2,24,1536]{3,2,1,0:T(8,128)(2,1)} %slice.37), channel_id=1, source_target_pairs={{0,384},{128,0},{256,128},{384,256},{1,385},{129,1},{257,129},{385... | collective-permute-start | bytes 884744 | tf_op jit(solution)/shard_map/ppermute | solution.py:196
  69.8 12.0 %collective-permute-start.13 = (bf16[4,2,24,1536]{3,2,1,0:T(8,128)(2,1)S(1)}, bf16[4,2,24,1536]{3,2,1,0:T(8,128)(2,1)}, u32[]{:S(2)}, u32[]{:S(2)}) collective-permute-start(bf16[4,2,24,1536]{3,2,1,0:T(8,128)(2,1)S(1)} %collective-permute-done.8.refs_8_), channel_id=1, source_target_pairs={{0,64},{64,0},{1,65},{65,1},{2,66},{66,2},{3,67},{67,3},{4,68},{68... | collective-permute-start | bytes 1769480 | tf_op jit(solution)/shard_map/ppermute | solution.py:196
  71.8 11.3 %collective-permute-start.7 = (bf16[4,2,24,1536]{3,2,1,0:T(8,128)(2,1)S(1)}, bf16[4,2,24,1536]{3,2,1,0:T(8,128)(2,1)}, u32[]{:S(2)}, u32[]{:S(2)}) collective-permute-start(bf16[4,2,24,1536]{3,2,1,0:T(8,128)(2,1)S(1)} %collective-permute-done.6.refs_2_), channel_id=1, source_target_pairs={{0,64},{64,0},{1,65},{65,1},{2,66},{66,2},{3,67},{67,3},{4,68},{68... | collective-permute-start | bytes 1769480 | tf_op jit(solution)/shard_map/ppermute | solution.py:196
  75.9 5.9 %collective-permute-start.10 = (bf16[2,2,24,1536]{3,2,1,0:T(8,128)(2,1)}, bf16[2,2,24,1536]{3,2,1,0:T(8,128)(2,1)}, u32[]{:S(2)}, u32[]{:S(2)}) collective-permute-start(bf16[2,2,24,1536]{3,2,1,0:T(8,128)(2,1)} %collective-permute-done.9.refs_4_), channel_id=1, source_target_pairs={{0,64},{64,0},{1,65},{65,1},{2,66},{66,2},{3,67},{67,3},{4,68},{68... | collective-permute-start | bytes 884744 | tf_op jit(solution)/shard_map/ppermute | solution.py:196
  79.2 3.8 %collective-permute-start.12 = (bf16[2,2,24,1536]{3,2,1,0:T(8,128)(2,1)}, bf16[2,2,24,1536]{3,2,1,0:T(8,128)(2,1)}, u32[]{:S(2)}, u32[]{:S(2)}) collective-permute-start(bf16[2,2,24,1536]{3,2,1,0:T(8,128)(2,1)} %collective-permute-done.11.refs_6_), channel_id=1, source_target_pairs={{0,64},{64,0},{1,65},{65,1},{2,66},{66,2},{3,67},{67,3},{4,68},{68... | collective-permute-start | bytes 884744 | tf_op jit(solution)/shard_map/ppermute | solution.py:196
  81.8 3.3 %copy-start.11 = (bf16[1,1,128,1536]{3,2,1,0:T(8,128)(2,1)S(1)}, bf16[1,1,128,1536]{3,2,1,0:T(8,128)(2,1)}, u32[]{:S(2)}) copy-start(bf16[1,1,128,1536]{3,2,1,0:T(8,128)(2,1)} %param.16) | copy-start | bytes 1179652
  85.1 2.1 %copy-start = (bf16[64,24,1536]{2,1,0:T(8,128)(2,1)}, bf16[64,24,1536]{2,1,0:T(8,128)(2,1)S(1)}, u32[]{:S(2)}) copy-start(bf16[64,24,1536]{2,1,0:T(8,128)(2,1)S(1)} %weight_in_place.1) | copy-start | bytes 14155780
  85.2 2.1 %copy-start.2 = (bf16[1,1,128,1536]{3,2,1,0:T(8,128)(2,1)S(1)}, bf16[1,1,128,1536]{3,2,1,0:T(8,128)(2,1)}, u32[]{:S(2)}) copy-start(bf16[1,1,128,1536]{3,2,1,0:T(8,128)(2,1)} %param.12) | copy-start | bytes 1179652
  85.2 2.1 %copy-start.3 = (bf16[1,1,128,1536]{3,2,1,0:T(8,128)(2,1)S(1)}, bf16[1,1,128,1536]{3,2,1,0:T(8,128)(2,1)}, u32[]{:S(2)}) copy-start(bf16[1,1,128,1536]{3,2,1,0:T(8,128)(2,1)} %param.11) | copy-start | bytes 1179652
  85.2 2.1 %copy-start.4 = (bf16[1,1,128,1536]{3,2,1,0:T(8,128)(2,1)S(1)}, bf16[1,1,128,1536]{3,2,1,0:T(8,128)(2,1)}, u32[]{:S(2)}) copy-start(bf16[1,1,128,1536]{3,2,1,0:T(8,128)(2,1)} %param.10) | copy-start | bytes 1179652
  88.6 0.9 copy-start.5
  89.5 0.6 copy-start.7
  104.7 0.6 copy-start.9
  105.3 10.9 %copy-start.8 = (f32[1,1536]{1,0:T(1,128)S(1)}, f32[1,1536]{1,0:T(1,128)}, u32[]{:S(2)}) copy-start(f32[1,1536]{1,0:T(1,128)} %copy-done.7) | copy-start | bytes 18436
  105.3 10.9 %copy-start.10 = (f32[1,1536]{1,0:T(1,128)S(1)}, f32[1,1536]{1,0:T(1,128)}, u32[]{:S(2)}) copy-start(f32[1,1536]{1,0:T(1,128)} %copy-done.9) | copy-start | bytes 18436
  105.3 53.3 %all-to-all-start.1 = ((bf16[16,2,8,1536]{3,2,1,0:T(8,128)(2,1)}), bf16[16,2,8,1536]{3,2,1,0:T(8,128)(2,1)S(1)}, u32[]{:S(2)}, u32[]{:S(2)}) async-start(bf16[16,2,8,1536]{3,2,1,0:T(8,128)(2,1)} %get-tuple-element.25), calls=%async_computation.1 | async-start | bytes 1572864 | tf_op jit(solution)/shard_map/all_to_all | solution.py:307
  141.5 11.7 %collective-permute-start.15 = (f32[1,3072]{1,0:T(1,128)S(1)}, f32[1,3072]{1,0:T(1,128)S(1)}, u32[]{:S(2)}, u32[]{:S(2)}) collective-permute-start(f32[1,3072]{1,0:T(1,128)S(1)} %bitcast.99), channel_id=1, source_target_pairs={{0,1},{1,0},{2,3},{3,2},{4,5},{5,4},{6,7},{7,6},{8,9},{9,8},{10,11... | collective-permute-start | bytes 36872 | tf_op jit(solution)/shard_map/ppermute | solution.py:274
  148.4 9.5 %collective-permute-start.14 = (f32[1,3072]{1,0:T(1,128)S(1)}, f32[1,3072]{1,0:T(1,128)S(1)}, u32[]{:S(2)}, u32[]{:S(2)}) collective-permute-start(f32[1,3072]{1,0:T(1,128)S(1)} %bitcast.100), channel_id=1, source_target_pairs={{64,66},{65,67},{66,64},{67,65},{68,70},{69,71},{70,68},{71,69},{7... | collective-permute-start | bytes 36872 | tf_op jit(solution)/shard_map/ppermute | solution.py:274
  158.6 45.3 %all-to-all-start.2 = ((bf16[16,2,8,1536]{3,2,1,0:T(8,128)(2,1)}), bf16[16,2,8,1536]{3,2,1,0:T(8,128)(2,1)S(1)}, u32[]{:S(2)}, u32[]{:S(2)}) async-start(bf16[16,2,8,1536]{3,2,1,0:T(8,128)(2,1)} %get-tuple-element.34), calls=%async_computation.2 | async-start | bytes 1572864 | tf_op jit(solution)/shard_map/all_to_all | solution.py:307
  166.6 2.3 %copy-start.1 = (bf16[64,24,1536]{2,1,0:T(8,128)(2,1)S(1)}, bf16[64,24,1536]{2,1,0:T(8,128)(2,1)}, u32[]{:S(2)}) copy-start(bf16[64,24,1536]{2,1,0:T(8,128)(2,1)} %copy-done) | copy-start | bytes 14155780
  168.9 1.1 copy-start.6
  170.0 3.5 %copy-start.13 = (f32[1,3072]{1,0:T(1,128)S(1)}, f32[1,3072]{1,0:T(1,128)}, u32[]{:S(2)}) copy-start(f32[1,3072]{1,0:T(1,128)} %fusion.5) | copy-start | bytes 36868

commit v4 on v3

--- a/solution.py
+++ b/solution.py
@@ -12,6 +12,7 @@
 NEGATIVE = -1e30
 VMEM_BYTES = 20 * 1024 * 1024
 WEIGHT_FLOPS = 36_800_000_000
+OUTPUT_FLOPS = 18_400_000_000
 DISTANCES = (((0, 8), (4, -4)), ((1, -1), (7, -7)), ((2, -2), (6, -6)), ((3, -3), (5, -5)))
 
 
@@ -167,6 +168,7 @@
         out_specs=(columns,) * 2,
         scratch_shapes=[pltpu.VMEM((tokens, channels), jnp.bfloat16)],
         compiler_params=pltpu.CompilerParams(vmem_limit_bytes=VMEM_BYTES),
+        cost_estimate=pl.CostEstimate(flops=OUTPUT_FLOPS, bytes_accessed=0, transcendentals=0),
         name="output",
     )(returned, returned, space, grad, gate_space, gate_time, weight)
 
@@ -326,8 +328,9 @@
     early = exchange(early)
 
     parts = jnp.concatenate([part_space, part_time], axis=1)
-    parts = frame_pair(all_sum(all_sum(parts, ("x", "core")), "fsdp"))
-    early, late, parts = lax.optimization_barrier((early, late, parts))
+    parts = all_sum(all_sum(parts, ("x", "core")), "fsdp")
+    early, late, _ = lax.optimization_barrier((early, late, parts))
+    parts = frame_pair(parts)
     late = exchange(late)
     tokens = lax.axis_size("x") * lax.axis_size("core") * lax.axis_size("fsdp") * owners * frames_here * positions
     totals = group_sum(parts) / math.sqrt(tokens)

time: 208 us -> 205 us (0.986)
    ppermute x2, waiting for transfers between devices: 5.25 us -> 0.01 us  [frame_pair(): fetched.append(lax.ppermute(array, ('x', 'core', 'seq'), pairs))]
    all_to_all x3, waiting for transfers between devices: 24.2 us -> 28 us  [exchange(): return lax.all_to_all(array, 'seq', split_axis=0, concat_axis=0, tiled=True)]
    unnamed x34 -> x28, local copies, waits for them, and re-layouts: 6.05 us -> 6.61 us
  transfers between devices with their start and end apart: 19 -> 19, of which waited for: 9 -> 8; matrix products, arithmetic and copies ran while one was open for 4% -> 4% of each run, Pallas kernels for 3% -> 3%
where the time goes in v4:
time: 205 us; the launch traced here: 203 us
  starting transfers between devices  86.8 us (42%)
  waiting for transfers between devices  46.8 us (23%)
  blocking collectives  37.9 us (18%)
  Pallas kernels  11 us (5%)
  local copies, waits for them, and re-layouts  9.64 us (5%)
  matrix products  5.58 us (3%)
  other arithmetic  3.28 us (2%)
  between operations  2.48 us (1%)
    ppermute x12, starting transfers between devices, shift(): lax.ppermute(array, axis, [(i, (i + by) % size) for i in range(size)])  32.7 us
    all_to_all x3, starting transfers between devices, exchange(): return lax.all_to_all(array, 'seq', split_axis=0, concat_axis=0, tiled=True)  28.7 us
    all_to_all x3, waiting for transfers between devices, exchange(): return lax.all_to_all(array, 'seq', split_axis=0, concat_axis=0, tiled=True)  28 us
    all_gather x2, blocking collectives, all_sum(): lax.all_gather(array, axis, axis=0, tiled=True)  25.2 us
    ppermute x12, waiting for transfers between devices, shift(): lax.ppermute(array, axis, [(i, (i + by) % size) for i in range(size)])  18.8 us
    ppermute x2, starting transfers between devices, fetch_rows(): fetched.append(lax.ppermute(out_weight, ('x', 'core', 'seq'), pairs))  14.2 us
    all_gather x1, blocking collectives, group_sum(): terms = list(lax.all_gather(total, ('x', 'core'), axis=0, tiled=True))  12.7 us
    ppermute x2, starting transfers between devices, frame_pair(): fetched.append(lax.ppermute(array, ('x', 'core', 'seq'), pairs))  11.1 us
  transfers between devices with their start and end apart: 19, of which 8 were waited for; matrix products, arithmetic and copies ran while one was open for 4% of the time, Pallas kernels for 3%

profile of v4, /device:TPU:6, one launch (start us, length us, event | category | flops | bytes accessed | tf_op | source)
XLA Modules:
  0.0 203.5 jit_solution(10918216256578620426)
XLA Ops:
  0.6 12.3 %collective-permute-start = (bf16[24,1536]{1,0:T(8,128)(2,1)}, bf16[24,1536]{1,0:T(8,128)(2,1)S(1)}, u32[]{:S(2)}, u32[]{:S(2)}) collective-permute-start(bf16[24,1536]{1,0:T(8,128)(2,1)} %param.13), channel_id=1, source_target_pairs={{68,64},{69,65},{70,66},{71,67},{72,68},{73,69},{74,70},{75,71},{7... | collective-permute-start | bytes 221192 | tf_op jit(solution)/shard_map/ppermute | solution.py:218
  12.9 1.9 collective-permute-start.1
  14.9 2.8 %pad_maximum_fusion = bf16[16,4,8,1536]{3,2,1,0:T(8,128)(2,1)} fusion(bf16[16,1,8,1536]{3,2,1,0:T(8,128)(2,1)} %bitcast.94, bf16[16,1,8,1536]{3,2,1,0:T(8,128)(2,1)} %bitcast.88, bf16[16,1,8,1536]{3,2,1,0:T(8,128)(2,1)} %bitcast.90, bf16[16,1,8,1536]{3,2,1,0:T(8,128)(2,1)} %bitcast.92), kind=kLoop, calls=%fused_computation.1 | loop fusion | flops 2359296 | bytes 3145728 | tf_op jit(solution)/shard_map/stack | solution.py:312
  17.6 9.5 %all-to-all-start = ((bf16[16,4,8,1536]{3,2,1,0:T(8,128)(2,1)}), bf16[16,4,8,1536]{3,2,1,0:T(8,128)(2,1)S(1)}, u32[]{:S(2)}, u32[]{:S(2)}) async-start(bf16[16,4,8,1536]{3,2,1,0:T(8,128)(2,1)} %pad_maximum_fusion), calls=%async_computation | async-start | bytes 3145728 | tf_op jit(solution)/shard_map/all_to_all | solution.py:309
  27.3 5.1 %collective-permute-start.3 = (bf16[2,24,1536]{2,1,0:T(8,128)(2,1)S(1)}, bf16[2,24,1536]{2,1,0:T(8,128)(2,1)S(1)}, u32[]{:S(2)}, u32[]{:S(2)}) collective-permute-start(bf16[2,24,1536]{2,1,0:T(8,128)(2,1)S(1)} %get-tuple-element.41), channel_id=1, source_target_pairs={{0,32},{16,48},{32,0},{48,16},{1,33},{17,49},{33,1},{49,17},{2,34}... | collective-permute-start | bytes 442376 | tf_op jit(solution)/shard_map/ppermute | solution.py:198
  32.4 3.0 %collective-permute-start.2 = (bf16[2,24,1536]{2,1,0:T(8,128)(2,1)S(1)}, bf16[2,24,1536]{2,1,0:T(8,128)(2,1)S(1)}, u32[]{:S(2)}, u32[]{:S(2)}) collective-permute-start(bf16[2,24,1536]{2,1,0:T(8,128)(2,1)S(1)} %get-tuple-element.41), channel_id=1, source_target_pairs={{0,48},{16,0},{32,16},{48,32},{1,49},{17,1},{33,17},{49,33},{2,50}... | collective-permute-start | bytes 442376 | tf_op jit(solution)/shard_map/ppermute | solution.py:198
  35.4 2.9 %collective-permute-start.4 = (bf16[2,24,1536]{2,1,0:T(8,128)(2,1)S(1)}, bf16[2,24,1536]{2,1,0:T(8,128)(2,1)S(1)}, u32[]{:S(2)}, u32[]{:S(2)}) collective-permute-start(bf16[2,24,1536]{2,1,0:T(8,128)(2,1)S(1)} %get-tuple-element.41), channel_id=1, source_target_pairs={{0,16},{16,32},{32,48},{48,0},{1,17},{17,33},{33,49},{49,1},{2,18}... | collective-permute-start | bytes 442376 | tf_op jit(solution)/shard_map/ppermute | solution.py:198
  38.3 2.4 %collective-permute-done.2 = bf16[2,24,1536]{2,1,0:T(8,128)(2,1)S(1)} collective-permute-done((bf16[2,24,1536]{2,1,0:T(8,128)(2,1)S(1)}, bf16[2,24,1536]{2,1,0:T(8,128)(2,1)S(1)}, u32[]{:S(2)}, u32[]{:S(2)}) %collective-permute-start.2) | collective-permute-done | bytes 147488 | tf_op jit(solution)/shard_map/ppermute | solution.py:198
  40.7 4.4 %collective-permute-done.4 = bf16[2,24,1536]{2,1,0:T(8,128)(2,1)S(1)} collective-permute-done((bf16[2,24,1536]{2,1,0:T(8,128)(2,1)S(1)}, bf16[2,24,1536]{2,1,0:T(8,128)(2,1)S(1)}, u32[]{:S(2)}, u32[]{:S(2)}) %collective-permute-start.4) | collective-permute-done | bytes 147488 | tf_op jit(solution)/shard_map/ppermute | solution.py:198
  45.1 1.9 collective-permute-start.8
  47.0 3.9 %collective-permute-start.6 = (bf16[4,2,24,1536]{3,2,1,0:T(8,128)(2,1)S(1)}, bf16[4,2,24,1536]{3,2,1,0:T(8,128)(2,1)S(1)}, u32[]{:S(2)}, u32[]{:S(2)}) collective-permute-start(bf16[4,2,24,1536]{3,2,1,0:T(8,128)(2,1)S(1)} %pad_maximum_fusion.1.refs_0_), channel_id=1, source_target_pairs={{0,384},{128,0},{256,128},{384,256},{1,385},{129,1},{257,129},{385... | collective-permute-start | bytes 1769480 | tf_op jit(solution)/shard_map/ppermute | solution.py:198
  51.1 1.9 collective-permute-start.5
  53.0 9.5 %collective-permute-done.8.refs_8_ = bf16[4,2,24,1536]{3,2,1,0:T(8,128)(2,1)S(1)} collective-permute-done((bf16[4,2,24,1536]{3,2,1,0:T(8,128)(2,1)S(1)}, bf16[4,2,24,1536]{3,2,1,0:T(8,128)(2,1)S(1)}, u32[]{:S(2)}, u32[]{:S(2)}) %collective-permute-start.8) | collective-permute-done | bytes 589856 | tf_op jit(solution)/shard_map/ppermute | solution.py:198
  62.5 0.7 slice.36
  63.3 3.4 %collective-permute-start.9 = (bf16[2,2,24,1536]{3,2,1,0:T(8,128)(2,1)}, bf16[2,2,24,1536]{3,2,1,0:T(8,128)(2,1)}, u32[]{:S(2)}, u32[]{:S(2)}) collective-permute-start(bf16[2,2,24,1536]{3,2,1,0:T(8,128)(2,1)} %slice.36), channel_id=1, source_target_pairs={{0,128},{128,256},{256,384},{384,0},{1,129},{129,257},{257,385},{3... | collective-permute-start | bytes 884744 | tf_op jit(solution)/shard_map/ppermute | solution.py:198
  66.7 0.7 slice.37
  67.4 2.4 %collective-permute-start.11 = (bf16[2,2,24,1536]{3,2,1,0:T(8,128)(2,1)}, bf16[2,2,24,1536]{3,2,1,0:T(8,128)(2,1)}, u32[]{:S(2)}, u32[]{:S(2)}) collective-permute-start(bf16[2,2,24,1536]{3,2,1,0:T(8,128)(2,1)} %slice.37), channel_id=1, source_target_pairs={{0,384},{128,0},{256,128},{384,256},{1,385},{129,1},{257,129},{385... | collective-permute-start | bytes 884744 | tf_op jit(solution)/shard_map/ppermute | solution.py:198
  69.8 1.9 collective-permute-start.13
  71.8 2.4 %collective-permute-start.7 = (bf16[4,2,24,1536]{3,2,1,0:T(8,128)(2,1)S(1)}, bf16[4,2,24,1536]{3,2,1,0:T(8,128)(2,1)}, u32[]{:S(2)}, u32[]{:S(2)}) collective-permute-start(bf16[4,2,24,1536]{3,2,1,0:T(8,128)(2,1)S(1)} %collective-permute-done.6.refs_2_), channel_id=1, source_target_pairs={{0,64},{64,0},{1,65},{65,1},{2,66},{66,2},{3,67},{67,3},{4,68},{68... | collective-permute-start | bytes 1769480 | tf_op jit(solution)/shard_map/ppermute | solution.py:198
  75.9 1.9 collective-permute-start.10
  77.9 1.4 collective-permute-done.11.refs_6_
  79.2 1.9 collective-permute-start.12
  81.2 0.1 add.605
  81.9 1.2 collective-permute-done.12.refs_7_
  83.0 2.1 %weight_in_place.1 = bf16[64,24,1536]{2,1,0:T(8,128)(2,1)S(1)} custom-call(s32[64]{0:T(128)S(1)} %concatenate.6.place_ref, bf16[4,2,24,1536]{3,2,1,0:T(8,128)(2,1)S(1)} %pad_maximum_fusion.1.refs_0_, bf16[4,2,24,1536]{3,2,1,0:T(8,128)(2,1)} %collective-permute-done.5.refs_1_, bf16[4,2,24,1536]{3,2,1,0:T(8,128)(2,1)S(1)} %collective-permute-done.6.refs_2_, ...), custom_call_target="tpu_custom_call" | custom-call | flops 36800000000 | bytes 4718592 | tf_op jit(solution)/shard_map/weight_in_place/pallas_call | solution.py:251
  85.2 1.6 convolution_bitcast_fusion.mixed_ref
  86.8 0.5 copy-done
  87.3 1.3 space_attention.1
  88.6 0.9 copy-done.5
  89.5 0.7 copy-done.7
  90.2 8.0 %all-to-all-done.moved_ref = bf16[16,4,8,1536]{3,2,1,0:T(8,128)(2,1)S(1)} async-done(((bf16[16,4,8,1536]{3,2,1,0:T(8,128)(2,1)}), bf16[16,4,8,1536]{3,2,1,0:T(8,128)(2,1)S(1)}, u32[]{:S(2)}, u32[]{:S(2)}) %all-to-all-start) | async-done | bytes 1572896 | tf_op jit(solution)/shard_map/all_to_all | solution.py:309
  98.2 4.0 %fusion.mixed_ref = f32[128,1536]{1,0:T(8,128)S(1)} fusion(bf16[1536,1536]{1,0:T(8,128)(2,1)} %bitcast.86, bf16[16,4,8,1536]{3,2,1,0:T(8,128)(2,1)S(1)} %all-to-all-done.moved_ref), kind=kOutput, calls=%fused_computation.3 | convolution fusion | flops 603979776 | bytes 5898240 | tf_op jit(solution)/shard_map/td,nd->tn/dot_general | solution.py:320
  102.2 2.5 %time_attention.1 = (bf16[16,2,8,1536]{3,2,1,0:T(8,128)(2,1)}, bf16[16,2,8,1536]{3,2,1,0:T(8,128)(2,1)}, f32[1,1536]{1,0:T(1,128)S(1)}) custom-call(s32[1]{0:T(128)S(6)} %copy.21.count_ref, bf16[16,4,8,1536]{3,2,1,0:T(8,128)(2,1)S(1)} %all-to-all-done.moved_ref, f32[128,1536]{1,0:T(8,128)S(1)} %fusion.mixed_ref, f32[1,1536]{1,0:T(1,128)S(1)} %reshape.305.gate_ref.gate_time_ref), custom_call_target="tpu_custom_call" | custom-call | flops 301989888 | bytes 3145728 | tf_op jit(solution)/shard_map/time_attention/pallas_call | solution.py:104
  104.7 10.8 %all-to-all-start.1 = ((bf16[16,2,8,1536]{3,2,1,0:T(8,128)(2,1)}), bf16[16,2,8,1536]{3,2,1,0:T(8,128)(2,1)S(1)}, u32[]{:S(2)}, u32[]{:S(2)}) async-start(bf16[16,2,8,1536]{3,2,1,0:T(8,128)(2,1)} %get-tuple-element.24), calls=%async_computation.1 | async-start | bytes 1572864 | tf_op jit(solution)/shard_map/all_to_all | solution.py:309
  115.5 12.7 %all-gather.1 = f32[8,1,3072]{2,1,0:T(1,128)S(1)} all-gather(f32[1,1,3072]{2,1,0:T(1,128)S(1)} %maximum_bitcast_fusion), channel_id=1, replica_groups=mesh['x'=4,'core'=2,'fsdp'=4,'seq'=16] {'x','core'}, dimensions={0}, use_global_device_ids=true | all-gather | bytes 110592 | tf_op jit(solution)/shard_map/all_gather | solution.py:264
  128.3 12.4 %all-gather = f32[12288]{0:T(1024)S(1)} all-gather(f32[3072]{0:T(1024)S(1)} %reduce_sum.18), channel_id=2, replica_groups=mesh['x'=4,'core'=2,'fsdp'=4,'seq'=16] {'fsdp'}, dimensions={0}, use_global_device_ids=true | all-gather | bytes 61440 | tf_op jit(solution)/shard_map/all_gather | solution.py:264
  140.8 6.8 %collective-permute-start.15 = (f32[1,3072]{1,0:T(1,128)S(1)}, f32[1,3072]{1,0:T(1,128)S(1)}, u32[]{:S(2)}, u32[]{:S(2)}) collective-permute-start(f32[1,3072]{1,0:T(1,128)S(1)} %bitcast.99), channel_id=1, source_target_pairs={{0,1},{1,0},{2,3},{3,2},{4,5},{5,4},{6,7},{7,6},{8,9},{9,8},{10,11... | collective-permute-start | bytes 36872 | tf_op jit(solution)/shard_map/ppermute | solution.py:276
  147.7 4.3 %collective-permute-start.14 = (f32[1,3072]{1,0:T(1,128)S(1)}, f32[1,3072]{1,0:T(1,128)S(1)}, u32[]{:S(2)}, u32[]{:S(2)}) collective-permute-start(f32[1,3072]{1,0:T(1,128)S(1)} %bitcast.100), channel_id=1, source_target_pairs={{64,66},{65,67},{66,64},{67,65},{68,70},{69,71},{70,68},{71,69},{7... | collective-permute-start | bytes 36872 | tf_op jit(solution)/shard_map/ppermute | solution.py:276
  151.9 3.0 %all-to-all-done.1.time_ref.moved_ref = bf16[16,2,8,1536]{3,2,1,0:T(8,128)(2,1)S(1)} async-done(((bf16[16,2,8,1536]{3,2,1,0:T(8,128)(2,1)}), bf16[16,2,8,1536]{3,2,1,0:T(8,128)(2,1)S(1)}, u32[]{:S(2)}, u32[]{:S(2)}) %all-to-all-start.1) | async-done | bytes 786464 | tf_op jit(solution)/shard_map/all_to_all | solution.py:309
  154.9 8.4 %all-to-all-start.2 = ((bf16[16,2,8,1536]{3,2,1,0:T(8,128)(2,1)}), bf16[16,2,8,1536]{3,2,1,0:T(8,128)(2,1)S(1)}, u32[]{:S(2)}, u32[]{:S(2)}) async-start(bf16[16,2,8,1536]{3,2,1,0:T(8,128)(2,1)} %get-tuple-element.33), calls=%async_computation.2 | async-start | bytes 1572864 | tf_op jit(solution)/shard_map/all_to_all | solution.py:309
  163.4 12.7 %all-gather.2 = f32[8,1,3072]{2,1,0:T(1,128)S(1)} all-gather(f32[1,1,3072]{2,1,0:T(1,128)S(1)} %fusion.9), channel_id=1, replica_groups=mesh['x'=4,'core'=2,'fsdp'=4,'seq'=16] {'x','core'}, dimensions={0}, use_global_device_ids=true | all-gather | bytes 110592 | tf_op jit(solution)/shard_map/all_gather | solution.py:282
  176.2 0.6 slice_reduce_fusion
  176.9 2.3 %copy-done.1 = bf16[64,24,1536]{2,1,0:T(8,128)(2,1)S(1)} copy-done((bf16[64,24,1536]{2,1,0:T(8,128)(2,1)S(1)}, bf16[64,24,1536]{2,1,0:T(8,128)(2,1)}, u32[]{:S(2)}) %copy-start.1) | copy-done | bytes 4718616
  179.2 1.1 copy-done.6
  180.3 1.0 copy-done.8
  181.3 3.5 %output.1 = (bf16[128,1536]{1,0:T(8,128)(2,1)}, bf16[128,1536]{1,0:T(8,128)(2,1)}) custom-call(bf16[16,2,8,1536]{3,2,1,0:T(8,128)(2,1)S(1)} %all-to-all-done.1.time_ref.moved_ref, bf16[16,2,8,1536]{3,2,1,0:T(8,128)(2,1)S(1)} %all-to-all-done.1.time_ref.moved_ref, bf16[128,1536]{1,0:T(8,128)(2,1)S(1)} %copy-done.8, f32[128,1536]{1,0:T(8,128)S(1)} %copy-done.6, ...), custom_call_target="tpu_custom_call" | custom-call | flops 18400000000 | tf_op jit(solution)/shard_map/output/pallas_call | solution.py:158
  184.8 17.0 %all-to-all-done.2.moved_ref = bf16[16,2,8,1536]{3,2,1,0:T(8,128)(2,1)S(1)} async-done(((bf16[16,2,8,1536]{3,2,1,0:T(8,128)(2,1)}), bf16[16,2,8,1536]{3,2,1,0:T(8,128)(2,1)S(1)}, u32[]{:S(2)}, u32[]{:S(2)}) %all-to-all-start.2) | async-done | bytes 786464 | tf_op jit(solution)/shard_map/all_to_all | solution.py:309
  201.9 1.6 add_returned.1
  (59 shorter events, 1.5 us)
Async XLA Ops:
  0.6 26.6 %collective-permute-start = (bf16[24,1536]{1,0:T(8,128)(2,1)}, bf16[24,1536]{1,0:T(8,128)(2,1)S(1)}, u32[]{:S(2)}, u32[]{:S(2)}) collective-permute-start(bf16[24,1536]{1,0:T(8,128)(2,1)} %param.13), channel_id=1, source_target_pairs={{68,64},{69,65},{70,66},{71,67},{72,68},{73,69},{74,70},{75,71},{7... | collective-permute-start | bytes 221192 | tf_op jit(solution)/shard_map/ppermute | solution.py:218
  12.9 14.3 %collective-permute-start.1 = (bf16[24,1536]{1,0:T(8,128)(2,1)}, bf16[24,1536]{1,0:T(8,128)(2,1)S(1)}, u32[]{:S(2)}, u32[]{:S(2)}) collective-permute-start(bf16[24,1536]{1,0:T(8,128)(2,1)} %param.13), channel_id=1, source_target_pairs={{8,0},{9,1},{10,2},{11,3},{12,4},{13,5},{14,6},{15,7},{0,8},{1,9},... | collective-permute-start | bytes 221192 | tf_op jit(solution)/shard_map/ppermute | solution.py:218
  17.6 9.6 %copy-start.10 = (bf16[24,1536]{1,0:T(8,128)(2,1)S(1)}, bf16[24,1536]{1,0:T(8,128)(2,1)}, u32[]{:S(2)}) copy-start(bf16[24,1536]{1,0:T(8,128)(2,1)} %param.13) | copy-start | bytes 221188
  17.6 80.6 %all-to-all-start = ((bf16[16,4,8,1536]{3,2,1,0:T(8,128)(2,1)}), bf16[16,4,8,1536]{3,2,1,0:T(8,128)(2,1)S(1)}, u32[]{:S(2)}, u32[]{:S(2)}) async-start(bf16[16,4,8,1536]{3,2,1,0:T(8,128)(2,1)} %pad_maximum_fusion), calls=%async_computation | async-start | bytes 3145728 | tf_op jit(solution)/shard_map/all_to_all | solution.py:309
  27.2 23.9 %copy-start.13 = (s32[4,2,2]{2,1,0:T(2,128)S(1)}, s32[4,2,2]{2,1,0:T(2,128)}, u32[]{:S(2)}) copy-start(s32[4,2,2]{2,1,0:T(2,128)} %constant.192.clone) | copy-start | bytes 196
  27.2 48.7 %copy-start.11 = (f32[1536]{0:T(1024)S(1)}, f32[1536]{0:T(1024)}, u32[]{:S(2)}) copy-start(f32[1536]{0:T(1024)} %param.14) | copy-start | bytes 18436
  27.2 48.7 %copy-start.12 = (f32[1536]{0:T(1024)S(1)}, f32[1536]{0:T(1024)}, u32[]{:S(2)}) copy-start(f32[1536]{0:T(1024)} %param.15) | copy-start | bytes 18436
  27.3 11.0 %collective-permute-start.3 = (bf16[2,24,1536]{2,1,0:T(8,128)(2,1)S(1)}, bf16[2,24,1536]{2,1,0:T(8,128)(2,1)S(1)}, u32[]{:S(2)}, u32[]{:S(2)}) collective-permute-start(bf16[2,24,1536]{2,1,0:T(8,128)(2,1)S(1)} %get-tuple-element.41), channel_id=1, source_target_pairs={{0,32},{16,48},{32,0},{48,16},{1,33},{17,49},{33,1},{49,17},{2,34}... | collective-permute-start | bytes 442376 | tf_op jit(solution)/shard_map/ppermute | solution.py:198
  32.4 8.3 %collective-permute-start.2 = (bf16[2,24,1536]{2,1,0:T(8,128)(2,1)S(1)}, bf16[2,24,1536]{2,1,0:T(8,128)(2,1)S(1)}, u32[]{:S(2)}, u32[]{:S(2)}) collective-permute-start(bf16[2,24,1536]{2,1,0:T(8,128)(2,1)S(1)} %get-tuple-element.41), channel_id=1, source_target_pairs={{0,48},{16,0},{32,16},{48,32},{1,49},{17,1},{33,17},{49,33},{2,50}... | collective-permute-start | bytes 442376 | tf_op jit(solution)/shard_map/ppermute | solution.py:198
  35.4 9.7 %collective-permute-start.4 = (bf16[2,24,1536]{2,1,0:T(8,128)(2,1)S(1)}, bf16[2,24,1536]{2,1,0:T(8,128)(2,1)S(1)}, u32[]{:S(2)}, u32[]{:S(2)}) collective-permute-start(bf16[2,24,1536]{2,1,0:T(8,128)(2,1)S(1)} %get-tuple-element.41), channel_id=1, source_target_pairs={{0,16},{16,32},{32,48},{48,0},{1,17},{17,33},{33,49},{49,1},{2,18}... | collective-permute-start | bytes 442376 | tf_op jit(solution)/shard_map/ppermute | solution.py:198
  45.1 17.4 %collective-permute-start.8 = (bf16[4,2,24,1536]{3,2,1,0:T(8,128)(2,1)S(1)}, bf16[4,2,24,1536]{3,2,1,0:T(8,128)(2,1)S(1)}, u32[]{:S(2)}, u32[]{:S(2)}) collective-permute-start(bf16[4,2,24,1536]{3,2,1,0:T(8,128)(2,1)S(1)} %pad_maximum_fusion.1.refs_0_), channel_id=1, source_target_pairs={{0,128},{128,256},{256,384},{384,0},{1,129},{129,257},{257,385},{3... | collective-permute-start | bytes 1769480 | tf_op jit(solution)/shard_map/ppermute | solution.py:198
  47.0 19.6 %collective-permute-start.6 = (bf16[4,2,24,1536]{3,2,1,0:T(8,128)(2,1)S(1)}, bf16[4,2,24,1536]{3,2,1,0:T(8,128)(2,1)S(1)}, u32[]{:S(2)}, u32[]{:S(2)}) collective-permute-start(bf16[4,2,24,1536]{3,2,1,0:T(8,128)(2,1)S(1)} %pad_maximum_fusion.1.refs_0_), channel_id=1, source_target_pairs={{0,384},{128,0},{256,128},{384,256},{1,385},{129,1},{257,129},{385... | collective-permute-start | bytes 1769480 | tf_op jit(solution)/shard_map/ppermute | solution.py:198
  51.1 30.7 %collective-permute-start.5 = (bf16[4,2,24,1536]{3,2,1,0:T(8,128)(2,1)S(1)}, bf16[4,2,24,1536]{3,2,1,0:T(8,128)(2,1)}, u32[]{:S(2)}, u32[]{:S(2)}) collective-permute-start(bf16[4,2,24,1536]{3,2,1,0:T(8,128)(2,1)S(1)} %pad_maximum_fusion.1.refs_0_), channel_id=1, source_target_pairs={{0,64},{64,0},{1,65},{65,1},{2,66},{66,2},{3,67},{67,3},{4,68},{68... | collective-permute-start | bytes 1769480 | tf_op jit(solution)/shard_map/ppermute | solution.py:198
  63.3 12.7 %collective-permute-start.9 = (bf16[2,2,24,1536]{3,2,1,0:T(8,128)(2,1)}, bf16[2,2,24,1536]{3,2,1,0:T(8,128)(2,1)}, u32[]{:S(2)}, u32[]{:S(2)}) collective-permute-start(bf16[2,2,24,1536]{3,2,1,0:T(8,128)(2,1)} %slice.36), channel_id=1, source_target_pairs={{0,128},{128,256},{256,384},{384,0},{1,129},{129,257},{257,385},{3... | collective-permute-start | bytes 884744 | tf_op jit(solution)/shard_map/ppermute | solution.py:198
  67.4 11.8 %collective-permute-start.11 = (bf16[2,2,24,1536]{3,2,1,0:T(8,128)(2,1)}, bf16[2,2,24,1536]{3,2,1,0:T(8,128)(2,1)}, u32[]{:S(2)}, u32[]{:S(2)}) collective-permute-start(bf16[2,2,24,1536]{3,2,1,0:T(8,128)(2,1)} %slice.37), channel_id=1, source_target_pairs={{0,384},{128,0},{256,128},{384,256},{1,385},{129,1},{257,129},{385... | collective-permute-start | bytes 884744 | tf_op jit(solution)/shard_map/ppermute | solution.py:198
  69.8 12.0 %collective-permute-start.13 = (bf16[4,2,24,1536]{3,2,1,0:T(8,128)(2,1)S(1)}, bf16[4,2,24,1536]{3,2,1,0:T(8,128)(2,1)}, u32[]{:S(2)}, u32[]{:S(2)}) collective-permute-start(bf16[4,2,24,1536]{3,2,1,0:T(8,128)(2,1)S(1)} %collective-permute-done.8.refs_8_), channel_id=1, source_target_pairs={{0,64},{64,0},{1,65},{65,1},{2,66},{66,2},{3,67},{67,3},{4,68},{68... | collective-permute-start | bytes 1769480 | tf_op jit(solution)/shard_map/ppermute | solution.py:198
  71.8 11.3 %collective-permute-start.7 = (bf16[4,2,24,1536]{3,2,1,0:T(8,128)(2,1)S(1)}, bf16[4,2,24,1536]{3,2,1,0:T(8,128)(2,1)}, u32[]{:S(2)}, u32[]{:S(2)}) collective-permute-start(bf16[4,2,24,1536]{3,2,1,0:T(8,128)(2,1)S(1)} %collective-permute-done.6.refs_2_), channel_id=1, source_target_pairs={{0,64},{64,0},{1,65},{65,1},{2,66},{66,2},{3,67},{67,3},{4,68},{68... | collective-permute-start | bytes 1769480 | tf_op jit(solution)/shard_map/ppermute | solution.py:198
  75.9 5.9 %collective-permute-start.10 = (bf16[2,2,24,1536]{3,2,1,0:T(8,128)(2,1)}, bf16[2,2,24,1536]{3,2,1,0:T(8,128)(2,1)}, u32[]{:S(2)}, u32[]{:S(2)}) collective-permute-start(bf16[2,2,24,1536]{3,2,1,0:T(8,128)(2,1)} %collective-permute-done.9.refs_4_), channel_id=1, source_target_pairs={{0,64},{64,0},{1,65},{65,1},{2,66},{66,2},{3,67},{67,3},{4,68},{68... | collective-permute-start | bytes 884744 | tf_op jit(solution)/shard_map/ppermute | solution.py:198
  79.2 3.8 %collective-permute-start.12 = (bf16[2,2,24,1536]{3,2,1,0:T(8,128)(2,1)}, bf16[2,2,24,1536]{3,2,1,0:T(8,128)(2,1)}, u32[]{:S(2)}, u32[]{:S(2)}) collective-permute-start(bf16[2,2,24,1536]{3,2,1,0:T(8,128)(2,1)} %collective-permute-done.11.refs_6_), channel_id=1, source_target_pairs={{0,64},{64,0},{1,65},{65,1},{2,66},{66,2},{3,67},{67,3},{4,68},{68... | collective-permute-start | bytes 884744 | tf_op jit(solution)/shard_map/ppermute | solution.py:198
  81.8 3.3 %copy-start.9 = (bf16[1,1,128,1536]{3,2,1,0:T(8,128)(2,1)S(1)}, bf16[1,1,128,1536]{3,2,1,0:T(8,128)(2,1)}, u32[]{:S(2)}) copy-start(bf16[1,1,128,1536]{3,2,1,0:T(8,128)(2,1)} %param.16) | copy-start | bytes 1179652
  85.1 2.1 %copy-start = (bf16[64,24,1536]{2,1,0:T(8,128)(2,1)}, bf16[64,24,1536]{2,1,0:T(8,128)(2,1)S(1)}, u32[]{:S(2)}) copy-start(bf16[64,24,1536]{2,1,0:T(8,128)(2,1)S(1)} %weight_in_place.1) | copy-start | bytes 14155780
  85.2 2.1 %copy-start.2 = (bf16[1,1,128,1536]{3,2,1,0:T(8,128)(2,1)S(1)}, bf16[1,1,128,1536]{3,2,1,0:T(8,128)(2,1)}, u32[]{:S(2)}) copy-start(bf16[1,1,128,1536]{3,2,1,0:T(8,128)(2,1)} %param.12) | copy-start | bytes 1179652
  85.2 2.1 %copy-start.3 = (bf16[1,1,128,1536]{3,2,1,0:T(8,128)(2,1)S(1)}, bf16[1,1,128,1536]{3,2,1,0:T(8,128)(2,1)}, u32[]{:S(2)}) copy-start(bf16[1,1,128,1536]{3,2,1,0:T(8,128)(2,1)} %param.11) | copy-start | bytes 1179652
  85.2 2.1 %copy-start.4 = (bf16[1,1,128,1536]{3,2,1,0:T(8,128)(2,1)S(1)}, bf16[1,1,128,1536]{3,2,1,0:T(8,128)(2,1)}, u32[]{:S(2)}) copy-start(bf16[1,1,128,1536]{3,2,1,0:T(8,128)(2,1)} %param.10) | copy-start | bytes 1179652
  88.6 0.9 copy-start.5
  89.5 0.7 copy-start.7
  104.7 50.2 %all-to-all-start.1 = ((bf16[16,2,8,1536]{3,2,1,0:T(8,128)(2,1)}), bf16[16,2,8,1536]{3,2,1,0:T(8,128)(2,1)S(1)}, u32[]{:S(2)}, u32[]{:S(2)}) async-start(bf16[16,2,8,1536]{3,2,1,0:T(8,128)(2,1)} %get-tuple-element.24), calls=%async_computation.1 | async-start | bytes 1572864 | tf_op jit(solution)/shard_map/all_to_all | solution.py:309
  140.8 22.6 %collective-permute-start.15 = (f32[1,3072]{1,0:T(1,128)S(1)}, f32[1,3072]{1,0:T(1,128)S(1)}, u32[]{:S(2)}, u32[]{:S(2)}) collective-permute-start(f32[1,3072]{1,0:T(1,128)S(1)} %bitcast.99), channel_id=1, source_target_pairs={{0,1},{1,0},{2,3},{3,2},{4,5},{5,4},{6,7},{7,6},{8,9},{9,8},{10,11... | collective-permute-start | bytes 36872 | tf_op jit(solution)/shard_map/ppermute | solution.py:276
  147.7 15.7 %collective-permute-start.14 = (f32[1,3072]{1,0:T(1,128)S(1)}, f32[1,3072]{1,0:T(1,128)S(1)}, u32[]{:S(2)}, u32[]{:S(2)}) collective-permute-start(f32[1,3072]{1,0:T(1,128)S(1)} %bitcast.100), channel_id=1, source_target_pairs={{64,66},{65,67},{66,64},{67,65},{68,70},{69,71},{70,68},{71,69},{7... | collective-permute-start | bytes 36872 | tf_op jit(solution)/shard_map/ppermute | solution.py:276
  154.9 46.9 %all-to-all-start.2 = ((bf16[16,2,8,1536]{3,2,1,0:T(8,128)(2,1)}), bf16[16,2,8,1536]{3,2,1,0:T(8,128)(2,1)S(1)}, u32[]{:S(2)}, u32[]{:S(2)}) async-start(bf16[16,2,8,1536]{3,2,1,0:T(8,128)(2,1)} %get-tuple-element.33), calls=%async_computation.2 | async-start | bytes 1572864 | tf_op jit(solution)/shard_map/all_to_all | solution.py:309
  176.9 2.3 %copy-start.1 = (bf16[64,24,1536]{2,1,0:T(8,128)(2,1)S(1)}, bf16[64,24,1536]{2,1,0:T(8,128)(2,1)}, u32[]{:S(2)}) copy-start(bf16[64,24,1536]{2,1,0:T(8,128)(2,1)} %copy-done) | copy-start | bytes 14155780
  179.2 1.1 copy-start.6
  180.3 1.0 copy-start.8

commit v5 on v4

--- a/solution.py
+++ b/solution.py
@@ -11,8 +11,9 @@
 HEAD = 128
 NEGATIVE = -1e30
 VMEM_BYTES = 20 * 1024 * 1024
+STREAMING_BYTES = 60 * 1024 * 1024
 WEIGHT_FLOPS = 36_800_000_000
-OUTPUT_FLOPS = 18_400_000_000
+OUTPUT_FLOPS = 16_100_000_000
 DISTANCES = (((0, 8), (4, -4)), ((1, -1), (7, -7)), ((2, -2), (6, -6)), ((3, -3), (5, -5)))
 
 
@@ -25,25 +26,34 @@
     )
 
 
-def head_gradients(query, key, value, grad_mixed, gate, keep):
-    scale = HEAD ** (-0.5)
-    incoming = (gate * grad_mixed).astype(jnp.bfloat16)
-    scores = jnp.where(keep, contract(key, query, 1, 1) * scale, NEGATIVE)
+def head_probs(query, key, keep):
+    scores = jnp.where(keep, contract(key, query, 1, 1) * HEAD ** (-0.5), NEGATIVE)
     raised = jnp.exp(scores - jnp.max(scores, axis=0, keepdims=True))
-    probs = raised / jnp.sum(raised, axis=0, keepdims=True)
+    return raised / jnp.sum(raised, axis=0, keepdims=True)
+
+
+def head_values(probs, value, grad_mixed, gate):
     rounded = probs.astype(jnp.bfloat16)
     result = contract(rounded, value, 0, 0).astype(jnp.bfloat16)
     part = jnp.sum(grad_mixed * result.astype(jnp.float32), axis=0, keepdims=True)
-    grad_value = contract(rounded, incoming, 1, 0)
-    grad_probs = contract(value, incoming, 1, 1)
+    return result, contract(rounded, (gate * grad_mixed).astype(jnp.bfloat16), 1, 0), part
+
+
+def head_scores(probs, query, key, value, grad_mixed, gate):
+    grad_probs = contract(value, (gate * grad_mixed).astype(jnp.bfloat16), 1, 1)
     inner = jnp.sum(probs * grad_probs, axis=0, keepdims=True)
-    grad_scores = (probs * (grad_probs - inner) * scale).astype(jnp.bfloat16)
-    grad_query = contract(grad_scores, key, 0, 0)
-    grad_key = contract(grad_scores, query, 1, 0)
+    grad_scores = (probs * (grad_probs - inner) * HEAD ** (-0.5)).astype(jnp.bfloat16)
+    return contract(grad_scores, key, 0, 0), contract(grad_scores, query, 1, 0)
+
+
+def head_gradients(query, key, value, grad_mixed, gate, keep):
+    probs = head_probs(query, key, keep)
+    result, grad_value, part = head_values(probs, value, grad_mixed, gate)
+    grad_query, grad_key = head_scores(probs, query, key, value, grad_mixed, gate)
     return result, grad_query, grad_key, grad_value, part
 
 
-def time_kernel(count_ref, moved_ref, mixed_ref, gate_ref, out_ref, grad_ref, part_ref):
+def time_heads(count_ref, moved_ref, mixed_ref, gate_ref):
     frames, _, near, channels = moved_ref.shape
     tokens = frames * near
     key_at = lax.broadcasted_iota(jnp.int32, (tokens, tokens), 0)
@@ -51,20 +61,32 @@
     keep = (key_at % near == query_at % near) & (key_at < count_ref[0] * near)
     for head in range(channels // HEAD):
         lanes = slice(head * HEAD, (head + 1) * HEAD)
-
-        def load(which):
-            wide = moved_ref[:, which, :, lanes].astype(jnp.float32)
-            return wide.reshape(tokens, HEAD).astype(jnp.bfloat16)
-
-        result, grad_query, grad_key, grad_value, part = head_gradients(
-            load(0), load(1), load(2), mixed_ref[:, lanes], gate_ref[:, lanes], keep
-        )
+        arrays = [
+            moved_ref[:, which, :, lanes].astype(jnp.float32).reshape(tokens, HEAD).astype(jnp.bfloat16)
+            for which in range(3)
+        ]
+        probs = head_probs(arrays[0], arrays[1], keep)
+        yield lanes, probs, arrays, mixed_ref[:, lanes], gate_ref[:, lanes]
+
+
+def put_by_frame(target, which, lanes, array):
+    frames, _, near, _ = target.shape
+    wide = array.astype(jnp.float32).reshape(frames, near, HEAD)
+    target[:, which, :, lanes] = wide.astype(jnp.bfloat16)
+
+
+def time_values_kernel(count_ref, moved_ref, mixed_ref, gate_ref, out_ref, part_ref):
+    for lanes, probs, arrays, mixed, gate in time_heads(count_ref, moved_ref, mixed_ref, gate_ref):
+        result, grad_value, part = head_values(probs, arrays[2], mixed, gate)
         part_ref[:, lanes] = part
-        for target, which, array in (
-            (out_ref, 0, result), (out_ref, 1, grad_query), (grad_ref, 0, grad_key), (grad_ref, 1, grad_value),
-        ):
-            wide = array.astype(jnp.float32).reshape(frames, near, HEAD)
-            target[:, which, :, lanes] = wide.astype(jnp.bfloat16)
+        put_by_frame(out_ref, 0, lanes, result)
+        put_by_frame(out_ref, 1, lanes, grad_value)
+
+
+def time_scores_kernel(count_ref, moved_ref, mixed_ref, gate_ref, out_ref):
+    for lanes, probs, arrays, mixed, gate in time_heads(count_ref, moved_ref, mixed_ref, gate_ref):
+        for which, array in enumerate(head_scores(probs, *arrays, mixed, gate)):
+            put_by_frame(out_ref, which, lanes, array)
 
 
 def space_kernel(
@@ -98,17 +120,18 @@
     )
 
 
-def time_attention(count, moved, grad_mixed, gate):
+def time_attention(kernel, name, terms, count, moved, grad_mixed, gate):
     frames, _, near, channels = moved.shape
-    pair = jax.ShapeDtypeStruct((frames, 2, near, channels), jnp.bfloat16)
+    shapes = (jax.ShapeDtypeStruct((frames, 2, near, channels), jnp.bfloat16),)
+    shapes += (jax.ShapeDtypeStruct((1, channels), jnp.float32),) * terms
     return pl.pallas_call(
-        time_kernel,
-        out_shape=(pair, pair, jax.ShapeDtypeStruct((1, channels), jnp.float32)),
+        kernel,
+        out_shape=shapes,
         in_specs=[pl.BlockSpec(memory_space=pltpu.SMEM)] + in_vmem(3),
-        out_specs=tuple(in_vmem(3)),
+        out_specs=tuple(in_vmem(len(shapes))),
         cost_estimate=attention_cost(frames * near, channels),
         compiler_params=pltpu.CompilerParams(vmem_limit_bytes=VMEM_BYTES),
-        name="time_attention",
+        name=name,
     )(count, moved, grad_mixed, gate)
 
 
@@ -167,7 +190,7 @@
         ],
         out_specs=(columns,) * 2,
         scratch_shapes=[pltpu.VMEM((tokens, channels), jnp.bfloat16)],
-        compiler_params=pltpu.CompilerParams(vmem_limit_bytes=VMEM_BYTES),
+        compiler_params=pltpu.CompilerParams(vmem_limit_bytes=STREAMING_BYTES),
         cost_estimate=pl.CostEstimate(flops=OUTPUT_FLOPS, bytes_accessed=0, transcendentals=0),
         name="output",
     )(returned, returned, space, grad, gate_space, gate_time, weight)
@@ -282,7 +305,7 @@
     terms = list(lax.all_gather(total, ("x", "core"), axis=0, tiled=True))
     while len(terms) > 1:
         terms = [left + right for left, right in zip(terms[::2], terms[1::2])]
-    return terms[0]
+    return all_sum(terms[0][None], "fsdp")[0]
 
 
 def on_device(
@@ -324,19 +347,22 @@
     )
     moved, part_space = lax.optimization_barrier((moved, part_space))
     there = project(moved[:, 3].reshape(positions, channels))
-    early, late, part_time = time_attention(frame_count, moved, there, gate_time)
+    early, part_time = time_attention(
+        time_values_kernel, "time_attention", 1, frame_count, moved, there, gate_time
+    )
+    (late,) = time_attention(time_scores_kernel, "time_scores", 0, frame_count, moved, there, gate_time)
     early = exchange(early)
 
     parts = jnp.concatenate([part_space, part_time], axis=1)
-    parts = all_sum(all_sum(parts, ("x", "core")), "fsdp")
+    parts = all_sum(parts, ("x", "core"))
     early, late, _ = lax.optimization_barrier((early, late, parts))
     parts = frame_pair(parts)
     late = exchange(late)
     tokens = lax.axis_size("x") * lax.axis_size("core") * lax.axis_size("fsdp") * owners * frames_here * positions
     totals = group_sum(parts) / math.sqrt(tokens)
 
-    results = output(early, space, grad_query, gate_space, gate_time, weight)
-    results += add_returned(late, grad_key, grad_value)
+    results = output(early, space, grad_value, gate_space, gate_time, weight)
+    results = (results[0], *add_returned(late, grad_query, grad_key), results[1])
     shaped = tuple(array.reshape(query_states.shape) for array in results)
     return shaped + (totals[:channels], totals[channels:])
 

time: 205 us -> 204 us (level)
  Pallas kernels: 11 us -> 17.8 us
  waiting for transfers between devices: 46.8 us -> 42.5 us
  local copies, waits for them, and re-layouts: 9.64 us -> 6.07 us
    all_to_all x3, waiting for transfers between devices: 28 us -> 23.7 us  [exchange(): return lax.all_to_all(array, 'seq', split_axis=0, concat_axis=0, tiled=True)]
    pallas_call x1 -> x2, Pallas kernels: 2.52 us -> 6.4 us  [time_attention(): pl.pallas_call(kernel, out_shape=shapes, in_specs=[pl.BlockSpec(memory_sp...]
    unnamed x28 -> x30, local copies, waits for them, and re-layouts: 6.61 us -> 3.08 us
    pallas_call x1, Pallas kernels: 3.51 us -> 6.42 us  [output(): pl.pallas_call(output_kernel, grid=(channels // block,), out_shape=(jax.S...]
  transfers between devices with their start and end apart: 19 -> 19, of which waited for: 8 -> 8; matrix products, arithmetic and copies ran while one was open for 4% -> 4% of each run, Pallas kernels for 3% -> 7%
where the time goes in v5:
time: 204 us; the launch traced here: 203 us
  starting transfers between devices  87.4 us (43%)
  waiting for transfers between devices  42.5 us (21%)
  blocking collectives  37.9 us (19%)
  Pallas kernels  17.8 us (9%)
  local copies, waits for them, and re-layouts  6.07 us (3%)
  matrix products  5.57 us (3%)
  other arithmetic  3.3 us (2%)
  between operations  2.51 us (1%)
    ppermute x12, starting transfers between devices, shift(): lax.ppermute(array, axis, [(i, (i + by) % size) for i in range(size)])  32.7 us
    all_to_all x3, starting transfers between devices, exchange(): return lax.all_to_all(array, 'seq', split_axis=0, concat_axis=0, tiled=True)  29.4 us
    all_gather x2, blocking collectives, all_sum(): lax.all_gather(array, axis, axis=0, tiled=True)  25.2 us
    all_to_all x3, waiting for transfers between devices, exchange(): return lax.all_to_all(array, 'seq', split_axis=0, concat_axis=0, tiled=True)  23.7 us
    ppermute x12, waiting for transfers between devices, shift(): lax.ppermute(array, axis, [(i, (i + by) % size) for i in range(size)])  18.8 us
    ppermute x2, starting transfers between devices, fetch_rows(): fetched.append(lax.ppermute(out_weight, ('x', 'core', 'seq'), pairs))  14.2 us
    all_gather x1, blocking collectives, group_sum(): terms = list(lax.all_gather(total, ('x', 'core'), axis=0, tiled=True))  12.7 us
    ppermute x2, starting transfers between devices, frame_pair(): fetched.append(lax.ppermute(array, ('x', 'core', 'seq'), pairs))  11.1 us
  transfers between devices with their start and end apart: 19, of which 8 were waited for; matrix products, arithmetic and copies ran while one was open for 4% of the time, Pallas kernels for 7%

profile of v5, /device:TPU:6, one launch (start us, length us, event | category | flops | bytes accessed | tf_op | source)
XLA Modules:
  0.0 203.0 jit_solution(14221974309092573358)
XLA Ops:
  0.6 12.3 %collective-permute-start = (bf16[24,1536]{1,0:T(8,128)(2,1)}, bf16[24,1536]{1,0:T(8,128)(2,1)S(1)}, u32[]{:S(2)}, u32[]{:S(2)}) collective-permute-start(bf16[24,1536]{1,0:T(8,128)(2,1)} %param.13), channel_id=1, source_target_pairs={{68,64},{69,65},{70,66},{71,67},{72,68},{73,69},{74,70},{75,71},{7... | collective-permute-start | bytes 221192 | tf_op jit(solution)/shard_map/ppermute | solution.py:241
  12.9 1.9 collective-permute-start.1
  14.9 2.8 %pad_maximum_fusion = bf16[16,4,8,1536]{3,2,1,0:T(8,128)(2,1)} fusion(bf16[16,1,8,1536]{3,2,1,0:T(8,128)(2,1)} %bitcast.92, bf16[16,1,8,1536]{3,2,1,0:T(8,128)(2,1)} %bitcast.86, bf16[16,1,8,1536]{3,2,1,0:T(8,128)(2,1)} %bitcast.88, bf16[16,1,8,1536]{3,2,1,0:T(8,128)(2,1)} %bitcast.90), kind=kLoop, calls=%fused_computation.1 | loop fusion | flops 2359296 | bytes 3145728 | tf_op jit(solution)/shard_map/stack | solution.py:335
  17.6 9.5 %all-to-all-start = ((bf16[16,4,8,1536]{3,2,1,0:T(8,128)(2,1)}), bf16[16,4,8,1536]{3,2,1,0:T(8,128)(2,1)S(1)}, u32[]{:S(2)}, u32[]{:S(2)}) async-start(bf16[16,4,8,1536]{3,2,1,0:T(8,128)(2,1)} %pad_maximum_fusion), calls=%async_computation | async-start | bytes 3145728 | tf_op jit(solution)/shard_map/all_to_all | solution.py:332
  27.3 5.1 %collective-permute-start.3 = (bf16[2,24,1536]{2,1,0:T(8,128)(2,1)S(1)}, bf16[2,24,1536]{2,1,0:T(8,128)(2,1)S(1)}, u32[]{:S(2)}, u32[]{:S(2)}) collective-permute-start(bf16[2,24,1536]{2,1,0:T(8,128)(2,1)S(1)} %get-tuple-element.37), channel_id=1, source_target_pairs={{0,32},{16,48},{32,0},{48,16},{1,33},{17,49},{33,1},{49,17},{2,34}... | collective-permute-start | bytes 442376 | tf_op jit(solution)/shard_map/ppermute | solution.py:221
  32.4 3.0 %collective-permute-start.2 = (bf16[2,24,1536]{2,1,0:T(8,128)(2,1)S(1)}, bf16[2,24,1536]{2,1,0:T(8,128)(2,1)S(1)}, u32[]{:S(2)}, u32[]{:S(2)}) collective-permute-start(bf16[2,24,1536]{2,1,0:T(8,128)(2,1)S(1)} %get-tuple-element.37), channel_id=1, source_target_pairs={{0,48},{16,0},{32,16},{48,32},{1,49},{17,1},{33,17},{49,33},{2,50}... | collective-permute-start | bytes 442376 | tf_op jit(solution)/shard_map/ppermute | solution.py:221
  35.4 2.9 %collective-permute-start.4 = (bf16[2,24,1536]{2,1,0:T(8,128)(2,1)S(1)}, bf16[2,24,1536]{2,1,0:T(8,128)(2,1)S(1)}, u32[]{:S(2)}, u32[]{:S(2)}) collective-permute-start(bf16[2,24,1536]{2,1,0:T(8,128)(2,1)S(1)} %get-tuple-element.37), channel_id=1, source_target_pairs={{0,16},{16,32},{32,48},{48,0},{1,17},{17,33},{33,49},{49,1},{2,18}... | collective-permute-start | bytes 442376 | tf_op jit(solution)/shard_map/ppermute | solution.py:221
  38.3 2.4 %collective-permute-done.2 = bf16[2,24,1536]{2,1,0:T(8,128)(2,1)S(1)} collective-permute-done((bf16[2,24,1536]{2,1,0:T(8,128)(2,1)S(1)}, bf16[2,24,1536]{2,1,0:T(8,128)(2,1)S(1)}, u32[]{:S(2)}, u32[]{:S(2)}) %collective-permute-start.2) | collective-permute-done | bytes 147488 | tf_op jit(solution)/shard_map/ppermute | solution.py:221
  40.7 4.4 %collective-permute-done.4 = bf16[2,24,1536]{2,1,0:T(8,128)(2,1)S(1)} collective-permute-done((bf16[2,24,1536]{2,1,0:T(8,128)(2,1)S(1)}, bf16[2,24,1536]{2,1,0:T(8,128)(2,1)S(1)}, u32[]{:S(2)}, u32[]{:S(2)}) %collective-permute-start.4) | collective-permute-done | bytes 147488 | tf_op jit(solution)/shard_map/ppermute | solution.py:221
  45.1 1.9 collective-permute-start.8
  47.0 3.9 %collective-permute-start.6 = (bf16[4,2,24,1536]{3,2,1,0:T(8,128)(2,1)S(1)}, bf16[4,2,24,1536]{3,2,1,0:T(8,128)(2,1)S(1)}, u32[]{:S(2)}, u32[]{:S(2)}) collective-permute-start(bf16[4,2,24,1536]{3,2,1,0:T(8,128)(2,1)S(1)} %pad_maximum_fusion.1.refs_0_), channel_id=1, source_target_pairs={{0,384},{128,0},{256,128},{384,256},{1,385},{129,1},{257,129},{385... | collective-permute-start | bytes 1769480 | tf_op jit(solution)/shard_map/ppermute | solution.py:221
  51.1 1.9 collective-permute-start.5
  53.0 9.5 %collective-permute-done.8.refs_8_ = bf16[4,2,24,1536]{3,2,1,0:T(8,128)(2,1)S(1)} collective-permute-done((bf16[4,2,24,1536]{3,2,1,0:T(8,128)(2,1)S(1)}, bf16[4,2,24,1536]{3,2,1,0:T(8,128)(2,1)S(1)}, u32[]{:S(2)}, u32[]{:S(2)}) %collective-permute-start.8) | collective-permute-done | bytes 589856 | tf_op jit(solution)/shard_map/ppermute | solution.py:221
  62.5 0.7 slice.28
  63.3 3.4 %collective-permute-start.9 = (bf16[2,2,24,1536]{3,2,1,0:T(8,128)(2,1)}, bf16[2,2,24,1536]{3,2,1,0:T(8,128)(2,1)}, u32[]{:S(2)}, u32[]{:S(2)}) collective-permute-start(bf16[2,2,24,1536]{3,2,1,0:T(8,128)(2,1)} %slice.28), channel_id=1, source_target_pairs={{0,128},{128,256},{256,384},{384,0},{1,129},{129,257},{257,385},{3... | collective-permute-start | bytes 884744 | tf_op jit(solution)/shard_map/ppermute | solution.py:221
  66.7 0.7 slice.29
  67.4 2.4 %collective-permute-start.11 = (bf16[2,2,24,1536]{3,2,1,0:T(8,128)(2,1)}, bf16[2,2,24,1536]{3,2,1,0:T(8,128)(2,1)}, u32[]{:S(2)}, u32[]{:S(2)}) collective-permute-start(bf16[2,2,24,1536]{3,2,1,0:T(8,128)(2,1)} %slice.29), channel_id=1, source_target_pairs={{0,384},{128,0},{256,128},{384,256},{1,385},{129,1},{257,129},{385... | collective-permute-start | bytes 884744 | tf_op jit(solution)/shard_map/ppermute | solution.py:221
  69.8 1.9 collective-permute-start.13
  71.8 2.4 %collective-permute-start.7 = (bf16[4,2,24,1536]{3,2,1,0:T(8,128)(2,1)S(1)}, bf16[4,2,24,1536]{3,2,1,0:T(8,128)(2,1)}, u32[]{:S(2)}, u32[]{:S(2)}) collective-permute-start(bf16[4,2,24,1536]{3,2,1,0:T(8,128)(2,1)S(1)} %collective-permute-done.6.refs_2_), channel_id=1, source_target_pairs={{0,64},{64,0},{1,65},{65,1},{2,66},{66,2},{3,67},{67,3},{4,68},{68... | collective-permute-start | bytes 1769480 | tf_op jit(solution)/shard_map/ppermute | solution.py:221
  76.0 1.9 collective-permute-start.10
  77.9 1.3 collective-permute-done.11.refs_6_
  79.2 1.9 collective-permute-start.12
  81.2 0.1 add.605
  81.3 0.1 add.547
  81.9 1.2 collective-permute-done.12.refs_7_
  83.0 2.1 %weight_in_place.1 = bf16[64,24,1536]{2,1,0:T(8,128)(2,1)S(1)} custom-call(s32[64]{0:T(128)S(1)} %concatenate.6.place_ref, bf16[4,2,24,1536]{3,2,1,0:T(8,128)(2,1)S(1)} %pad_maximum_fusion.1.refs_0_, bf16[4,2,24,1536]{3,2,1,0:T(8,128)(2,1)} %collective-permute-done.5.refs_1_, bf16[4,2,24,1536]{3,2,1,0:T(8,128)(2,1)S(1)} %collective-permute-done.6.refs_2_, ...), custom_call_target="tpu_custom_call" | custom-call | flops 36800000000 | bytes 4718592 | tf_op jit(solution)/shard_map/weight_in_place/pallas_call | solution.py:274
  85.2 1.6 convolution_bitcast_fusion.mixed_ref
  86.8 0.5 copy-done
  87.3 1.3 space_attention.1
  88.6 0.9 copy-done.4
  89.5 0.9 copy-done.8
  90.4 0.7 copy-done.9
  91.2 7.0 %all-to-all-done.moved_ref = bf16[16,4,8,1536]{3,2,1,0:T(8,128)(2,1)S(1)} async-done(((bf16[16,4,8,1536]{3,2,1,0:T(8,128)(2,1)}), bf16[16,4,8,1536]{3,2,1,0:T(8,128)(2,1)S(1)}, u32[]{:S(2)}, u32[]{:S(2)}) %all-to-all-start) | async-done | bytes 1572896 | tf_op jit(solution)/shard_map/all_to_all | solution.py:332
  98.2 4.0 %fusion.mixed_ref = f32[128,1536]{1,0:T(8,128)S(1)} fusion(bf16[1536,1536]{1,0:T(8,128)(2,1)} %bitcast.84, bf16[16,4,8,1536]{3,2,1,0:T(8,128)(2,1)S(1)} %all-to-all-done.moved_ref), kind=kOutput, calls=%fused_computation.3 | convolution fusion | flops 603979776 | bytes 5898240 | tf_op jit(solution)/shard_map/td,nd->tn/dot_general | solution.py:343
  102.2 1.8 time_attention.1
  104.0 10.8 %all-to-all-start.1 = ((bf16[16,2,8,1536]{3,2,1,0:T(8,128)(2,1)}), bf16[16,2,8,1536]{3,2,1,0:T(8,128)(2,1)}, u32[]{:S(2)}, u32[]{:S(2)}) async-start(bf16[16,2,8,1536]{3,2,1,0:T(8,128)(2,1)} %get-tuple-element.23), calls=%async_computation.1 | async-start | bytes 1572864 | tf_op jit(solution)/shard_map/all_to_all | solution.py:332
  114.8 12.7 %all-gather = f32[8,1,3072]{2,1,0:T(1,128)S(1)} all-gather(f32[1,1,3072]{2,1,0:T(1,128)S(1)} %maximum_bitcast_fusion), channel_id=1, replica_groups=mesh['x'=4,'core'=2,'fsdp'=4,'seq'=16] {'x','core'}, dimensions={0}, use_global_device_ids=true | all-gather | bytes 110592 | tf_op jit(solution)/shard_map/all_gather | solution.py:287
  127.7 6.8 %collective-permute-start.15 = (f32[1,3072]{1,0:T(1,128)S(1)}, f32[1,3072]{1,0:T(1,128)S(1)}, u32[]{:S(2)}, u32[]{:S(2)}) collective-permute-start(f32[1,3072]{1,0:T(1,128)S(1)} %bitcast.97), channel_id=1, source_target_pairs={{0,1},{1,0},{2,3},{3,2},{4,5},{5,4},{6,7},{7,6},{8,9},{9,8},{10,11... | collective-permute-start | bytes 36872 | tf_op jit(solution)/shard_map/ppermute | solution.py:299
  134.5 4.3 %collective-permute-start.14 = (f32[1,3072]{1,0:T(1,128)S(1)}, f32[1,3072]{1,0:T(1,128)S(1)}, u32[]{:S(2)}, u32[]{:S(2)}) collective-permute-start(f32[1,3072]{1,0:T(1,128)S(1)} %bitcast.98), channel_id=1, source_target_pairs={{64,66},{65,67},{66,64},{67,65},{68,70},{69,71},{70,68},{71,69},{7... | collective-permute-start | bytes 36872 | tf_op jit(solution)/shard_map/ppermute | solution.py:299
  138.7 4.6 %time_scores.1 = bf16[16,2,8,1536]{3,2,1,0:T(8,128)(2,1)} custom-call(s32[1]{0:T(128)S(6)} %copy.20.count_ref, bf16[16,4,8,1536]{3,2,1,0:T(8,128)(2,1)S(1)} %all-to-all-done.moved_ref, f32[128,1536]{1,0:T(8,128)S(1)} %fusion.mixed_ref, f32[1,1536]{1,0:T(1,128)S(1)} %reshape.294.gate_ref.gate_time_ref), custom_call_target="tpu_custom_call" | custom-call | flops 301989888 | bytes 3145728 | tf_op jit(solution)/shard_map/time_scores/pallas_call | solution.py:127
  143.3 11.0 %all-to-all-done.1.time_ref.moved_ref = bf16[16,2,8,1536]{3,2,1,0:T(8,128)(2,1)} async-done(((bf16[16,2,8,1536]{3,2,1,0:T(8,128)(2,1)}), bf16[16,2,8,1536]{3,2,1,0:T(8,128)(2,1)}, u32[]{:S(2)}, u32[]{:S(2)}) %all-to-all-start.1) | async-done | bytes 786464 | tf_op jit(solution)/shard_map/all_to_all | solution.py:332
  154.3 9.1 %all-to-all-start.2 = ((bf16[16,2,8,1536]{3,2,1,0:T(8,128)(2,1)}), bf16[16,2,8,1536]{3,2,1,0:T(8,128)(2,1)S(1)}, u32[]{:S(2)}, u32[]{:S(2)}) async-start(bf16[16,2,8,1536]{3,2,1,0:T(8,128)(2,1)} %time_scores.1), calls=%async_computation.2 | async-start | bytes 1572864 | tf_op jit(solution)/shard_map/all_to_all | solution.py:332
  163.5 12.7 %all-gather.1 = f32[8,1,3072]{2,1,0:T(1,128)S(1)} all-gather(f32[1,1,3072]{2,1,0:T(1,128)S(1)} %fusion.9), channel_id=1, replica_groups=mesh['x'=4,'core'=2,'fsdp'=4,'seq'=16] {'x','core'}, dimensions={0}, use_global_device_ids=true | all-gather | bytes 110592 | tf_op jit(solution)/shard_map/all_gather | solution.py:305
  176.3 12.4 %all-gather.2 = f32[4,1,3072]{2,1,0:T(1,128)S(1)} all-gather(f32[1,1,3072]{2,1,0:T(1,128)S(1)} %fusion.7), channel_id=1, replica_groups=mesh['x'=4,'core'=2,'fsdp'=4,'seq'=16] {'fsdp'}, dimensions={0}, use_global_device_ids=true | all-gather | bytes 61440 | tf_op jit(solution)/shard_map/all_gather | solution.py:287
  188.8 0.6 fusion.41
  189.4 6.4 %output.1 = (bf16[128,1536]{1,0:T(8,128)(2,1)}, bf16[128,1536]{1,0:T(8,128)(2,1)}) custom-call(bf16[16,2,8,1536]{3,2,1,0:T(8,128)(2,1)} %all-to-all-done.1.time_ref.moved_ref, bf16[16,2,8,1536]{3,2,1,0:T(8,128)(2,1)} %all-to-all-done.1.time_ref.moved_ref, bf16[128,1536]{1,0:T(8,128)(2,1)} %copy-done.9, f32[128,1536]{1,0:T(8,128)} %copy-done.8, ...), custom_call_target="tpu_custom_call" | custom-call | flops 16099999744 | tf_op jit(solution)/shard_map/output/pallas_call | solution.py:181
  195.8 5.6 %all-to-all-done.2.moved_ref = bf16[16,2,8,1536]{3,2,1,0:T(8,128)(2,1)S(1)} async-done(((bf16[16,2,8,1536]{3,2,1,0:T(8,128)(2,1)}), bf16[16,2,8,1536]{3,2,1,0:T(8,128)(2,1)S(1)}, u32[]{:S(2)}, u32[]{:S(2)}) %all-to-all-start.2) | async-done | bytes 786464 | tf_op jit(solution)/shard_map/all_to_all | solution.py:332
  201.4 1.6 add_returned.1
  (62 shorter events, 1.4 us)
Async XLA Ops:
  0.6 26.6 %collective-permute-start = (bf16[24,1536]{1,0:T(8,128)(2,1)}, bf16[24,1536]{1,0:T(8,128)(2,1)S(1)}, u32[]{:S(2)}, u32[]{:S(2)}) collective-permute-start(bf16[24,1536]{1,0:T(8,128)(2,1)} %param.13), channel_id=1, source_target_pairs={{68,64},{69,65},{70,66},{71,67},{72,68},{73,69},{74,70},{75,71},{7... | collective-permute-start | bytes 221192 | tf_op jit(solution)/shard_map/ppermute | solution.py:241
  12.9 14.3 %collective-permute-start.1 = (bf16[24,1536]{1,0:T(8,128)(2,1)}, bf16[24,1536]{1,0:T(8,128)(2,1)S(1)}, u32[]{:S(2)}, u32[]{:S(2)}) collective-permute-start(bf16[24,1536]{1,0:T(8,128)(2,1)} %param.13), channel_id=1, source_target_pairs={{8,0},{9,1},{10,2},{11,3},{12,4},{13,5},{14,6},{15,7},{0,8},{1,9},... | collective-permute-start | bytes 221192 | tf_op jit(solution)/shard_map/ppermute | solution.py:241
  17.6 9.6 %copy-start.11 = (bf16[24,1536]{1,0:T(8,128)(2,1)S(1)}, bf16[24,1536]{1,0:T(8,128)(2,1)}, u32[]{:S(2)}) copy-start(bf16[24,1536]{1,0:T(8,128)(2,1)} %param.13) | copy-start | bytes 221188
  17.6 80.6 %all-to-all-start = ((bf16[16,4,8,1536]{3,2,1,0:T(8,128)(2,1)}), bf16[16,4,8,1536]{3,2,1,0:T(8,128)(2,1)S(1)}, u32[]{:S(2)}, u32[]{:S(2)}) async-start(bf16[16,4,8,1536]{3,2,1,0:T(8,128)(2,1)} %pad_maximum_fusion), calls=%async_computation | async-start | bytes 3145728 | tf_op jit(solution)/shard_map/all_to_all | solution.py:332
  27.2 23.9 %copy-start.14 = (s32[4,2,2]{2,1,0:T(2,128)S(1)}, s32[4,2,2]{2,1,0:T(2,128)}, u32[]{:S(2)}) copy-start(s32[4,2,2]{2,1,0:T(2,128)} %constant.192.clone) | copy-start | bytes 196
  27.2 48.7 %copy-start.12 = (f32[1536]{0:T(1024)S(1)}, f32[1536]{0:T(1024)}, u32[]{:S(2)}) copy-start(f32[1536]{0:T(1024)} %param.15) | copy-start | bytes 18436
  27.2 48.7 %copy-start.13 = (f32[1536]{0:T(1024)S(1)}, f32[1536]{0:T(1024)}, u32[]{:S(2)}) copy-start(f32[1536]{0:T(1024)} %param.14) | copy-start | bytes 18436
  27.3 11.0 %collective-permute-start.3 = (bf16[2,24,1536]{2,1,0:T(8,128)(2,1)S(1)}, bf16[2,24,1536]{2,1,0:T(8,128)(2,1)S(1)}, u32[]{:S(2)}, u32[]{:S(2)}) collective-permute-start(bf16[2,24,1536]{2,1,0:T(8,128)(2,1)S(1)} %get-tuple-element.37), channel_id=1, source_target_pairs={{0,32},{16,48},{32,0},{48,16},{1,33},{17,49},{33,1},{49,17},{2,34}... | collective-permute-start | bytes 442376 | tf_op jit(solution)/shard_map/ppermute | solution.py:221
  32.4 8.3 %collective-permute-start.2 = (bf16[2,24,1536]{2,1,0:T(8,128)(2,1)S(1)}, bf16[2,24,1536]{2,1,0:T(8,128)(2,1)S(1)}, u32[]{:S(2)}, u32[]{:S(2)}) collective-permute-start(bf16[2,24,1536]{2,1,0:T(8,128)(2,1)S(1)} %get-tuple-element.37), channel_id=1, source_target_pairs={{0,48},{16,0},{32,16},{48,32},{1,49},{17,1},{33,17},{49,33},{2,50}... | collective-permute-start | bytes 442376 | tf_op jit(solution)/shard_map/ppermute | solution.py:221
  35.4 9.7 %collective-permute-start.4 = (bf16[2,24,1536]{2,1,0:T(8,128)(2,1)S(1)}, bf16[2,24,1536]{2,1,0:T(8,128)(2,1)S(1)}, u32[]{:S(2)}, u32[]{:S(2)}) collective-permute-start(bf16[2,24,1536]{2,1,0:T(8,128)(2,1)S(1)} %get-tuple-element.37), channel_id=1, source_target_pairs={{0,16},{16,32},{32,48},{48,0},{1,17},{17,33},{33,49},{49,1},{2,18}... | collective-permute-start | bytes 442376 | tf_op jit(solution)/shard_map/ppermute | solution.py:221
  45.1 17.4 %collective-permute-start.8 = (bf16[4,2,24,1536]{3,2,1,0:T(8,128)(2,1)S(1)}, bf16[4,2,24,1536]{3,2,1,0:T(8,128)(2,1)S(1)}, u32[]{:S(2)}, u32[]{:S(2)}) collective-permute-start(bf16[4,2,24,1536]{3,2,1,0:T(8,128)(2,1)S(1)} %pad_maximum_fusion.1.refs_0_), channel_id=1, source_target_pairs={{0,128},{128,256},{256,384},{384,0},{1,129},{129,257},{257,385},{3... | collective-permute-start | bytes 1769480 | tf_op jit(solution)/shard_map/ppermute | solution.py:221
  47.0 19.6 %collective-permute-start.6 = (bf16[4,2,24,1536]{3,2,1,0:T(8,128)(2,1)S(1)}, bf16[4,2,24,1536]{3,2,1,0:T(8,128)(2,1)S(1)}, u32[]{:S(2)}, u32[]{:S(2)}) collective-permute-start(bf16[4,2,24,1536]{3,2,1,0:T(8,128)(2,1)S(1)} %pad_maximum_fusion.1.refs_0_), channel_id=1, source_target_pairs={{0,384},{128,0},{256,128},{384,256},{1,385},{129,1},{257,129},{385... | collective-permute-start | bytes 1769480 | tf_op jit(solution)/shard_map/ppermute | solution.py:221
  51.1 30.7 %collective-permute-start.5 = (bf16[4,2,24,1536]{3,2,1,0:T(8,128)(2,1)S(1)}, bf16[4,2,24,1536]{3,2,1,0:T(8,128)(2,1)}, u32[]{:S(2)}, u32[]{:S(2)}) collective-permute-start(bf16[4,2,24,1536]{3,2,1,0:T(8,128)(2,1)S(1)} %pad_maximum_fusion.1.refs_0_), channel_id=1, source_target_pairs={{0,64},{64,0},{1,65},{65,1},{2,66},{66,2},{3,67},{67,3},{4,68},{68... | collective-permute-start | bytes 1769480 | tf_op jit(solution)/shard_map/ppermute | solution.py:221
  63.3 12.7 %collective-permute-start.9 = (bf16[2,2,24,1536]{3,2,1,0:T(8,128)(2,1)}, bf16[2,2,24,1536]{3,2,1,0:T(8,128)(2,1)}, u32[]{:S(2)}, u32[]{:S(2)}) collective-permute-start(bf16[2,2,24,1536]{3,2,1,0:T(8,128)(2,1)} %slice.28), channel_id=1, source_target_pairs={{0,128},{128,256},{256,384},{384,0},{1,129},{129,257},{257,385},{3... | collective-permute-start | bytes 884744 | tf_op jit(solution)/shard_map/ppermute | solution.py:221
  67.4 11.8 %collective-permute-start.11 = (bf16[2,2,24,1536]{3,2,1,0:T(8,128)(2,1)}, bf16[2,2,24,1536]{3,2,1,0:T(8,128)(2,1)}, u32[]{:S(2)}, u32[]{:S(2)}) collective-permute-start(bf16[2,2,24,1536]{3,2,1,0:T(8,128)(2,1)} %slice.29), channel_id=1, source_target_pairs={{0,384},{128,0},{256,128},{384,256},{1,385},{129,1},{257,129},{385... | collective-permute-start | bytes 884744 | tf_op jit(solution)/shard_map/ppermute | solution.py:221
  69.8 12.0 %collective-permute-start.13 = (bf16[4,2,24,1536]{3,2,1,0:T(8,128)(2,1)S(1)}, bf16[4,2,24,1536]{3,2,1,0:T(8,128)(2,1)}, u32[]{:S(2)}, u32[]{:S(2)}) collective-permute-start(bf16[4,2,24,1536]{3,2,1,0:T(8,128)(2,1)S(1)} %collective-permute-done.8.refs_8_), channel_id=1, source_target_pairs={{0,64},{64,0},{1,65},{65,1},{2,66},{66,2},{3,67},{67,3},{4,68},{68... | collective-permute-start | bytes 1769480 | tf_op jit(solution)/shard_map/ppermute | solution.py:221
  71.8 11.3 %collective-permute-start.7 = (bf16[4,2,24,1536]{3,2,1,0:T(8,128)(2,1)S(1)}, bf16[4,2,24,1536]{3,2,1,0:T(8,128)(2,1)}, u32[]{:S(2)}, u32[]{:S(2)}) collective-permute-start(bf16[4,2,24,1536]{3,2,1,0:T(8,128)(2,1)S(1)} %collective-permute-done.6.refs_2_), channel_id=1, source_target_pairs={{0,64},{64,0},{1,65},{65,1},{2,66},{66,2},{3,67},{67,3},{4,68},{68... | collective-permute-start | bytes 1769480 | tf_op jit(solution)/shard_map/ppermute | solution.py:221
  75.9 62.8 %copy-start.6 = (f32[1,1536]{1,0:T(1,128)}, f32[1,1536]{1,0:T(1,128)S(1)}, u32[]{:S(2)}) copy-start(f32[1,1536]{1,0:T(1,128)S(1)} %reshape.294.gate_ref.gate_time_ref) | copy-start | bytes 18436
  75.9 11.4 %copy-start.7 = (f32[1,1536]{1,0:T(1,128)}, f32[1,1536]{1,0:T(1,128)S(1)}, u32[]{:S(2)}) copy-start(f32[1,1536]{1,0:T(1,128)S(1)} %reshape.293.gate_ref.gate_space_ref) | copy-start | bytes 18436
  76.0 5.9 %collective-permute-start.10 = (bf16[2,2,24,1536]{3,2,1,0:T(8,128)(2,1)}, bf16[2,2,24,1536]{3,2,1,0:T(8,128)(2,1)}, u32[]{:S(2)}, u32[]{:S(2)}) collective-permute-start(bf16[2,2,24,1536]{3,2,1,0:T(8,128)(2,1)} %collective-permute-done.9.refs_4_), channel_id=1, source_target_pairs={{0,64},{64,0},{1,65},{65,1},{2,66},{66,2},{3,67},{67,3},{4,68},{68... | collective-permute-start | bytes 884744 | tf_op jit(solution)/shard_map/ppermute | solution.py:221
  79.2 3.8 %collective-permute-start.12 = (bf16[2,2,24,1536]{3,2,1,0:T(8,128)(2,1)}, bf16[2,2,24,1536]{3,2,1,0:T(8,128)(2,1)}, u32[]{:S(2)}, u32[]{:S(2)}) collective-permute-start(bf16[2,2,24,1536]{3,2,1,0:T(8,128)(2,1)} %collective-permute-done.11.refs_6_), channel_id=1, source_target_pairs={{0,64},{64,0},{1,65},{65,1},{2,66},{66,2},{3,67},{67,3},{4,68},{68... | collective-permute-start | bytes 884744 | tf_op jit(solution)/shard_map/ppermute | solution.py:221
  81.8 3.3 %copy-start.10 = (bf16[1,1,128,1536]{3,2,1,0:T(8,128)(2,1)S(1)}, bf16[1,1,128,1536]{3,2,1,0:T(8,128)(2,1)}, u32[]{:S(2)}) copy-start(bf16[1,1,128,1536]{3,2,1,0:T(8,128)(2,1)} %param.16) | copy-start | bytes 1179652
  85.1 2.1 %copy-start = (bf16[64,24,1536]{2,1,0:T(8,128)(2,1)}, bf16[64,24,1536]{2,1,0:T(8,128)(2,1)S(1)}, u32[]{:S(2)}) copy-start(bf16[64,24,1536]{2,1,0:T(8,128)(2,1)S(1)} %weight_in_place.1) | copy-start | bytes 14155780
  85.2 2.1 %copy-start.1 = (bf16[1,1,128,1536]{3,2,1,0:T(8,128)(2,1)S(1)}, bf16[1,1,128,1536]{3,2,1,0:T(8,128)(2,1)}, u32[]{:S(2)}) copy-start(bf16[1,1,128,1536]{3,2,1,0:T(8,128)(2,1)} %param.12) | copy-start | bytes 1179652
  85.2 2.1 %copy-start.2 = (bf16[1,1,128,1536]{3,2,1,0:T(8,128)(2,1)S(1)}, bf16[1,1,128,1536]{3,2,1,0:T(8,128)(2,1)}, u32[]{:S(2)}) copy-start(bf16[1,1,128,1536]{3,2,1,0:T(8,128)(2,1)} %param.11) | copy-start | bytes 1179652
  85.2 2.1 %copy-start.3 = (bf16[1,1,128,1536]{3,2,1,0:T(8,128)(2,1)S(1)}, bf16[1,1,128,1536]{3,2,1,0:T(8,128)(2,1)}, u32[]{:S(2)}) copy-start(bf16[1,1,128,1536]{3,2,1,0:T(8,128)(2,1)} %param.10) | copy-start | bytes 1179652
  88.6 0.9 copy-start.4
  89.5 0.9 copy-start.8
  90.4 0.7 copy-start.9
  104.0 50.4 %all-to-all-start.1 = ((bf16[16,2,8,1536]{3,2,1,0:T(8,128)(2,1)}), bf16[16,2,8,1536]{3,2,1,0:T(8,128)(2,1)}, u32[]{:S(2)}, u32[]{:S(2)}) async-start(bf16[16,2,8,1536]{3,2,1,0:T(8,128)(2,1)} %get-tuple-element.23), calls=%async_computation.1 | async-start | bytes 1572864 | tf_op jit(solution)/shard_map/all_to_all | solution.py:332
  127.7 35.8 %collective-permute-start.15 = (f32[1,3072]{1,0:T(1,128)S(1)}, f32[1,3072]{1,0:T(1,128)S(1)}, u32[]{:S(2)}, u32[]{:S(2)}) collective-permute-start(f32[1,3072]{1,0:T(1,128)S(1)} %bitcast.97), channel_id=1, source_target_pairs={{0,1},{1,0},{2,3},{3,2},{4,5},{5,4},{6,7},{7,6},{8,9},{9,8},{10,11... | collective-permute-start | bytes 36872 | tf_op jit(solution)/shard_map/ppermute | solution.py:299
  134.5 29.0 %collective-permute-start.14 = (f32[1,3072]{1,0:T(1,128)S(1)}, f32[1,3072]{1,0:T(1,128)S(1)}, u32[]{:S(2)}, u32[]{:S(2)}) collective-permute-start(f32[1,3072]{1,0:T(1,128)S(1)} %bitcast.98), channel_id=1, source_target_pairs={{64,66},{65,67},{66,64},{67,65},{68,70},{69,71},{70,68},{71,69},{7... | collective-permute-start | bytes 36872 | tf_op jit(solution)/shard_map/ppermute | solution.py:299
  154.3 47.1 %all-to-all-start.2 = ((bf16[16,2,8,1536]{3,2,1,0:T(8,128)(2,1)}), bf16[16,2,8,1536]{3,2,1,0:T(8,128)(2,1)S(1)}, u32[]{:S(2)}, u32[]{:S(2)}) async-start(bf16[16,2,8,1536]{3,2,1,0:T(8,128)(2,1)} %time_scores.1), calls=%async_computation.2 | async-start | bytes 1572864 | tf_op jit(solution)/shard_map/all_to_all | solution.py:332
  189.4 12.0 %copy-start.5 = (f32[128,1536]{1,0:T(8,128)S(1)}, f32[128,1536]{1,0:T(8,128)}, u32[]{:S(2)}) copy-start(f32[128,1536]{1,0:T(8,128)} %copy-done.4) | copy-start | bytes 2359300

commit v6 on v5

--- a/solution.py
+++ b/solution.py
@@ -172,7 +172,7 @@
     out_grad_ref[...] = combine(grad_ref[...], moved_ref[...])
 
 
-def output(returned, space, grad, gate_space, gate_time, weight, block=256):
+def output(returned, space, grad, gate_space, gate_time, weight, block=512):
     owners, _, near, channels = returned.shape
     tokens = owners * near
     whole = pl.BlockSpec((tokens, channels), lambda j: (0, 0))

time: 204 us -> 204 us (level)
  transfers between devices with their start and end apart: 19 -> 19, of which waited for: 8 -> 8; matrix products, arithmetic and copies ran while one was open for 4% -> 4% of each run, Pallas kernels for 7% -> 6%
where the time goes in v6:
time: 204 us; the launch traced here: 203 us
  starting transfers between devices  87.4 us (43%)
  waiting for transfers between devices  43.7 us (21%)
  blocking collectives  37.9 us (19%)
  Pallas kernels  16.5 us (8%)
  local copies, waits for them, and re-layouts  6.07 us (3%)
  matrix products  5.57 us (3%)
  other arithmetic  3.3 us (2%)
  between operations  2.51 us (1%)
    ppermute x12, starting transfers between devices, shift(): lax.ppermute(array, axis, [(i, (i + by) % size) for i in range(size)])  32.7 us
    all_to_all x3, starting transfers between devices, exchange(): return lax.all_to_all(array, 'seq', split_axis=0, concat_axis=0, tiled=True)  29.4 us
    all_gather x2, blocking collectives, all_sum(): lax.all_gather(array, axis, axis=0, tiled=True)  25.2 us
    all_to_all x3, waiting for transfers between devices, exchange(): return lax.all_to_all(array, 'seq', split_axis=0, concat_axis=0, tiled=True)  24.9 us
    ppermute x12, waiting for transfers between devices, shift(): lax.ppermute(array, axis, [(i, (i + by) % size) for i in range(size)])  18.8 us
    ppermute x2, starting transfers between devices, fetch_rows(): fetched.append(lax.ppermute(out_weight, ('x', 'core', 'seq'), pairs))  14.2 us
    all_gather x1, blocking collectives, group_sum(): terms = list(lax.all_gather(total, ('x', 'core'), axis=0, tiled=True))  12.7 us
    ppermute x2, starting transfers between devices, frame_pair(): fetched.append(lax.ppermute(array, ('x', 'core', 'seq'), pairs))  11.1 us
  transfers between devices with their start and end apart: 19, of which 8 were waited for; matrix products, arithmetic and copies ran while one was open for 4% of the time, Pallas kernels for 6%

profile of v6, /device:TPU:6, one launch (start us, length us, event | category | flops | bytes accessed | tf_op | source)
XLA Modules:
  0.0 203.0 jit_solution(15720232754774168016)
XLA Ops:
  0.6 12.3 %collective-permute-start = (bf16[24,1536]{1,0:T(8,128)(2,1)}, bf16[24,1536]{1,0:T(8,128)(2,1)S(1)}, u32[]{:S(2)}, u32[]{:S(2)}) collective-permute-start(bf16[24,1536]{1,0:T(8,128)(2,1)} %param.13), channel_id=1, source_target_pairs={{68,64},{69,65},{70,66},{71,67},{72,68},{73,69},{74,70},{75,71},{7... | collective-permute-start | bytes 221192 | tf_op jit(solution)/shard_map/ppermute | solution.py:241
  12.9 1.9 collective-permute-start.1
  14.9 2.8 %pad_maximum_fusion = bf16[16,4,8,1536]{3,2,1,0:T(8,128)(2,1)} fusion(bf16[16,1,8,1536]{3,2,1,0:T(8,128)(2,1)} %bitcast.92, bf16[16,1,8,1536]{3,2,1,0:T(8,128)(2,1)} %bitcast.86, bf16[16,1,8,1536]{3,2,1,0:T(8,128)(2,1)} %bitcast.88, bf16[16,1,8,1536]{3,2,1,0:T(8,128)(2,1)} %bitcast.90), kind=kLoop, calls=%fused_computation.1 | loop fusion | flops 2359296 | bytes 3145728 | tf_op jit(solution)/shard_map/stack | solution.py:335
  17.6 9.5 %all-to-all-start = ((bf16[16,4,8,1536]{3,2,1,0:T(8,128)(2,1)}), bf16[16,4,8,1536]{3,2,1,0:T(8,128)(2,1)S(1)}, u32[]{:S(2)}, u32[]{:S(2)}) async-start(bf16[16,4,8,1536]{3,2,1,0:T(8,128)(2,1)} %pad_maximum_fusion), calls=%async_computation | async-start | bytes 3145728 | tf_op jit(solution)/shard_map/all_to_all | solution.py:332
  27.3 5.1 %collective-permute-start.3 = (bf16[2,24,1536]{2,1,0:T(8,128)(2,1)S(1)}, bf16[2,24,1536]{2,1,0:T(8,128)(2,1)S(1)}, u32[]{:S(2)}, u32[]{:S(2)}) collective-permute-start(bf16[2,24,1536]{2,1,0:T(8,128)(2,1)S(1)} %get-tuple-element.37), channel_id=1, source_target_pairs={{0,32},{16,48},{32,0},{48,16},{1,33},{17,49},{33,1},{49,17},{2,34}... | collective-permute-start | bytes 442376 | tf_op jit(solution)/shard_map/ppermute | solution.py:221
  32.4 3.0 %collective-permute-start.2 = (bf16[2,24,1536]{2,1,0:T(8,128)(2,1)S(1)}, bf16[2,24,1536]{2,1,0:T(8,128)(2,1)S(1)}, u32[]{:S(2)}, u32[]{:S(2)}) collective-permute-start(bf16[2,24,1536]{2,1,0:T(8,128)(2,1)S(1)} %get-tuple-element.37), channel_id=1, source_target_pairs={{0,48},{16,0},{32,16},{48,32},{1,49},{17,1},{33,17},{49,33},{2,50}... | collective-permute-start | bytes 442376 | tf_op jit(solution)/shard_map/ppermute | solution.py:221
  35.4 2.9 %collective-permute-start.4 = (bf16[2,24,1536]{2,1,0:T(8,128)(2,1)S(1)}, bf16[2,24,1536]{2,1,0:T(8,128)(2,1)S(1)}, u32[]{:S(2)}, u32[]{:S(2)}) collective-permute-start(bf16[2,24,1536]{2,1,0:T(8,128)(2,1)S(1)} %get-tuple-element.37), channel_id=1, source_target_pairs={{0,16},{16,32},{32,48},{48,0},{1,17},{17,33},{33,49},{49,1},{2,18}... | collective-permute-start | bytes 442376 | tf_op jit(solution)/shard_map/ppermute | solution.py:221
  38.3 2.4 %collective-permute-done.2 = bf16[2,24,1536]{2,1,0:T(8,128)(2,1)S(1)} collective-permute-done((bf16[2,24,1536]{2,1,0:T(8,128)(2,1)S(1)}, bf16[2,24,1536]{2,1,0:T(8,128)(2,1)S(1)}, u32[]{:S(2)}, u32[]{:S(2)}) %collective-permute-start.2) | collective-permute-done | bytes 147488 | tf_op jit(solution)/shard_map/ppermute | solution.py:221
  40.7 4.4 %collective-permute-done.4 = bf16[2,24,1536]{2,1,0:T(8,128)(2,1)S(1)} collective-permute-done((bf16[2,24,1536]{2,1,0:T(8,128)(2,1)S(1)}, bf16[2,24,1536]{2,1,0:T(8,128)(2,1)S(1)}, u32[]{:S(2)}, u32[]{:S(2)}) %collective-permute-start.4) | collective-permute-done | bytes 147488 | tf_op jit(solution)/shard_map/ppermute | solution.py:221
  45.1 1.9 collective-permute-start.8
  47.0 3.9 %collective-permute-start.6 = (bf16[4,2,24,1536]{3,2,1,0:T(8,128)(2,1)S(1)}, bf16[4,2,24,1536]{3,2,1,0:T(8,128)(2,1)S(1)}, u32[]{:S(2)}, u32[]{:S(2)}) collective-permute-start(bf16[4,2,24,1536]{3,2,1,0:T(8,128)(2,1)S(1)} %pad_maximum_fusion.1.refs_0_), channel_id=1, source_target_pairs={{0,384},{128,0},{256,128},{384,256},{1,385},{129,1},{257,129},{385... | collective-permute-start | bytes 1769480 | tf_op jit(solution)/shard_map/ppermute | solution.py:221
  51.1 1.9 collective-permute-start.5
  53.0 9.5 %collective-permute-done.8.refs_8_ = bf16[4,2,24,1536]{3,2,1,0:T(8,128)(2,1)S(1)} collective-permute-done((bf16[4,2,24,1536]{3,2,1,0:T(8,128)(2,1)S(1)}, bf16[4,2,24,1536]{3,2,1,0:T(8,128)(2,1)S(1)}, u32[]{:S(2)}, u32[]{:S(2)}) %collective-permute-start.8) | collective-permute-done | bytes 589856 | tf_op jit(solution)/shard_map/ppermute | solution.py:221
  62.5 0.7 slice.28
  63.3 3.4 %collective-permute-start.9 = (bf16[2,2,24,1536]{3,2,1,0:T(8,128)(2,1)}, bf16[2,2,24,1536]{3,2,1,0:T(8,128)(2,1)}, u32[]{:S(2)}, u32[]{:S(2)}) collective-permute-start(bf16[2,2,24,1536]{3,2,1,0:T(8,128)(2,1)} %slice.28), channel_id=1, source_target_pairs={{0,128},{128,256},{256,384},{384,0},{1,129},{129,257},{257,385},{3... | collective-permute-start | bytes 884744 | tf_op jit(solution)/shard_map/ppermute | solution.py:221
  66.7 0.7 slice.29
  67.4 2.4 %collective-permute-start.11 = (bf16[2,2,24,1536]{3,2,1,0:T(8,128)(2,1)}, bf16[2,2,24,1536]{3,2,1,0:T(8,128)(2,1)}, u32[]{:S(2)}, u32[]{:S(2)}) collective-permute-start(bf16[2,2,24,1536]{3,2,1,0:T(8,128)(2,1)} %slice.29), channel_id=1, source_target_pairs={{0,384},{128,0},{256,128},{384,256},{1,385},{129,1},{257,129},{385... | collective-permute-start | bytes 884744 | tf_op jit(solution)/shard_map/ppermute | solution.py:221
  69.8 1.9 collective-permute-start.13
  71.8 2.4 %collective-permute-start.7 = (bf16[4,2,24,1536]{3,2,1,0:T(8,128)(2,1)S(1)}, bf16[4,2,24,1536]{3,2,1,0:T(8,128)(2,1)}, u32[]{:S(2)}, u32[]{:S(2)}) collective-permute-start(bf16[4,2,24,1536]{3,2,1,0:T(8,128)(2,1)S(1)} %collective-permute-done.6.refs_2_), channel_id=1, source_target_pairs={{0,64},{64,0},{1,65},{65,1},{2,66},{66,2},{3,67},{67,3},{4,68},{68... | collective-permute-start | bytes 1769480 | tf_op jit(solution)/shard_map/ppermute | solution.py:221
  76.0 1.9 collective-permute-start.10
  77.9 1.3 collective-permute-done.11.refs_6_
  79.2 1.9 collective-permute-start.12
  81.2 0.1 add.605
  81.5 0.1 add.562
  81.9 1.2 collective-permute-done.12.refs_7_
  83.0 2.1 %weight_in_place.1 = bf16[64,24,1536]{2,1,0:T(8,128)(2,1)S(1)} custom-call(s32[64]{0:T(128)S(1)} %concatenate.6.place_ref, bf16[4,2,24,1536]{3,2,1,0:T(8,128)(2,1)S(1)} %pad_maximum_fusion.1.refs_0_, bf16[4,2,24,1536]{3,2,1,0:T(8,128)(2,1)} %collective-permute-done.5.refs_1_, bf16[4,2,24,1536]{3,2,1,0:T(8,128)(2,1)S(1)} %collective-permute-done.6.refs_2_, ...), custom_call_target="tpu_custom_call" | custom-call | flops 36800000000 | bytes 4718592 | tf_op jit(solution)/shard_map/weight_in_place/pallas_call | solution.py:274
  85.2 1.6 convolution_bitcast_fusion.mixed_ref
  86.8 0.5 copy-done
  87.3 1.3 space_attention.1
  88.6 0.9 copy-done.4
  89.5 0.9 copy-done.8
  90.4 0.7 copy-done.9
  91.2 7.0 %all-to-all-done.moved_ref = bf16[16,4,8,1536]{3,2,1,0:T(8,128)(2,1)S(1)} async-done(((bf16[16,4,8,1536]{3,2,1,0:T(8,128)(2,1)}), bf16[16,4,8,1536]{3,2,1,0:T(8,128)(2,1)S(1)}, u32[]{:S(2)}, u32[]{:S(2)}) %all-to-all-start) | async-done | bytes 1572896 | tf_op jit(solution)/shard_map/all_to_all | solution.py:332
  98.2 4.0 %fusion.mixed_ref = f32[128,1536]{1,0:T(8,128)S(1)} fusion(bf16[1536,1536]{1,0:T(8,128)(2,1)} %bitcast.84, bf16[16,4,8,1536]{3,2,1,0:T(8,128)(2,1)S(1)} %all-to-all-done.moved_ref), kind=kOutput, calls=%fused_computation.3 | convolution fusion | flops 603979776 | bytes 5898240 | tf_op jit(solution)/shard_map/td,nd->tn/dot_general | solution.py:343
  102.2 1.8 time_attention.1
  104.0 10.8 %all-to-all-start.1 = ((bf16[16,2,8,1536]{3,2,1,0:T(8,128)(2,1)}), bf16[16,2,8,1536]{3,2,1,0:T(8,128)(2,1)}, u32[]{:S(2)}, u32[]{:S(2)}) async-start(bf16[16,2,8,1536]{3,2,1,0:T(8,128)(2,1)} %get-tuple-element.23), calls=%async_computation.1 | async-start | bytes 1572864 | tf_op jit(solution)/shard_map/all_to_all | solution.py:332
  114.8 12.7 %all-gather = f32[8,1,3072]{2,1,0:T(1,128)S(1)} all-gather(f32[1,1,3072]{2,1,0:T(1,128)S(1)} %maximum_bitcast_fusion), channel_id=1, replica_groups=mesh['x'=4,'core'=2,'fsdp'=4,'seq'=16] {'x','core'}, dimensions={0}, use_global_device_ids=true | all-gather | bytes 110592 | tf_op jit(solution)/shard_map/all_gather | solution.py:287
  127.7 6.8 %collective-permute-start.15 = (f32[1,3072]{1,0:T(1,128)S(1)}, f32[1,3072]{1,0:T(1,128)S(1)}, u32[]{:S(2)}, u32[]{:S(2)}) collective-permute-start(f32[1,3072]{1,0:T(1,128)S(1)} %bitcast.97), channel_id=1, source_target_pairs={{0,1},{1,0},{2,3},{3,2},{4,5},{5,4},{6,7},{7,6},{8,9},{9,8},{10,11... | collective-permute-start | bytes 36872 | tf_op jit(solution)/shard_map/ppermute | solution.py:299
  134.5 4.3 %collective-permute-start.14 = (f32[1,3072]{1,0:T(1,128)S(1)}, f32[1,3072]{1,0:T(1,128)S(1)}, u32[]{:S(2)}, u32[]{:S(2)}) collective-permute-start(f32[1,3072]{1,0:T(1,128)S(1)} %bitcast.98), channel_id=1, source_target_pairs={{64,66},{65,67},{66,64},{67,65},{68,70},{69,71},{70,68},{71,69},{7... | collective-permute-start | bytes 36872 | tf_op jit(solution)/shard_map/ppermute | solution.py:299
  138.7 4.6 %time_scores.1 = bf16[16,2,8,1536]{3,2,1,0:T(8,128)(2,1)} custom-call(s32[1]{0:T(128)S(6)} %copy.20.count_ref, bf16[16,4,8,1536]{3,2,1,0:T(8,128)(2,1)S(1)} %all-to-all-done.moved_ref, f32[128,1536]{1,0:T(8,128)S(1)} %fusion.mixed_ref, f32[1,1536]{1,0:T(1,128)S(1)} %reshape.294.gate_ref.gate_time_ref), custom_call_target="tpu_custom_call" | custom-call | flops 301989888 | bytes 3145728 | tf_op jit(solution)/shard_map/time_scores/pallas_call | solution.py:127
  143.3 11.0 %all-to-all-done.1.time_ref.moved_ref = bf16[16,2,8,1536]{3,2,1,0:T(8,128)(2,1)} async-done(((bf16[16,2,8,1536]{3,2,1,0:T(8,128)(2,1)}), bf16[16,2,8,1536]{3,2,1,0:T(8,128)(2,1)}, u32[]{:S(2)}, u32[]{:S(2)}) %all-to-all-start.1) | async-done | bytes 786464 | tf_op jit(solution)/shard_map/all_to_all | solution.py:332
  154.3 9.1 %all-to-all-start.2 = ((bf16[16,2,8,1536]{3,2,1,0:T(8,128)(2,1)}), bf16[16,2,8,1536]{3,2,1,0:T(8,128)(2,1)S(1)}, u32[]{:S(2)}, u32[]{:S(2)}) async-start(bf16[16,2,8,1536]{3,2,1,0:T(8,128)(2,1)} %time_scores.1), calls=%async_computation.2 | async-start | bytes 1572864 | tf_op jit(solution)/shard_map/all_to_all | solution.py:332
  163.5 12.7 %all-gather.1 = f32[8,1,3072]{2,1,0:T(1,128)S(1)} all-gather(f32[1,1,3072]{2,1,0:T(1,128)S(1)} %fusion.9), channel_id=1, replica_groups=mesh['x'=4,'core'=2,'fsdp'=4,'seq'=16] {'x','core'}, dimensions={0}, use_global_device_ids=true | all-gather | bytes 110592 | tf_op jit(solution)/shard_map/all_gather | solution.py:305
  176.3 12.4 %all-gather.2 = f32[4,1,3072]{2,1,0:T(1,128)S(1)} all-gather(f32[1,1,3072]{2,1,0:T(1,128)S(1)} %fusion.7), channel_id=1, replica_groups=mesh['x'=4,'core'=2,'fsdp'=4,'seq'=16] {'fsdp'}, dimensions={0}, use_global_device_ids=true | all-gather | bytes 61440 | tf_op jit(solution)/shard_map/all_gather | solution.py:287
  188.8 0.6 fusion.41
  189.4 5.2 %output.1 = (bf16[128,1536]{1,0:T(8,128)(2,1)}, bf16[128,1536]{1,0:T(8,128)(2,1)}) custom-call(bf16[16,2,8,1536]{3,2,1,0:T(8,128)(2,1)} %all-to-all-done.1.time_ref.moved_ref, bf16[16,2,8,1536]{3,2,1,0:T(8,128)(2,1)} %all-to-all-done.1.time_ref.moved_ref, bf16[128,1536]{1,0:T(8,128)(2,1)} %copy-done.9, f32[128,1536]{1,0:T(8,128)} %copy-done.8, ...), custom_call_target="tpu_custom_call" | custom-call | flops 16099999744 | tf_op jit(solution)/shard_map/output/pallas_call | solution.py:181
  194.6 6.9 %all-to-all-done.2.moved_ref = bf16[16,2,8,1536]{3,2,1,0:T(8,128)(2,1)S(1)} async-done(((bf16[16,2,8,1536]{3,2,1,0:T(8,128)(2,1)}), bf16[16,2,8,1536]{3,2,1,0:T(8,128)(2,1)S(1)}, u32[]{:S(2)}, u32[]{:S(2)}) %all-to-all-start.2) | async-done | bytes 786464 | tf_op jit(solution)/shard_map/all_to_all | solution.py:332
  201.4 1.6 add_returned.1
  (62 shorter events, 1.4 us)
Async XLA Ops:
  0.6 26.6 %collective-permute-start = (bf16[24,1536]{1,0:T(8,128)(2,1)}, bf16[24,1536]{1,0:T(8,128)(2,1)S(1)}, u32[]{:S(2)}, u32[]{:S(2)}) collective-permute-start(bf16[24,1536]{1,0:T(8,128)(2,1)} %param.13), channel_id=1, source_target_pairs={{68,64},{69,65},{70,66},{71,67},{72,68},{73,69},{74,70},{75,71},{7... | collective-permute-start | bytes 221192 | tf_op jit(solution)/shard_map/ppermute | solution.py:241
  12.9 14.3 %collective-permute-start.1 = (bf16[24,1536]{1,0:T(8,128)(2,1)}, bf16[24,1536]{1,0:T(8,128)(2,1)S(1)}, u32[]{:S(2)}, u32[]{:S(2)}) collective-permute-start(bf16[24,1536]{1,0:T(8,128)(2,1)} %param.13), channel_id=1, source_target_pairs={{8,0},{9,1},{10,2},{11,3},{12,4},{13,5},{14,6},{15,7},{0,8},{1,9},... | collective-permute-start | bytes 221192 | tf_op jit(solution)/shard_map/ppermute | solution.py:241
  17.6 9.6 %copy-start.11 = (bf16[24,1536]{1,0:T(8,128)(2,1)S(1)}, bf16[24,1536]{1,0:T(8,128)(2,1)}, u32[]{:S(2)}) copy-start(bf16[24,1536]{1,0:T(8,128)(2,1)} %param.13) | copy-start | bytes 221188
  17.6 80.6 %all-to-all-start = ((bf16[16,4,8,1536]{3,2,1,0:T(8,128)(2,1)}), bf16[16,4,8,1536]{3,2,1,0:T(8,128)(2,1)S(1)}, u32[]{:S(2)}, u32[]{:S(2)}) async-start(bf16[16,4,8,1536]{3,2,1,0:T(8,128)(2,1)} %pad_maximum_fusion), calls=%async_computation | async-start | bytes 3145728 | tf_op jit(solution)/shard_map/all_to_all | solution.py:332
  27.2 23.9 %copy-start.14 = (s32[4,2,2]{2,1,0:T(2,128)S(1)}, s32[4,2,2]{2,1,0:T(2,128)}, u32[]{:S(2)}) copy-start(s32[4,2,2]{2,1,0:T(2,128)} %constant.192.clone) | copy-start | bytes 196
  27.2 48.7 %copy-start.12 = (f32[1536]{0:T(1024)S(1)}, f32[1536]{0:T(1024)}, u32[]{:S(2)}) copy-start(f32[1536]{0:T(1024)} %param.15) | copy-start | bytes 18436
  27.2 48.7 %copy-start.13 = (f32[1536]{0:T(1024)S(1)}, f32[1536]{0:T(1024)}, u32[]{:S(2)}) copy-start(f32[1536]{0:T(1024)} %param.14) | copy-start | bytes 18436
  27.3 11.0 %collective-permute-start.3 = (bf16[2,24,1536]{2,1,0:T(8,128)(2,1)S(1)}, bf16[2,24,1536]{2,1,0:T(8,128)(2,1)S(1)}, u32[]{:S(2)}, u32[]{:S(2)}) collective-permute-start(bf16[2,24,1536]{2,1,0:T(8,128)(2,1)S(1)} %get-tuple-element.37), channel_id=1, source_target_pairs={{0,32},{16,48},{32,0},{48,16},{1,33},{17,49},{33,1},{49,17},{2,34}... | collective-permute-start | bytes 442376 | tf_op jit(solution)/shard_map/ppermute | solution.py:221
  32.4 8.3 %collective-permute-start.2 = (bf16[2,24,1536]{2,1,0:T(8,128)(2,1)S(1)}, bf16[2,24,1536]{2,1,0:T(8,128)(2,1)S(1)}, u32[]{:S(2)}, u32[]{:S(2)}) collective-permute-start(bf16[2,24,1536]{2,1,0:T(8,128)(2,1)S(1)} %get-tuple-element.37), channel_id=1, source_target_pairs={{0,48},{16,0},{32,16},{48,32},{1,49},{17,1},{33,17},{49,33},{2,50}... | collective-permute-start | bytes 442376 | tf_op jit(solution)/shard_map/ppermute | solution.py:221
  35.4 9.7 %collective-permute-start.4 = (bf16[2,24,1536]{2,1,0:T(8,128)(2,1)S(1)}, bf16[2,24,1536]{2,1,0:T(8,128)(2,1)S(1)}, u32[]{:S(2)}, u32[]{:S(2)}) collective-permute-start(bf16[2,24,1536]{2,1,0:T(8,128)(2,1)S(1)} %get-tuple-element.37), channel_id=1, source_target_pairs={{0,16},{16,32},{32,48},{48,0},{1,17},{17,33},{33,49},{49,1},{2,18}... | collective-permute-start | bytes 442376 | tf_op jit(solution)/shard_map/ppermute | solution.py:221
  45.1 17.4 %collective-permute-start.8 = (bf16[4,2,24,1536]{3,2,1,0:T(8,128)(2,1)S(1)}, bf16[4,2,24,1536]{3,2,1,0:T(8,128)(2,1)S(1)}, u32[]{:S(2)}, u32[]{:S(2)}) collective-permute-start(bf16[4,2,24,1536]{3,2,1,0:T(8,128)(2,1)S(1)} %pad_maximum_fusion.1.refs_0_), channel_id=1, source_target_pairs={{0,128},{128,256},{256,384},{384,0},{1,129},{129,257},{257,385},{3... | collective-permute-start | bytes 1769480 | tf_op jit(solution)/shard_map/ppermute | solution.py:221
  47.0 19.6 %collective-permute-start.6 = (bf16[4,2,24,1536]{3,2,1,0:T(8,128)(2,1)S(1)}, bf16[4,2,24,1536]{3,2,1,0:T(8,128)(2,1)S(1)}, u32[]{:S(2)}, u32[]{:S(2)}) collective-permute-start(bf16[4,2,24,1536]{3,2,1,0:T(8,128)(2,1)S(1)} %pad_maximum_fusion.1.refs_0_), channel_id=1, source_target_pairs={{0,384},{128,0},{256,128},{384,256},{1,385},{129,1},{257,129},{385... | collective-permute-start | bytes 1769480 | tf_op jit(solution)/shard_map/ppermute | solution.py:221
  51.1 30.7 %collective-permute-start.5 = (bf16[4,2,24,1536]{3,2,1,0:T(8,128)(2,1)S(1)}, bf16[4,2,24,1536]{3,2,1,0:T(8,128)(2,1)}, u32[]{:S(2)}, u32[]{:S(2)}) collective-permute-start(bf16[4,2,24,1536]{3,2,1,0:T(8,128)(2,1)S(1)} %pad_maximum_fusion.1.refs_0_), channel_id=1, source_target_pairs={{0,64},{64,0},{1,65},{65,1},{2,66},{66,2},{3,67},{67,3},{4,68},{68... | collective-permute-start | bytes 1769480 | tf_op jit(solution)/shard_map/ppermute | solution.py:221
  63.3 12.7 %collective-permute-start.9 = (bf16[2,2,24,1536]{3,2,1,0:T(8,128)(2,1)}, bf16[2,2,24,1536]{3,2,1,0:T(8,128)(2,1)}, u32[]{:S(2)}, u32[]{:S(2)}) collective-permute-start(bf16[2,2,24,1536]{3,2,1,0:T(8,128)(2,1)} %slice.28), channel_id=1, source_target_pairs={{0,128},{128,256},{256,384},{384,0},{1,129},{129,257},{257,385},{3... | collective-permute-start | bytes 884744 | tf_op jit(solution)/shard_map/ppermute | solution.py:221
  67.4 11.8 %collective-permute-start.11 = (bf16[2,2,24,1536]{3,2,1,0:T(8,128)(2,1)}, bf16[2,2,24,1536]{3,2,1,0:T(8,128)(2,1)}, u32[]{:S(2)}, u32[]{:S(2)}) collective-permute-start(bf16[2,2,24,1536]{3,2,1,0:T(8,128)(2,1)} %slice.29), channel_id=1, source_target_pairs={{0,384},{128,0},{256,128},{384,256},{1,385},{129,1},{257,129},{385... | collective-permute-start | bytes 884744 | tf_op jit(solution)/shard_map/ppermute | solution.py:221
  69.8 12.0 %collective-permute-start.13 = (bf16[4,2,24,1536]{3,2,1,0:T(8,128)(2,1)S(1)}, bf16[4,2,24,1536]{3,2,1,0:T(8,128)(2,1)}, u32[]{:S(2)}, u32[]{:S(2)}) collective-permute-start(bf16[4,2,24,1536]{3,2,1,0:T(8,128)(2,1)S(1)} %collective-permute-done.8.refs_8_), channel_id=1, source_target_pairs={{0,64},{64,0},{1,65},{65,1},{2,66},{66,2},{3,67},{67,3},{4,68},{68... | collective-permute-start | bytes 1769480 | tf_op jit(solution)/shard_map/ppermute | solution.py:221
  71.8 11.3 %collective-permute-start.7 = (bf16[4,2,24,1536]{3,2,1,0:T(8,128)(2,1)S(1)}, bf16[4,2,24,1536]{3,2,1,0:T(8,128)(2,1)}, u32[]{:S(2)}, u32[]{:S(2)}) collective-permute-start(bf16[4,2,24,1536]{3,2,1,0:T(8,128)(2,1)S(1)} %collective-permute-done.6.refs_2_), channel_id=1, source_target_pairs={{0,64},{64,0},{1,65},{65,1},{2,66},{66,2},{3,67},{67,3},{4,68},{68... | collective-permute-start | bytes 1769480 | tf_op jit(solution)/shard_map/ppermute | solution.py:221
  75.9 62.8 %copy-start.6 = (f32[1,1536]{1,0:T(1,128)}, f32[1,1536]{1,0:T(1,128)S(1)}, u32[]{:S(2)}) copy-start(f32[1,1536]{1,0:T(1,128)S(1)} %reshape.294.gate_ref.gate_time_ref) | copy-start | bytes 18436
  75.9 11.4 %copy-start.7 = (f32[1,1536]{1,0:T(1,128)}, f32[1,1536]{1,0:T(1,128)S(1)}, u32[]{:S(2)}) copy-start(f32[1,1536]{1,0:T(1,128)S(1)} %reshape.293.gate_ref.gate_space_ref) | copy-start | bytes 18436
  76.0 5.9 %collective-permute-start.10 = (bf16[2,2,24,1536]{3,2,1,0:T(8,128)(2,1)}, bf16[2,2,24,1536]{3,2,1,0:T(8,128)(2,1)}, u32[]{:S(2)}, u32[]{:S(2)}) collective-permute-start(bf16[2,2,24,1536]{3,2,1,0:T(8,128)(2,1)} %collective-permute-done.9.refs_4_), channel_id=1, source_target_pairs={{0,64},{64,0},{1,65},{65,1},{2,66},{66,2},{3,67},{67,3},{4,68},{68... | collective-permute-start | bytes 884744 | tf_op jit(solution)/shard_map/ppermute | solution.py:221
  79.2 3.8 %collective-permute-start.12 = (bf16[2,2,24,1536]{3,2,1,0:T(8,128)(2,1)}, bf16[2,2,24,1536]{3,2,1,0:T(8,128)(2,1)}, u32[]{:S(2)}, u32[]{:S(2)}) collective-permute-start(bf16[2,2,24,1536]{3,2,1,0:T(8,128)(2,1)} %collective-permute-done.11.refs_6_), channel_id=1, source_target_pairs={{0,64},{64,0},{1,65},{65,1},{2,66},{66,2},{3,67},{67,3},{4,68},{68... | collective-permute-start | bytes 884744 | tf_op jit(solution)/shard_map/ppermute | solution.py:221
  81.8 3.3 %copy-start.10 = (bf16[1,1,128,1536]{3,2,1,0:T(8,128)(2,1)S(1)}, bf16[1,1,128,1536]{3,2,1,0:T(8,128)(2,1)}, u32[]{:S(2)}) copy-start(bf16[1,1,128,1536]{3,2,1,0:T(8,128)(2,1)} %param.16) | copy-start | bytes 1179652
  85.1 2.1 %copy-start = (bf16[64,24,1536]{2,1,0:T(8,128)(2,1)}, bf16[64,24,1536]{2,1,0:T(8,128)(2,1)S(1)}, u32[]{:S(2)}) copy-start(bf16[64,24,1536]{2,1,0:T(8,128)(2,1)S(1)} %weight_in_place.1) | copy-start | bytes 14155780
  85.2 2.1 %copy-start.1 = (bf16[1,1,128,1536]{3,2,1,0:T(8,128)(2,1)S(1)}, bf16[1,1,128,1536]{3,2,1,0:T(8,128)(2,1)}, u32[]{:S(2)}) copy-start(bf16[1,1,128,1536]{3,2,1,0:T(8,128)(2,1)} %param.12) | copy-start | bytes 1179652
  85.2 2.1 %copy-start.2 = (bf16[1,1,128,1536]{3,2,1,0:T(8,128)(2,1)S(1)}, bf16[1,1,128,1536]{3,2,1,0:T(8,128)(2,1)}, u32[]{:S(2)}) copy-start(bf16[1,1,128,1536]{3,2,1,0:T(8,128)(2,1)} %param.11) | copy-start | bytes 1179652
  85.2 2.1 %copy-start.3 = (bf16[1,1,128,1536]{3,2,1,0:T(8,128)(2,1)S(1)}, bf16[1,1,128,1536]{3,2,1,0:T(8,128)(2,1)}, u32[]{:S(2)}) copy-start(bf16[1,1,128,1536]{3,2,1,0:T(8,128)(2,1)} %param.10) | copy-start | bytes 1179652
  88.6 0.9 copy-start.4
  89.5 0.9 copy-start.8
  90.4 0.7 copy-start.9
  104.0 50.4 %all-to-all-start.1 = ((bf16[16,2,8,1536]{3,2,1,0:T(8,128)(2,1)}), bf16[16,2,8,1536]{3,2,1,0:T(8,128)(2,1)}, u32[]{:S(2)}, u32[]{:S(2)}) async-start(bf16[16,2,8,1536]{3,2,1,0:T(8,128)(2,1)} %get-tuple-element.23), calls=%async_computation.1 | async-start | bytes 1572864 | tf_op jit(solution)/shard_map/all_to_all | solution.py:332
  127.7 35.8 %collective-permute-start.15 = (f32[1,3072]{1,0:T(1,128)S(1)}, f32[1,3072]{1,0:T(1,128)S(1)}, u32[]{:S(2)}, u32[]{:S(2)}) collective-permute-start(f32[1,3072]{1,0:T(1,128)S(1)} %bitcast.97), channel_id=1, source_target_pairs={{0,1},{1,0},{2,3},{3,2},{4,5},{5,4},{6,7},{7,6},{8,9},{9,8},{10,11... | collective-permute-start | bytes 36872 | tf_op jit(solution)/shard_map/ppermute | solution.py:299
  134.5 29.0 %collective-permute-start.14 = (f32[1,3072]{1,0:T(1,128)S(1)}, f32[1,3072]{1,0:T(1,128)S(1)}, u32[]{:S(2)}, u32[]{:S(2)}) collective-permute-start(f32[1,3072]{1,0:T(1,128)S(1)} %bitcast.98), channel_id=1, source_target_pairs={{64,66},{65,67},{66,64},{67,65},{68,70},{69,71},{70,68},{71,69},{7... | collective-permute-start | bytes 36872 | tf_op jit(solution)/shard_map/ppermute | solution.py:299
  154.3 47.1 %all-to-all-start.2 = ((bf16[16,2,8,1536]{3,2,1,0:T(8,128)(2,1)}), bf16[16,2,8,1536]{3,2,1,0:T(8,128)(2,1)S(1)}, u32[]{:S(2)}, u32[]{:S(2)}) async-start(bf16[16,2,8,1536]{3,2,1,0:T(8,128)(2,1)} %time_scores.1), calls=%async_computation.2 | async-start | bytes 1572864 | tf_op jit(solution)/shard_map/all_to_all | solution.py:332
  189.4 12.0 %copy-start.5 = (f32[128,1536]{1,0:T(8,128)S(1)}, f32[128,1536]{1,0:T(8,128)}, u32[]{:S(2)}) copy-start(f32[128,1536]{1,0:T(8,128)} %copy-done.4) | copy-start | bytes 2359300
